TPU v7x, 256 devices: a whole 4x4x8 slice. The times are simulated.
256 devices in a mesh: space: 32 (over y_hi, z, core), ens: 8 (over y_lo, x).
Axes of the slice: x: 4, y: 4 (y_hi: 2, y_lo: 2; y = y_hi * 2 + y_lo), z: 8, core: 2. Of those that a mesh axis runs over, the one named last changes fastest.
Arguments:
- initial_state: bfloat16 [768, 2304], P('space'), may hold values from -6 to 6
- starting_field_nudges: bfloat16 [8, 768, 2304], P('ens', 'space'), may hold values from -4 to 4
- verifying_analysis: bfloat16 [768, 2304], P('space'), may hold values from -6 to 6
- seam_turns: int32 [32], replicated, may hold values from 0 to 3
- w_in: bfloat16 [864, 256], replicated, may hold values from -0.21875 to 0.21875
- b_in: bfloat16 [256], replicated, may hold values from -3 to 3
- w_depth: bfloat16 [49, 256], replicated, may hold values from -0.875 to 0.875
- b_depth: bfloat16 [256], replicated, may hold values from -3 to 3
- norm_gain: bfloat16 [256], replicated, may hold values from 0.5 to 2
- norm_shift: bfloat16 [256], replicated, may hold values from -3 to 3
- w_up: bfloat16 [256, 1024], replicated, may hold values from -0.375 to 0.375
- b_up: bfloat16 [1024], replicated, may hold values from -3 to 3
- w_down: bfloat16 [1024, 256], replicated, may hold values from -0.1875 to 0.1875
- b_down: bfloat16 [256], replicated, may hold values from -3 to 3
- head_weight: bfloat16 [256, 96], replicated, may hold values from -0.375 to 0.375
- head_bias: bfloat16 [96], replicated, may hold values from -3 to 3
Outputs:
- sampled_predictions: float32 [8, 768, 2304], P('ens', 'space')
- grad_w_in: float32 [864, 256], P(None, 'space')
- grad_b_in: float32 [256], P('space')
- grad_w_depth: float32 [49, 256], P(None, 'space')
- grad_b_depth: float32 [256], P('space')
- grad_norm_gain: float32 [256], P('space')
- grad_norm_shift: float32 [256], P('space')
- grad_w_up: float32 [256, 1024], P(None, 'space')
- grad_b_up: float32 [1024], P('space')
- grad_w_down: float32 [1024, 256], P(None, 'space')
- grad_b_down: float32 [256], P('space')
- grad_w_out: float32 [256, 96], P(None, 'space')
- grad_b_out: float32 [96], P('space')
Inputs may be any that keep to these rules, and one draw needn't show every extreme that they name: `seam_turns`: each seam's turn is a whole number of quarter turns.
All inputs are finite; a program needn't handle non-finite values.
Results may differ from a plain program's by a relative error of at most 0.01.
Values may be sent and summed in bfloat16 or wider, within the bound.
No kernel may reach another device: no remote copies, remote signals or barrier semaphores. Data moves between devices by JAX's collectives and lax.ppermute only.
A program may use at most 128 MiB of HBM per device.

v0:
```python
import functools
import math

import jax
import jax.numpy as jnp
from jax import lax
from jax.experimental import pallas as pl
from jax.experimental.pallas import tpu as pltpu
from jax.sharding import PartitionSpec as P

EPS = 1e-06
CUBIC = 0.044715
ROOT = math.sqrt(2.0 / math.pi)
SOFT_SQUARE = 0.01
F32 = jnp.float32
BF16 = jnp.bfloat16
SIDE = 24
CELLS = SIDE * SIDE
LANE = 128
SMALL = 64
VMEM_BYTES = 56 * 1024 * 1024


def dot(left, right, left_dim=1, right_dim=0):
    return lax.dot_general(
        left, right, (((left_dim,), (right_dim,)), ((), ())), preferred_element_type=F32
    )


def soft_slope(values):
    return values * lax.rsqrt(values * values + SOFT_SQUARE)


def turned_offset(quarter, row_off, col_off):
    return (
        (row_off, col_off),
        (2 - col_off, row_off),
        (2 - row_off, 2 - col_off),
        (col_off, 2 - row_off),
    )[quarter]


def gather_patches(turns_ref, wide_ref, stage_ref, patches_ref):
    bands = ((0, 0, 3), (3, 5, SIDE), (27, 31, 3))
    turn_of = {(1, 0): 0, (1, 2): 1, (0, 0): 2, (0, 2): 3, (2, 0): 4, (2, 2): 5}
    stage_ref[...] = jnp.zeros_like(stage_ref)
    for row_off in range(3):
        for col_off in range(3):
            for row_band, (row_to, row_from, row_len) in enumerate(bands):
                for col_band, (col_to, col_from, col_len) in enumerate(bands):

                    def read(quarter):
                        row, col = turned_offset(quarter, row_off, col_off)
                        return wide_ref[
                            row_from + row : row_from + row + row_len,
                            col_from + col : col_from + col + col_len,
                            :,
                        ]

                    piece = read(0)
                    if (row_band, col_band) in turn_of:
                        turn = turns_ref[turn_of[row_band, col_band]]
                        for quarter in range(1, 4):
                            piece = jnp.where(turn == quarter, read(quarter), piece)
                    stage_ref[row_to : row_to + row_len, col_to : col_to + col_len, :] = piece
            at = (3 * row_off + col_off) * LANE
            patches_ref[:, at : at + LANE] = stage_ref[...].reshape(960, LANE).astype(BF16)


def forward_kernel(
    turns_ref,
    source_ref,
    w_in_ref,
    b_in_ref,
    w_depth_ref,
    b_depth_ref,
    gain_ref,
    shift_ref,
    w_up_ref,
    b_up_ref,
    w_down_ref,
    b_down_ref,
    head_ref,
    head_bias_ref,
    patches_ref,
    stem_ref,
    normed_ref,
    inverse_ref,
    scaled_ref,
    slope_ref,
    active_ref,
    hidden_ref,
    field_ref,
    tight_ref,
    sent_ref,
    wide_ref,
    stage_ref,
):
    wide_ref[...] = source_ref[...].astype(F32)
    gather_patches(turns_ref, wide_ref, stage_ref, patches_ref)
    for part in range(5):
        rows = slice(part * 192, (part + 1) * 192)
        stem = dot(patches_ref[rows, :], w_in_ref[...]) + b_in_ref[...]
        stem = stem.astype(BF16).astype(F32)
        for half in range(2):
            stem_ref[half, part * 6 : (part + 1) * 6] = stem[
                :, half * LANE : (half + 1) * LANE
            ].reshape(6, 32, LANE)

    def normalise(block, carry):
        row = block * 4
        halves = []
        for half in range(2):
            lanes = slice(half * LANE, (half + 1) * LANE)
            total = jnp.zeros((4, SIDE, LANE), F32)
            for col_off in range(7):
                slab = stem_ref[half, pl.ds(row, 10), col_off : col_off + SIDE, :]
                for row_off in range(7):
                    tap = 7 * row_off + col_off
                    total = total + slab[row_off : row_off + 4] * w_depth_ref[tap : tap + 1, lanes][None]
            halves.append(total.reshape(4 * SIDE, LANE) + b_depth_ref[:, lanes])
        mean = (
            jnp.sum(halves[0], axis=-1, keepdims=True) + jnp.sum(halves[1], axis=-1, keepdims=True)
        ) / 256.0
        centers = [h - mean for h in halves]
        spread = (
            jnp.sum(centers[0] * centers[0], axis=-1, keepdims=True)
            + jnp.sum(centers[1] * centers[1], axis=-1, keepdims=True)
        ) / 256.0
        inverse = lax.rsqrt(spread + EPS)
        at = pl.ds(pl.multiple_of(block * 96, 96), 96)
        inverse_ref[at, :] = jnp.broadcast_to(inverse, (96, LANE))
        for half in range(2):
            lanes = slice(half * LANE, (half + 1) * LANE)
            normed = centers[half] * inverse
            normed_ref[at, lanes] = normed
            scaled_ref[at, lanes] = (normed * gain_ref[:, lanes] + shift_ref[:, lanes]).astype(BF16)
        return carry

    lax.fori_loop(0, 6, normalise, 0)

    def mix(part, carry):
        at = pl.ds(pl.multiple_of(part * 96, 96), 96)
        upward = dot(scaled_ref[at, :], w_up_ref[...]) + b_up_ref[...]
        square = upward * upward
        tanh_part = jnp.tanh(ROOT * (upward + CUBIC * square * upward))
        plus = 0.5 * (1.0 + tanh_part)
        slope_ref[at, :] = plus + 0.5 * upward * (1.0 - tanh_part * tanh_part) * (
            ROOT + (3.0 * CUBIC * ROOT) * square
        )
        active = (upward * plus).astype(BF16)
        active_ref[at, :] = active
        own = [
            stem_ref[half, pl.ds(3 + 4 * part, 4), 3 : 3 + SIDE, :].reshape(96, LANE)
            for half in range(2)
        ]
        own = jnp.concatenate(own, axis=1)
        hidden = (own + dot(active, w_down_ref[...]) + b_down_ref[...]).astype(BF16)
        hidden_ref[at, :] = hidden
        field_ref[at, :] = dot(hidden, head_ref[...]) + head_bias_ref[...]
        return carry

    lax.fori_loop(0, 6, mix, 0)
    for quarter in range(4):
        tight_ref[:, 96 * quarter : 96 * (quarter + 1)] = field_ref[
            144 * quarter : 144 * (quarter + 1), 0:96
        ]
    sent = tight_ref[...].astype(BF16)
    for member in range(sent_ref.shape[0]):
        sent_ref[member] = sent


def mixer_backward_kernel(
    coefficient,
    every_ref,
    own_ref,
    target_ref,
    hidden_ref,
    head_ref,
    pick_ref,
    active_ref,
    slope_ref,
    scaled_ref,
    w_down_ref,
    w_up_ref,
    early_ref,
    out_part_ref,
    hidden_grad_ref,
    scaled_grad_ref,
    small_ref,
    tight_ref,
    field_ref,
    low_ref,
    up_low_ref,
    up_sum_ref,
    down_ref,
):
    members = every_ref.shape[0]
    own = own_ref[...]
    own_sent = own.astype(BF16).astype(F32)
    pair_sum = soft_slope(own_sent - every_ref[0].astype(F32))
    for member in range(1, members):
        pair_sum = pair_sum + soft_slope(own_sent - every_ref[member].astype(F32))
    direct = soft_slope(own - target_ref[...].astype(F32))
    tight_ref[...] = (
        direct * (coefficient / members) - pair_sum * (coefficient / (members * (members - 1)))
    )
    field_ref[...] = jnp.zeros_like(field_ref)
    for quarter in range(4):
        field_ref[144 * quarter : 144 * (quarter + 1), 0:96] = tight_ref[
            :, 96 * quarter : 96 * (quarter + 1)
        ]
    grad_f = field_ref[...]
    grad_b_out = jnp.sum(grad_f, axis=0, keepdims=True)
    grad_f_low = grad_f.astype(BF16)
    picked = dot(grad_f_low, pick_ref[...]).astype(BF16)
    out_part_ref[...] = dot(picked, hidden_ref[...], 0, 0).astype(BF16)
    grad_hidden = dot(grad_f_low, head_ref[...], 1, 1)
    hidden_grad_ref[...] = grad_hidden
    low_ref[...] = grad_hidden.astype(BF16)
    grad_b_down = jnp.sum(grad_hidden, axis=0, keepdims=True)
    down_ref[...] = dot(low_ref[...], active_ref[...], 0, 0)
    up_sum_ref[...] = jnp.zeros_like(up_sum_ref)

    def widen(part, carry):
        at = pl.ds(pl.multiple_of(part * 96, 96), 96)
        grad_up = dot(low_ref[at, :], w_down_ref[...], 1, 1) * slope_ref[at, :]
        up_sum_ref[...] += jnp.sum(grad_up.reshape(12, 8, 1024), axis=0)
        up_low = grad_up.astype(BF16)
        up_low_ref[at, :] = up_low
        scaled_grad_ref[at, :] = dot(up_low, w_up_ref[...], 1, 1)
        return carry

    lax.fori_loop(0, 6, widen, 0)
    for chunk in range(4):
        up = dot(up_low_ref[:, chunk * 256 : (chunk + 1) * 256], scaled_ref[...], 0, 0)
        up = up.reshape(8, 4, 8, 256)
        for row_tile in range(4):
            for lane_tile in range(2):
                part = 2 * row_tile + lane_tile
                upper = down_ref[
                    chunk * 64 : (chunk + 1) * 64, part * LANE : (part + 1) * LANE
                ].reshape(8, 8, LANE)
                lower = up[:, row_tile, :, lane_tile * LANE : (lane_tile + 1) * LANE]
                early_ref[part, chunk * 8 : (chunk + 1) * 8] = jnp.concatenate(
                    [upper, lower], axis=1
                ).astype(BF16)
    up_sum = jnp.sum(up_sum_ref[...], axis=0, keepdims=True)
    unit = lax.broadcasted_iota(jnp.int32, (8, 1024), 1)
    row = lax.broadcasted_iota(jnp.int32, (8, 1024), 0)
    spread = jnp.where((unit & 3) == row, jnp.broadcast_to(up_sum, (8, 1024)), 0.0)
    fold = (
        lax.broadcasted_iota(jnp.int32, (1024, 256), 0) >> 2
        == lax.broadcasted_iota(jnp.int32, (1024, 256), 1)
    ).astype(F32).astype(BF16)
    column = lax.broadcasted_iota(jnp.int32, (LANE, 256), 1)
    place = (
        (lax.broadcasted_iota(jnp.int32, (LANE, 256), 0) == 3 * (column >> 3) + (column & 7))
        & ((column & 7) < 3)
    ).astype(F32).astype(BF16)
    b_out = jnp.broadcast_to(grad_b_out, (8, LANE))

    def two_part(values, matrix):
        high = values.astype(BF16)
        rest = (values - high.astype(F32)).astype(BF16)
        return dot(high, matrix) + dot(rest, matrix)

    small_ref[...] = jnp.zeros_like(small_ref)
    small_ref[0:1, :] = grad_b_down
    small_ref[1:5, :] = two_part(spread, fold)[0:4]
    small_ref[5:6, :] = two_part(b_out, place)[0:1]


def depth_backward_kernel(
    scaled_grad_ref,
    normed_ref,
    inverse_ref,
    gain_ref,
    hidden_grad_ref,
    stem_ref,
    w_depth_ref,
    patches_ref,
    order_ref,
    early_small_ref,
    out_part_ref,
    late_ref,
    deep_ref,
    stem_grad_ref,
    small_ref,
    sums_ref,
    low_ref,
    tight_ref,
):
    deep_ref[...] = jnp.zeros_like(deep_ref)
    small_ref[...] = jnp.zeros_like(small_ref)
    sums_ref[...] = jnp.zeros_like(sums_ref)

    def unnormalise(block, carry):
        at = pl.ds(pl.multiple_of(block * 96, 96), 96)
        halves = []
        first = jnp.zeros((96, 1), F32)
        second = jnp.zeros((96, 1), F32)
        for half in range(2):
            lanes = slice(half * LANE, (half + 1) * LANE)
            grad = scaled_grad_ref[at, lanes]
            normed = normed_ref[at, lanes]
            sums_ref[0, :, lanes] += jnp.sum((grad * normed).reshape(12, 8, LANE), axis=0)
            sums_ref[1, :, lanes] += jnp.sum(grad.reshape(12, 8, LANE), axis=0)
            grad = grad * gain_ref[:, lanes]
            first = first + jnp.sum(grad, axis=-1, keepdims=True)
            second = second + jnp.sum(grad * normed, axis=-1, keepdims=True)
            halves.append((grad, normed))
        first = first / 256.0
        second = second / 256.0
        inverse = inverse_ref[at, :]
        for half, (grad, normed) in enumerate(halves):
            lanes = slice(half * LANE, (half + 1) * LANE)
            deep = (grad - first - normed * second) * inverse
            sums_ref[2, :, lanes] += jnp.sum(deep.reshape(12, 8, LANE), axis=0)
            deep_ref[half, pl.ds(6 + block * 4, 4), 8 : 8 + SIDE, :] = deep.reshape(4, SIDE, LANE)
        return carry

    lax.fori_loop(0, 6, unnormalise, 0)
    for half in range(2):
        lanes = slice(half * LANE, (half + 1) * LANE)

        def spread(block, carry):
            row = block * 3
            total = jnp.zeros((3, 32, LANE), F32)
            for col_off in range(7):
                slab = deep_ref[half, pl.ds(row, 9), 8 - col_off : 40 - col_off, :]
                for row_off in range(7):
                    tap = 7 * row_off + col_off
                    total = total + slab[6 - row_off : 9 - row_off] * w_depth_ref[tap : tap + 1, lanes][None]
            stem_grad_ref[half, pl.ds(row, 3)] = total
            return carry

        lax.fori_loop(0, 10, spread, 0)
        for col_off in range(7):

            def weigh(block, totals):
                row = block * 4
                deep = deep_ref[half, pl.ds(6 + row, 4), 8 : 8 + SIDE, :]
                slab = stem_ref[half, pl.ds(row, 10), col_off : col_off + SIDE, :]
                return tuple(
                    totals[row_off]
                    + jnp.sum((slab[row_off : row_off + 4] * deep).reshape(12, 8, LANE), axis=0)
                    for row_off in range(7)
                )

            totals = lax.fori_loop(0, 6, weigh, tuple(jnp.zeros((8, LANE), F32) for _ in range(7)))
            for row_off in range(7):
                tap = 7 * row_off + col_off
                small_ref[tap : tap + 1, lanes] = jnp.sum(totals[row_off], axis=0, keepdims=True)

        def add_direct(block, carry):
            at = pl.ds(pl.multiple_of(block * 96, 96), 96)
            stem_grad_ref[half, pl.ds(3 + block * 4, 4), 3 : 3 + SIDE, :] += hidden_grad_ref[
                at, lanes
            ].reshape(4, SIDE, LANE)
            return carry

        lax.fori_loop(0, 6, add_direct, 0)
        grad_stem = stem_grad_ref[half].reshape(960, LANE)
        small_ref[52:53, lanes] = jnp.sum(grad_stem, axis=0, keepdims=True)
        low_ref[:, lanes] = grad_stem.astype(BF16)
    small_ref[49:50, :] = jnp.sum(sums_ref[2], axis=0, keepdims=True)
    small_ref[50:51, :] = jnp.sum(sums_ref[0], axis=0, keepdims=True)
    small_ref[51:52, :] = jnp.sum(sums_ref[1], axis=0, keepdims=True)
    small_ref[53:59, :] = early_small_ref[0:6, :]
    order = order_ref[...]
    ordered = dot(low_ref[...], order).astype(BF16)
    wide = dot(ordered, patches_ref[...], 0, 0)
    tight_ref[...] = jnp.zeros_like(tight_ref)
    for offset in range(9):
        tight_ref[:, 96 * offset : 96 * (offset + 1)] = wide[:, LANE * offset : LANE * offset + 96]
    late_ref[:, 0:896] = tight_ref[...].astype(BF16)
    small = small_ref[...]
    high = small.astype(BF16)
    rest = (small - high.astype(F32)).astype(BF16)
    both = jnp.concatenate([high, rest], axis=0)
    late_ref[:, 896:1024] = dot(order, both, 0, 1).astype(BF16)
    late_ref[:, 1024:1280] = out_part_ref[...]


def call(kernel, shapes, scratch, *operands, smem=0, flops=0):
    space = [pl.BlockSpec(memory_space=pltpu.SMEM)] * smem
    space += [pl.BlockSpec(memory_space=pltpu.VMEM)] * (len(operands) - smem)
    return pl.pallas_call(
        kernel,
        out_shape=[jax.ShapeDtypeStruct(s, d) for s, d in shapes],
        in_specs=space,
        out_specs=[pl.BlockSpec(memory_space=pltpu.VMEM)] * len(shapes),
        scratch_shapes=[pltpu.VMEM(s, d) for s, d in scratch],
        compiler_params=pltpu.CompilerParams(vmem_limit_bytes=VMEM_BYTES),
        cost_estimate=pl.CostEstimate(flops=flops, bytes_accessed=8_000_000, transcendentals=0),
    )(*operands)


def row_of(values):
    return values.astype(F32).reshape(1, -1)


def run_forward(turns, wide_source, weights, members):
    w_in, b_in, w_depth, b_depth, gain, shift, w_up, b_up, w_down, b_down, head, head_bias = weights
    w_in_wide = jnp.pad(w_in.reshape(9, 96, 256), ((0, 0), (0, 32), (0, 0))).reshape(1152, 256)
    source = jnp.pad(wide_source, ((0, 0), (0, 4), (0, 32)))
    head_wide = jnp.pad(head, ((0, 0), (0, 32)))
    bias_wide = jnp.pad(row_of(head_bias), ((0, 0), (0, 32)))
    w_depth_wide = jnp.pad(w_depth.astype(F32), ((0, 7), (0, 0)))
    outs = call(
        forward_kernel,
        [
            ((960, 1152), BF16),
            ((2, 30, 32, LANE), F32),
            ((CELLS, 256), F32),
            ((CELLS, LANE), F32),
            ((CELLS, 256), BF16),
            ((CELLS, 1024), F32),
            ((CELLS, 1024), BF16),
            ((CELLS, 256), BF16),
            ((CELLS, LANE), F32),
            ((144, 384), F32),
            ((members, 144, 384), BF16),
        ],
        [((36, 40, LANE), F32), ((30, 32, LANE), F32)],
        turns,
        source,
        w_in_wide,
        row_of(b_in),
        w_depth_wide,
        row_of(b_depth),
        row_of(gain),
        row_of(shift),
        w_up,
        row_of(b_up),
        w_down,
        row_of(b_down),
        head_wide,
        bias_wide,
        smem=1,
        flops=2_000_000_000,
    )
    return outs, head_wide, w_depth_wide


def run_mixer_backward(every, tight, target, saved, head_wide, w_down, w_up, coefficient):
    hidden, active, slope, scaled = saved
    column = jnp.arange(256)
    owner = 3 * (column % 32) + column // 32
    pick = ((jnp.arange(LANE)[:, None] == owner[None, :]) & (column[None, :] < 96)).astype(BF16)
    return call(
        functools.partial(mixer_backward_kernel, coefficient),
        [
            ((8, 32, 16, LANE), BF16),
            ((256, 256), BF16),
            ((CELLS, 256), F32),
            ((CELLS, 256), F32),
            ((8, 256), F32),
        ],
        [
            ((144, 384), F32),
            ((CELLS, LANE), F32),
            ((CELLS, 256), BF16),
            ((CELLS, 1024), BF16),
            ((8, 1024), F32),
            ((256, 1024), F32),
        ],
        every,
        tight,
        target,
        hidden,
        head_wide,
        pick,
        active,
        slope,
        scaled,
        w_down,
        w_up,
        flops=3_000_000_000,
    )


def run_depth_backward(
    scaled_grad, normed, inverse, gain, hidden_grad, stem, w_depth_wide, patches, early_small, out_part
):
    column = jnp.arange(256)
    order = (column[:, None] == (8 * (column % 32) + column // 32)[None, :]).astype(BF16)
    return call(
        depth_backward_kernel,
        [((256, 1280), BF16)],
        [
            ((2, 36, 40, LANE), F32),
            ((2, 30, 32, LANE), F32),
            ((SMALL, 256), F32),
            ((3, 8, 256), F32),
            ((960, 256), BF16),
            ((256, 896), F32),
        ],
        scaled_grad,
        normed,
        inverse,
        row_of(gain),
        hidden_grad,
        stem,
        w_depth_wide,
        patches,
        order,
        early_small,
        out_part,
        flops=3_000_000_000,
    )[0]


def shifted(value, axis, by):
    peers = lax.axis_size(axis)
    return lax.ppermute(value, axis, [(i, (i + by) % peers) for i in range(peers)])


def turned_edge(tile, turns, width, east):
    size = tile.shape[0]

    def columns(x):
        return x[:, size - width :] if east else x[:, :width]

    sides = (
        columns(tile),
        columns(jnp.rot90(tile, 1)),
        columns(jnp.rot90(tile, 2)),
        columns(jnp.rot90(tile, 3)),
    )
    result = sides[0]
    for quarter in range(1, 4):
        result = jnp.where(turns == quarter, sides[quarter], result)
    return result


def seam_pad(tile, my_turn, next_turn, margin, row_tiles):
    came_west = shifted(turned_edge(tile, next_turn, margin, True), "space", 1)
    came_east = shifted(turned_edge(tile, (4 - my_turn) % 4, margin, False), "space", -1)
    widened = jnp.concatenate([came_west, tile, came_east], axis=1)
    came_north = shifted(widened[-margin:], "space", row_tiles)
    came_south = shifted(widened[:margin], "space", -row_tiles)
    return jnp.concatenate([came_north, widened, came_south], axis=0)


def swap(value, axis):
    return lax.all_to_all(value, axis, 0, 0, tiled=True)


def body(
    initial_state,
    starting_field_nudges,
    verifying_analysis,
    seam_turns,
    w_in,
    b_in,
    w_depth,
    b_depth,
    norm_gain,
    norm_shift,
    w_up,
    b_up,
    w_down,
    b_down,
    head_weight,
    head_bias,
):
    spaces = lax.axis_size("space")
    members = lax.axis_size("ens")
    row_tiles = spaces // 4
    tile_index = lax.axis_index("space")

    def turn_at(offset):
        return lax.dynamic_index_in_dim(seam_turns, (tile_index + offset) % spaces, keepdims=False)

    my_turn = turn_at(0)
    next_turn = turn_at(1)
    turns = jnp.stack(
        [
            my_turn,
            (4 - next_turn) % 4,
            turn_at(spaces - row_tiles),
            (4 - turn_at(spaces - row_tiles + 1)) % 4,
            turn_at(row_tiles),
            (4 - turn_at(row_tiles + 1)) % 4,
        ]
    )
    source = (
        initial_state.astype(F32) + starting_field_nudges[0].astype(F32)
    ).astype(BF16).reshape(SIDE, SIDE, 96)
    near = seam_pad(source, my_turn, next_turn, 1, row_tiles)
    wide_source = seam_pad(near, my_turn, next_turn, 5, row_tiles)
    weights = (
        w_in, b_in, w_depth, b_depth, norm_gain, norm_shift, w_up, b_up, w_down, b_down, head_weight, head_bias
    )
    saved, head_wide, w_depth_wide = run_forward(turns, wide_source, weights, members)
    patches, stem, normed, inverse, scaled, slope, active, hidden, field, tight, sent = saved
    every = swap(sent, "ens")
    predicted = field[:, :96].reshape(1, SIDE, SIDE * 96)
    target = verifying_analysis.reshape(4, 144, 96).transpose(1, 0, 2).reshape(144, 384)
    coefficient = 1.0 / math.sqrt(spaces * CELLS * 96)
    early, out_part, hidden_grad, scaled_grad, early_small = run_mixer_backward(
        every, tight, target, (hidden, active, slope, scaled), head_wide, w_down, w_up, coefficient
    )
    early_sum = jnp.sum(swap(early, "ens").astype(F32), axis=0).astype(BF16)
    late = run_depth_backward(
        scaled_grad, normed, inverse, norm_gain, hidden_grad, stem, w_depth_wide, patches, early_small, out_part
    )
    late_sum = jnp.sum(swap(late.reshape(8, 32, 1280), "ens").astype(F32), axis=0)
    early_mine = jnp.sum(swap(early_sum, "space").astype(F32), axis=0)
    late_mine = jnp.sum(swap(late_sum, "space"), axis=0)
    mine = jnp.concatenate([early_mine.reshape(2048), late_mine])
    whole = swap(jnp.broadcast_to(mine, (members, 3328)), "ens")
    early_whole = whole[:, :2048].reshape(8, 16, LANE)
    late_whole = whole[:, 2048:]
    small = late_whole[:, 896:960] + late_whole[:, 960:1024]
    return (
        predicted,
        late_whole[:, :864].T,
        small[:, 52],
        small[:, :49].T,
        small[:, 49],
        small[:, 50],
        small[:, 51],
        early_whole[:, 8:].reshape(4, 2, 8, LANE).transpose(1, 3, 0, 2).reshape(256, 32),
        small[:, 54:58].reshape(32),
        early_whole[:, :8].transpose(0, 2, 1).reshape(1024, 8),
        small[:, 53],
        late_whole[:3, 1024:].T,
        small[:3, 58],
    )


def solution(mesh):
    return jax.shard_map(
        body,
        mesh=mesh,
        in_specs=(
            P("space", None),
            P("ens", "space", None),
            P("space", None),
            P(),
            P(),
            P(),
            P(),
            P(),
            P(),
            P(),
            P(),
            P(),
            P(),
            P(),
            P(),
            P(),
        ),
        out_specs=(
            P("ens", "space", None),
            P(None, "space"),
            P("space"),
            P(None, "space"),
            P("space"),
            P("space"),
            P("space"),
            P(None, "space"),
            P("space"),
            P(None, "space"),
            P("space"),
            P(None, "space"),
            P("space"),
        ),
        check_vma=False,
    )
```

profile of v0, /device:TPU:2, one launch (start us, length us, event | category | flops | bytes accessed | tf_op | source)
XLA Modules:
  0.0 193.4 jit_solution(11148589389747110695)
XLA Ops:
  0.7 1.5 fusion.28
  2.9 1.0 fusion.16
  6.5 8.0 %collective-permute-start.1 = (bf16[24,1,96]{2,0,1:T(8,128)(2,1)S(1)}, bf16[24,1,96]{2,0,1:T(8,128)(2,1)S(1)}, u32[]{:S(2)}, u32[]{:S(2)}) collective-permute-start(bf16[24,1,96]{2,0,1:T(8,128)(2,1)S(1)} %get-tuple-element.63), channel_id=1, source_target_pairs={{0,248},{8,0},{16,8},{24,16},{32,24},{40,32},{48,40},{56,48},{64,5... | collective-permute-start | bytes 13832 | tf_op jit(solution)/shard_map/ppermute | solution.py:517
  14.5 1.2 collective-permute-done
  15.9 4.9 %collective-permute-start.3 = (bf16[1,26,96]{2,0,1:T(2,128)(2,1)S(1)}, bf16[1,26,96]{2,0,1:T(2,128)(2,1)S(1)}, u32[]{:S(2)}, u32[]{:S(2)}) collective-permute-start(bf16[1,26,96]{2,0,1:T(2,128)(2,1)S(1)} %get-tuple-element.62), channel_id=1, source_target_pairs={{0,192},{8,200},{16,208},{24,216},{32,224},{40,232},{48,240},{56,2... | collective-permute-start | bytes 14984 | tf_op jit(solution)/shard_map/ppermute | solution.py:517
  20.8 1.2 collective-permute-start.2
  21.9 1.7 collective-permute-done.3
  23.6 7.2 %collective-permute-done.2 = bf16[1,26,96]{2,0,1:T(2,128)(2,1)S(1)} collective-permute-done((bf16[1,26,96]{2,0,1:T(2,128)(2,1)S(1)}, bf16[1,26,96]{2,0,1:T(2,128)(2,1)S(1)}, u32[]{:S(2)}, u32[]{:S(2)}) %collective-permute-start.2) | collective-permute-done | bytes 5024 | tf_op jit(solution)/shard_map/ppermute | solution.py:517
  33.2 5.6 %collective-permute-done.4 = bf16[26,5,96]{2,1,0:T(8,128)(2,1)S(1)} collective-permute-done((bf16[26,5,96]{2,1,0:T(8,128)(2,1)S(1)}, bf16[26,5,96]{2,1,0:T(8,128)(2,1)S(1)}, u32[]{:S(2)}, u32[]{:S(2)}) %collective-permute-start.4) | collective-permute-done | bytes 24992 | tf_op jit(solution)/shard_map/ppermute | solution.py:517
  38.9 2.7 %collective-permute-start.7 = (bf16[5,36,96]{2,1,0:T(8,128)(2,1)S(1)}, bf16[5,36,96]{2,1,0:T(8,128)(2,1)S(1)}, u32[]{:S(2)}, u32[]{:S(2)}) collective-permute-start(bf16[5,36,96]{2,1,0:T(8,128)(2,1)S(1)} %get-tuple-element.51), channel_id=1, source_target_pairs={{0,192},{8,200},{16,208},{24,216},{32,224},{40,232},{48,240},{56,2... | collective-permute-start | bytes 103688 | tf_op jit(solution)/shard_map/ppermute | solution.py:517
  41.6 3.3 %collective-permute-start.6 = (bf16[5,36,96]{2,1,0:T(8,128)(2,1)S(1)}, bf16[5,36,96]{2,1,0:T(8,128)(2,1)S(1)}, u32[]{:S(2)}, u32[]{:S(2)}) collective-permute-start(bf16[5,36,96]{2,1,0:T(8,128)(2,1)S(1)} %get-tuple-element.50), channel_id=1, source_target_pairs={{0,64},{8,72},{16,80},{24,88},{32,96},{40,104},{48,112},{56,120},{... | collective-permute-start | bytes 103688 | tf_op jit(solution)/shard_map/ppermute | solution.py:517
  51.0 0.9 pad.25
  52.9 0.8 reshape.171.target_ref
  53.6 2.5 %stack.18.turns_ref = s32[6]{0:T(128)} concatenate(s32[1]{0:T(128)} %get-tuple-element.74, s32[1]{0:T(128)} %bitcast.1, s32[1]{0:T(128)} %get-tuple-element.72, s32[1]{0:T(128)} %bitcast.3, s32[1]{0:T(128)} %get-tuple-element.75, s32[1]{0:T(128)} %bitcast.5), dimensions={0} | concatenate | bytes 48 | tf_op jit(solution)/shard_map/stack | solution.py:579
  56.2 1.0 fusion.8.source_ref
  57.2 14.4 %shard_map.255 = (bf16[960,1152]{1,0:T(8,128)(2,1)}, f32[2,30,32,128]{3,2,1,0:T(8,128)}, f32[576,256]{1,0:T(8,128)}, f32[576,128]{1,0:T(8,128)}, bf16[576,256]{1...) custom-call(s32[6]{0:T(128)} %stack.18.turns_ref, ...), custom_call_target="tpu_custom_call" | custom-call | flops 2000000000 | bytes 8000000 | tf_op jit(solution)/shard_map/pallas_call | solution.py:389
  71.6 4.9 %all-to-all-start = ((bf16[8,144,384]{2,1,0:T(8,128)(2,1)}), bf16[8,144,384]{2,1,0:T(8,128)(2,1)S(1)}, u32[]{:S(2)}, u32[]{:S(2)}) async-start(bf16[8,144,384]{2,1,0:T(8,128)(2,1)} %get-tuple-element.30), calls=%async_computation | async-start | bytes 1769472 | tf_op jit(solution)/shard_map/all_to_all | solution.py:548
  77.9 8.1 %all-to-all-done.every_ref = bf16[8,144,384]{2,1,0:T(8,128)(2,1)S(1)} async-done(((bf16[8,144,384]{2,1,0:T(8,128)(2,1)}), bf16[8,144,384]{2,1,0:T(8,128)(2,1)S(1)}, u32[]{:S(2)}, u32[]{:S(2)}) %all-to-all-start) | async-done | bytes 884768 | tf_op jit(solution)/shard_map/all_to_all | solution.py:548
  86.0 1.0 copy-done
  87.0 9.3 %shard_map.256 = (bf16[8,32,16,128]{3,2,1,0:T(8,128)(2,1)}, bf16[256,256]{1,0:T(8,128)(2,1)}, f32[576,256]{1,0:T(8,128)}, f32[576,256]{1,0:T(8,128)}, f32[8,256]{1,0:T(8,128)}) custom-call(bf16[8,144,384]{2,1,0:T(8,128)(2,1)} %copy-done, f32[144,384]{1,0:T(8,128)} %get-tuple-element.31.own_ref, bf16[144,384]{1,0:T(8,128)(2,1)} %reshape.171.target_ref, ...), custom_call_target="tpu_custom_call" | custom-call | flops 3000000000 | bytes 8000000 | tf_op jit(solution)/shard_map/pallas_call | solution.py:389
  96.3 13.6 %shard_map.257 = bf16[256,1280]{1,0:T(8,128)(2,1)} custom-call(f32[576,256]{1,0:T(8,128)} %get-tuple-element.37.scaled_grad_ref, f32[576,256]{1,0:T(8,128)} %get-tuple-element.38.normed_ref, f32[576,128]{1,0:T(8,128)} %get-tuple-element.39.inverse_ref, f32[1,256]{1,0:T(1,128)} %bitcast.78, f32[576,256]{1,0:T(8,128)} %get-tuple-element.40.hidden_grad_ref, ...), custom_call_target="tpu_custom_call" | custom-call | flops 3000000000 | bytes 8000000 | tf_op jit(solution)/shard_map/pallas_call | solution.py:389
  109.9 13.1 %all_to_all.38 = bf16[8,32,1280]{2,1,0:T(8,128)(2,1)S(1)} all-to-all(bf16[8,32,1280]{2,1,0:T(8,128)(2,1)} %bitcast.61), channel_id=1, replica_groups=mesh['space'=32,'ens'=8] {'ens'}, dimensions={0} | all-to-all | bytes 1310720 | tf_op jit(solution)/shard_map/all_to_all | solution.py:548
  123.0 4.4 %all-to-all-start.1 = ((bf16[8,32,16,128]{3,2,1,0:T(8,128)(2,1)}), bf16[8,32,16,128]{3,2,1,0:T(8,128)(2,1)S(1)}, u32[]{:S(2)}, u32[]{:S(2)}) async-start(bf16[8,32,16,128]{3,2,1,0:T(8,128)(2,1)} %get-tuple-element.36), calls=%async_computation.1 | async-start | bytes 2097152 | tf_op jit(solution)/shard_map/all_to_all | solution.py:548
  128.3 9.5 %all-to-all-done.1 = bf16[8,32,16,128]{3,2,1,0:T(8,128)(2,1)S(1)} async-done(((bf16[8,32,16,128]{3,2,1,0:T(8,128)(2,1)}), bf16[8,32,16,128]{3,2,1,0:T(8,128)(2,1)S(1)}, u32[]{:S(2)}, u32[]{:S(2)}) %all-to-all-start.1) | async-done | bytes 1048608 | tf_op jit(solution)/shard_map/all_to_all | solution.py:548
  137.8 11.4 %all-to-all-start.4 = ((f32[32,1,1280]{2,1,0:T(1,128)}), f32[32,1,1280]{2,1,0:T(1,128)S(1)}, u32[]{:S(2)}, u32[]{:S(2)}) async-start(f32[32,1,1280]{2,1,0:T(1,128)} %all_to_all.28), calls=%async_computation.4 | async-start | bytes 327680 | tf_op jit(solution)/shard_map/all_to_all | solution.py:548
  149.2 0.8 reduce_sum.39
  150.0 11.8 %all-to-all-done.4 = f32[32,1,1280]{2,1,0:T(1,128)S(1)} async-done(((f32[32,1,1280]{2,1,0:T(1,128)}), f32[32,1,1280]{2,1,0:T(1,128)S(1)}, u32[]{:S(2)}, u32[]{:S(2)}) %all-to-all-start.4) | async-done | bytes 163872 | tf_op jit(solution)/shard_map/all_to_all | solution.py:548
  161.8 3.9 %all-to-all-start.2 = ((bf16[32,16,128]{2,1,0:T(8,128)(2,1)}), bf16[32,16,128]{2,1,0:T(8,128)(2,1)S(1)}, u32[]{:S(2)}, u32[]{:S(2)}) async-start(bf16[32,16,128]{2,1,0:T(8,128)(2,1)} %reduce_sum.39), calls=%async_computation.2 | async-start | bytes 262144 | tf_op jit(solution)/shard_map/all_to_all | solution.py:548
  165.8 11.8 %all-to-all-done.2 = bf16[32,16,128]{2,1,0:T(8,128)(2,1)S(1)} async-done(((bf16[32,16,128]{2,1,0:T(8,128)(2,1)}), bf16[32,16,128]{2,1,0:T(8,128)(2,1)S(1)}, u32[]{:S(2)}, u32[]{:S(2)}) %all-to-all-start.2) | async-done | bytes 131104 | tf_op jit(solution)/shard_map/all_to_all | solution.py:548
  178.4 4.4 %all-to-all-start.5 = ((f32[8,1,3328]{2,1,0:T(1,128)}), f32[8,1,3328]{2,1,0:T(1,128)S(1)}, u32[]{:S(2)}, u32[]{:S(2)}) async-start(f32[8,1,3328]{2,1,0:T(1,128)} %broadcast_in_dim.2), calls=%async_computation.5 | async-start | bytes 212992 | tf_op jit(solution)/shard_map/all_to_all | solution.py:548
  182.8 0.8 reshape.169
  183.7 4.5 %all-to-all-done.5 = f32[8,1,3328]{2,1,0:T(1,128)S(1)} async-done(((f32[8,1,3328]{2,1,0:T(1,128)}), f32[8,1,3328]{2,1,0:T(1,128)S(1)}, u32[]{:S(2)}, u32[]{:S(2)}) %all-to-all-start.5) | async-done | bytes 106528 | tf_op jit(solution)/shard_map/all_to_all | solution.py:548
  (92 shorter events, 16.5 us)
Async XLA Ops:
  3.9 28.3 %copy-start.5 = (bf16[49,256]{1,0:T(8,128)(2,1)S(1)}, bf16[49,256]{1,0:T(8,128)(2,1)}, u32[]{:S(2)}) copy-start(bf16[49,256]{1,0:T(8,128)(2,1)} %param.22) | copy-start | bytes 75268
  4.1 40.8 %copy-start.7 = (bf16[96]{0:T(256)(128)(2,1)S(1)}, bf16[96]{0:T(256)(128)(2,1)}, u32[]{:S(2)}) copy-start(bf16[96]{0:T(256)(128)(2,1)} %param.31) | copy-start | bytes 580
  4.1 43.4 %copy-start.8 = (bf16[256]{0:T(256)(128)(2,1)S(1)}, bf16[256]{0:T(256)(128)(2,1)}, u32[]{:S(2)}) copy-start(bf16[256]{0:T(256)(128)(2,1)} %param.21) | copy-start | bytes 1540
  4.1 43.9 %copy-start.9 = (bf16[256]{0:T(256)(128)(2,1)S(1)}, bf16[256]{0:T(256)(128)(2,1)}, u32[]{:S(2)}) copy-start(bf16[256]{0:T(256)(128)(2,1)} %param.23) | copy-start | bytes 1540
  4.2 44.5 %copy-start.10 = (bf16[256]{0:T(256)(128)(2,1)S(1)}, bf16[256]{0:T(256)(128)(2,1)}, u32[]{:S(2)}) copy-start(bf16[256]{0:T(256)(128)(2,1)} %param.24) | copy-start | bytes 1540
  4.2 45.0 %copy-start.11 = (bf16[256]{0:T(256)(128)(2,1)S(1)}, bf16[256]{0:T(256)(128)(2,1)}, u32[]{:S(2)}) copy-start(bf16[256]{0:T(256)(128)(2,1)} %param.25) | copy-start | bytes 1540
  4.2 45.6 %copy-start.6 = (bf16[1024]{0:T(1024)(128)(2,1)S(1)}, bf16[1024]{0:T(1024)(128)(2,1)}, u32[]{:S(2)}) copy-start(bf16[1024]{0:T(1024)(128)(2,1)} %param.27) | copy-start | bytes 6148
  4.2 46.2 %copy-start.12 = (bf16[256]{0:T(256)(128)(2,1)S(1)}, bf16[256]{0:T(256)(128)(2,1)}, u32[]{:S(2)}) copy-start(bf16[256]{0:T(256)(128)(2,1)} %param.29) | copy-start | bytes 1540
  4.2 46.7 %copy-start.4 = (bf16[256,96]{0,1:T(8,128)(2,1)S(1)}, bf16[256,96]{0,1:T(8,128)(2,1)}, u32[]{:S(2)}) copy-start(bf16[256,96]{0,1:T(8,128)(2,1)} %param.30) | copy-start | bytes 147460
  4.2 46.8 %copy-start.1 = (bf16[864,256]{1,0:T(8,128)(2,1)S(1)}, bf16[864,256]{1,0:T(8,128)(2,1)}, u32[]{:S(2)}) copy-start(bf16[864,256]{1,0:T(8,128)(2,1)} %param.20) | copy-start | bytes 1327108
  6.4 9.3 %collective-permute-start = (bf16[24,1,96]{2,0,1:T(8,128)(2,1)S(1)}, bf16[24,1,96]{2,0,1:T(8,128)(2,1)S(1)}, u32[]{:S(2)}, u32[]{:S(2)}) collective-permute-start(bf16[24,1,96]{2,0,1:T(8,128)(2,1)S(1)} %slice_select_fusion.2), channel_id=1, source_target_pairs={{0,8},{8,16},{16,24},{24,32},{32,40},{40,48},{48,56},{56,64},{64,7... | collective-permute-start | bytes 13832 | tf_op jit(solution)/shard_map/ppermute | solution.py:517
  6.5 9.3 %collective-permute-start.1 = (bf16[24,1,96]{2,0,1:T(8,128)(2,1)S(1)}, bf16[24,1,96]{2,0,1:T(8,128)(2,1)S(1)}, u32[]{:S(2)}, u32[]{:S(2)}) collective-permute-start(bf16[24,1,96]{2,0,1:T(8,128)(2,1)S(1)} %get-tuple-element.63), channel_id=1, source_target_pairs={{0,248},{8,0},{16,8},{24,16},{32,24},{40,32},{48,40},{56,48},{64,5... | collective-permute-start | bytes 13832 | tf_op jit(solution)/shard_map/ppermute | solution.py:517
  15.9 7.7 %collective-permute-start.3 = (bf16[1,26,96]{2,0,1:T(2,128)(2,1)S(1)}, bf16[1,26,96]{2,0,1:T(2,128)(2,1)S(1)}, u32[]{:S(2)}, u32[]{:S(2)}) collective-permute-start(bf16[1,26,96]{2,0,1:T(2,128)(2,1)S(1)} %get-tuple-element.62), channel_id=1, source_target_pairs={{0,192},{8,200},{16,208},{24,216},{32,224},{40,232},{48,240},{56,2... | collective-permute-start | bytes 14984 | tf_op jit(solution)/shard_map/ppermute | solution.py:517
  20.8 31.8 %copy-start.3 = (bf16[24,2304]{1,0:T(8,128)(2,1)S(1)}, bf16[24,2304]{1,0:T(8,128)(2,1)}, u32[]{:S(2)}) copy-start(bf16[24,2304]{1,0:T(8,128)(2,1)} %param.18) | copy-start | bytes 331780
  20.8 10.0 %collective-permute-start.2 = (bf16[1,26,96]{2,0,1:T(2,128)(2,1)S(1)}, bf16[1,26,96]{2,0,1:T(2,128)(2,1)S(1)}, u32[]{:S(2)}, u32[]{:S(2)}) collective-permute-start(bf16[1,26,96]{2,0,1:T(2,128)(2,1)S(1)} %get-tuple-element.61), channel_id=1, source_target_pairs={{0,64},{8,72},{16,80},{24,88},{32,96},{40,104},{48,112},{56,120},{... | collective-permute-start | bytes 14984 | tf_op jit(solution)/shard_map/ppermute | solution.py:517
  31.4 1.9 collective-permute-start.5
  31.6 7.3 %collective-permute-start.4 = (bf16[26,5,96]{2,1,0:T(8,128)(2,1)S(1)}, bf16[26,5,96]{2,1,0:T(8,128)(2,1)S(1)}, u32[]{:S(2)}, u32[]{:S(2)}) collective-permute-start(bf16[26,5,96]{2,1,0:T(8,128)(2,1)S(1)} %fusion.20), channel_id=1, source_target_pairs={{0,8},{8,16},{16,24},{24,32},{32,40},{40,48},{48,56},{56,64},{64,7... | collective-permute-start | bytes 74888 | tf_op jit(solution)/shard_map/ppermute | solution.py:517
  38.9 17.3 %collective-permute-start.7 = (bf16[5,36,96]{2,1,0:T(8,128)(2,1)S(1)}, bf16[5,36,96]{2,1,0:T(8,128)(2,1)S(1)}, u32[]{:S(2)}, u32[]{:S(2)}) collective-permute-start(bf16[5,36,96]{2,1,0:T(8,128)(2,1)S(1)} %get-tuple-element.51), channel_id=1, source_target_pairs={{0,192},{8,200},{16,208},{24,216},{32,224},{40,232},{48,240},{56,2... | collective-permute-start | bytes 103688 | tf_op jit(solution)/shard_map/ppermute | solution.py:517
  41.6 14.6 %collective-permute-start.6 = (bf16[5,36,96]{2,1,0:T(8,128)(2,1)S(1)}, bf16[5,36,96]{2,1,0:T(8,128)(2,1)S(1)}, u32[]{:S(2)}, u32[]{:S(2)}) collective-permute-start(bf16[5,36,96]{2,1,0:T(8,128)(2,1)S(1)} %get-tuple-element.50), channel_id=1, source_target_pairs={{0,64},{8,72},{16,80},{24,88},{32,96},{40,104},{48,112},{56,120},{... | collective-permute-start | bytes 103688 | tf_op jit(solution)/shard_map/ppermute | solution.py:517
  71.6 14.4 %all-to-all-start = ((bf16[8,144,384]{2,1,0:T(8,128)(2,1)}), bf16[8,144,384]{2,1,0:T(8,128)(2,1)S(1)}, u32[]{:S(2)}, u32[]{:S(2)}) async-start(bf16[8,144,384]{2,1,0:T(8,128)(2,1)} %get-tuple-element.30), calls=%async_computation | async-start | bytes 1769472 | tf_op jit(solution)/shard_map/all_to_all | solution.py:548
  86.0 1.0 copy-start
  123.0 14.8 %all-to-all-start.1 = ((bf16[8,32,16,128]{3,2,1,0:T(8,128)(2,1)}), bf16[8,32,16,128]{3,2,1,0:T(8,128)(2,1)S(1)}, u32[]{:S(2)}, u32[]{:S(2)}) async-start(bf16[8,32,16,128]{3,2,1,0:T(8,128)(2,1)} %get-tuple-element.36), calls=%async_computation.1 | async-start | bytes 2097152 | tf_op jit(solution)/shard_map/all_to_all | solution.py:548
  127.4 55.4 %copy-start.2 = (f32[576,128]{1,0:T(8,128)S(1)}, f32[576,128]{1,0:T(8,128)}, u32[]{:S(2)}) copy-start(f32[576,128]{1,0:T(8,128)} %get-tuple-element.29) | copy-start | bytes 884740
  137.8 24.1 %all-to-all-start.4 = ((f32[32,1,1280]{2,1,0:T(1,128)}), f32[32,1,1280]{2,1,0:T(1,128)S(1)}, u32[]{:S(2)}, u32[]{:S(2)}) async-start(f32[32,1,1280]{2,1,0:T(1,128)} %all_to_all.28), calls=%async_computation.4 | async-start | bytes 327680 | tf_op jit(solution)/shard_map/all_to_all | solution.py:548
  161.8 15.8 %all-to-all-start.2 = ((bf16[32,16,128]{2,1,0:T(8,128)(2,1)}), bf16[32,16,128]{2,1,0:T(8,128)(2,1)S(1)}, u32[]{:S(2)}, u32[]{:S(2)}) async-start(bf16[32,16,128]{2,1,0:T(8,128)(2,1)} %reduce_sum.39), calls=%async_computation.2 | async-start | bytes 262144 | tf_op jit(solution)/shard_map/all_to_all | solution.py:548
  178.4 9.8 %all-to-all-start.5 = ((f32[8,1,3328]{2,1,0:T(1,128)}), f32[8,1,3328]{2,1,0:T(1,128)S(1)}, u32[]{:S(2)}, u32[]{:S(2)}) async-start(f32[8,1,3328]{2,1,0:T(1,128)} %broadcast_in_dim.2), calls=%async_computation.5 | async-start | bytes 212992 | tf_op jit(solution)/shard_map/all_to_all | solution.py:548
where the time goes:
time: 194 us; the launch traced here: 193 us
  waiting for transfers between devices  62 us (32%)
  starting transfers between devices  49.8 us (26%)
  Pallas kernels  37.3 us (19%)
  local copies, waits for them, and re-layouts  16.2 us (8%)
  blocking collectives  13.1 us (7%)
  other arithmetic  9.38 us (5%)
  between operations  5.7 us (3%)
    all_to_all x5, waiting for transfers between devices, swap(): return lax.all_to_all(value, axis, 0, 0, tiled=True)  45.8 us
    pallas_call x3, Pallas kernels, call(): pl.pallas_call(kernel, out_shape=[jax.ShapeDtypeStruct(s, d) for s, d in...  37.3 us
    all_to_all x5, starting transfers between devices, swap(): return lax.all_to_all(value, axis, 0, 0, tiled=True)  29.1 us
    ppermute x8, starting transfers between devices, shifted(): lax.ppermute(value, axis, [(i, (i + by) % peers) for i in range(peers)])  20.8 us
    ppermute x8, waiting for transfers between devices, shifted(): lax.ppermute(value, axis, [(i, (i + by) % peers) for i in range(peers)])  16.2 us
    all_to_all x1, blocking collectives, swap(): return lax.all_to_all(value, axis, 0, 0, tiled=True)  13.1 us
  transfers between devices with their start and end apart: 13, of which 11 were waited for; matrix products, arithmetic and copies ran while one was open for 7% of the time, Pallas kernels for 0%

commit v1 on v0

--- a/solution.py
+++ b/solution.py
@@ -18,7 +18,7 @@
 CELLS = SIDE * SIDE
 LANE = 128
 SMALL = 64
-VMEM_BYTES = 56 * 1024 * 1024
+VMEM_BYTES = 24 * 1024 * 1024
 
 
 def dot(left, right, left_dim=1, right_dim=0):
@@ -40,7 +40,7 @@
     )[quarter]
 
 
-def gather_patches(turns_ref, wide_ref, stage_ref, patches_ref):
+def gather_patches(turns, wide_ref, stage_ref, patches_ref):
     bands = ((0, 0, 3), (3, 5, SIDE), (27, 31, 3))
     turn_of = {(1, 0): 0, (1, 2): 1, (0, 0): 2, (0, 2): 3, (2, 0): 4, (2, 2): 5}
     stage_ref[...] = jnp.zeros_like(stage_ref)
@@ -59,7 +59,7 @@
 
                     piece = read(0)
                     if (row_band, col_band) in turn_of:
-                        turn = turns_ref[turn_of[row_band, col_band]]
+                        turn = turns[turn_of[row_band, col_band]]
                         for quarter in range(1, 4):
                             piece = jnp.where(turn == quarter, read(quarter), piece)
                     stage_ref[row_to : row_to + row_len, col_to : col_to + col_len, :] = piece
@@ -68,20 +68,14 @@
 
 
 def forward_kernel(
-    turns_ref,
+    seam_turns_ref,
     source_ref,
     w_in_ref,
-    b_in_ref,
-    w_depth_ref,
-    b_depth_ref,
-    gain_ref,
-    shift_ref,
+    w_depth_low_ref,
+    vectors_ref,
     w_up_ref,
-    b_up_ref,
     w_down_ref,
-    b_down_ref,
     head_ref,
-    head_bias_ref,
     patches_ref,
     stem_ref,
     normed_ref,
@@ -93,14 +87,39 @@
     field_ref,
     tight_ref,
     sent_ref,
+    w_depth_ref,
     wide_ref,
     stage_ref,
+    w_in_wide_ref,
 ):
-    wide_ref[...] = source_ref[...].astype(F32)
-    gather_patches(turns_ref, wide_ref, stage_ref, patches_ref)
+    tile = lax.axis_index("space")
+    tiles = seam_turns_ref.shape[0]
+    across = tiles // 4
+
+    def turn_at(offset):
+        return seam_turns_ref[lax.rem(tile + (tiles + offset), tiles)]
+
+    turns = (
+        turn_at(0),
+        (4 - turn_at(1)) & 3,
+        turn_at(-across),
+        (4 - turn_at(1 - across)) & 3,
+        turn_at(across),
+        (4 - turn_at(across + 1)) & 3,
+    )
+    b_in, b_depth, gain, shift, b_down = (vectors_ref[k : k + 1, :] for k in range(5))
+    head_bias = vectors_ref[5:6, 0:96]
+    b_up = jnp.concatenate([vectors_ref[6 + k : 7 + k, :] for k in range(4)], axis=1)
+    w_depth_ref[...] = w_depth_low_ref[...].astype(F32)
+    for offset in range(9):
+        w_in_wide_ref[offset * LANE : offset * LANE + 96, :] = w_in_ref[offset * 96 : (offset + 1) * 96, :]
+        w_in_wide_ref[offset * LANE + 96 : (offset + 1) * LANE, :] = jnp.zeros((32, 256), BF16)
+    wide_ref[...] = jnp.zeros_like(wide_ref)
+    wide_ref[:, 0:36, 0:96] = source_ref[...].astype(F32)
+    gather_patches(turns, wide_ref, stage_ref, patches_ref)
     for part in range(5):
         rows = slice(part * 192, (part + 1) * 192)
-        stem = dot(patches_ref[rows, :], w_in_ref[...]) + b_in_ref[...]
+        stem = dot(patches_ref[rows, :], w_in_wide_ref[...]) + b_in
         stem = stem.astype(BF16).astype(F32)
         for half in range(2):
             stem_ref[half, part * 6 : (part + 1) * 6] = stem[
@@ -118,7 +137,7 @@
                 for row_off in range(7):
                     tap = 7 * row_off + col_off
                     total = total + slab[row_off : row_off + 4] * w_depth_ref[tap : tap + 1, lanes][None]
-            halves.append(total.reshape(4 * SIDE, LANE) + b_depth_ref[:, lanes])
+            halves.append(total.reshape(4 * SIDE, LANE) + b_depth[:, lanes])
         mean = (
             jnp.sum(halves[0], axis=-1, keepdims=True) + jnp.sum(halves[1], axis=-1, keepdims=True)
         ) / 256.0
@@ -134,14 +153,14 @@
             lanes = slice(half * LANE, (half + 1) * LANE)
             normed = centers[half] * inverse
             normed_ref[at, lanes] = normed
-            scaled_ref[at, lanes] = (normed * gain_ref[:, lanes] + shift_ref[:, lanes]).astype(BF16)
+            scaled_ref[at, lanes] = (normed * gain[:, lanes] + shift[:, lanes]).astype(BF16)
         return carry
 
     lax.fori_loop(0, 6, normalise, 0)
 
     def mix(part, carry):
         at = pl.ds(pl.multiple_of(part * 96, 96), 96)
-        upward = dot(scaled_ref[at, :], w_up_ref[...]) + b_up_ref[...]
+        upward = dot(scaled_ref[at, :], w_up_ref[...]) + b_up
         square = upward * upward
         tanh_part = jnp.tanh(ROOT * (upward + CUBIC * square * upward))
         plus = 0.5 * (1.0 + tanh_part)
@@ -155,15 +174,15 @@
             for half in range(2)
         ]
         own = jnp.concatenate(own, axis=1)
-        hidden = (own + dot(active, w_down_ref[...]) + b_down_ref[...]).astype(BF16)
+        hidden = (own + dot(active, w_down_ref[...]) + b_down).astype(BF16)
         hidden_ref[at, :] = hidden
-        field_ref[at, :] = dot(hidden, head_ref[...]) + head_bias_ref[...]
+        field_ref[at, :] = dot(hidden, head_ref[...], 1, 1) + head_bias
         return carry
 
     lax.fori_loop(0, 6, mix, 0)
     for quarter in range(4):
         tight_ref[:, 96 * quarter : 96 * (quarter + 1)] = field_ref[
-            144 * quarter : 144 * (quarter + 1), 0:96
+            144 * quarter : 144 * (quarter + 1), :
         ]
     sent = tight_ref[...].astype(BF16)
     for member in range(sent_ref.shape[0]):
@@ -215,7 +234,7 @@
     grad_f_low = grad_f.astype(BF16)
     picked = dot(grad_f_low, pick_ref[...]).astype(BF16)
     out_part_ref[...] = dot(picked, hidden_ref[...], 0, 0).astype(BF16)
-    grad_hidden = dot(grad_f_low, head_ref[...], 1, 1)
+    grad_hidden = dot(grad_f_low[:, 0:96], head_ref[...])
     hidden_grad_ref[...] = grad_hidden
     low_ref[...] = grad_hidden.astype(BF16)
     grad_b_down = jnp.sum(grad_hidden, axis=0, keepdims=True)
@@ -275,7 +294,7 @@
     scaled_grad_ref,
     normed_ref,
     inverse_ref,
-    gain_ref,
+    vectors_ref,
     hidden_grad_ref,
     stem_ref,
     w_depth_ref,
@@ -306,7 +325,7 @@
             normed = normed_ref[at, lanes]
             sums_ref[0, :, lanes] += jnp.sum((grad * normed).reshape(12, 8, LANE), axis=0)
             sums_ref[1, :, lanes] += jnp.sum(grad.reshape(12, 8, LANE), axis=0)
-            grad = grad * gain_ref[:, lanes]
+            grad = grad * vectors_ref[2:3, lanes]
             first = first + jnp.sum(grad, axis=-1, keepdims=True)
             second = second + jnp.sum(grad * normed, axis=-1, keepdims=True)
             halves.append((grad, normed))
@@ -383,6 +402,55 @@
     late_ref[:, 1024:1280] = out_part_ref[...]
 
 
+def combine_kernel(early_ref, late_ref, share_ref, rows_ref):
+    members = early_ref.shape[0]
+    early = early_ref[0].astype(F32)
+    late = late_ref[0].astype(F32)
+    for member in range(1, members):
+        early = early + early_ref[member].astype(F32)
+        late = late + late_ref[member].astype(F32)
+    rows_ref[:, 0:16, :] = early
+    rows_ref[:, 26:32, :] = jnp.zeros_like(rows_ref[:, 26:32, :])
+    for row in range(10):
+        piece = late[:, row * LANE : (row + 1) * LANE]
+        if row == 7:
+            piece = piece + jnp.concatenate([piece[:, SMALL:], jnp.zeros_like(piece[:, SMALL:])], axis=1)
+        rows_ref[:, 16 + row : 17 + row, :] = piece[:, None, :]
+    share_ref[...] = rows_ref[...].astype(BF16)
+
+
+def total_kernel(share_ref, copies_ref):
+    total = share_ref[0].astype(F32)
+    for tile in range(1, share_ref.shape[0]):
+        total = total + share_ref[tile].astype(F32)
+    for member in range(copies_ref.shape[0]):
+        copies_ref[member] = total
+
+
+def unpack_kernel(
+    whole_ref, w_in_ref, w_depth_ref, w_up_ref, w_down_ref, w_out_ref, small_ref, b_up_ref
+):
+    parts = whole_ref.shape[0]
+    for part in range(parts):
+        for row in range(7):
+            lanes = slice(row * LANE, min((row + 1) * LANE, 864))
+            w_in_ref[part : part + 1, lanes] = whole_ref[part, 16 + row : 17 + row, 0 : lanes.stop - lanes.start]
+        w_down_ref[:, part * LANE : (part + 1) * LANE] = whole_ref[part, 0:8, :]
+        row_tile, lane_tile = divmod(part, 2)
+        w_up_ref[8 * row_tile : 8 * row_tile + 8, lane_tile * LANE : (lane_tile + 1) * LANE] = whole_ref[
+            part, 8:16, :
+        ]
+        w_depth_ref[part : part + 1, :] = whole_ref[part, 23:24, 0:49]
+        b_up_ref[0:1, 4 * part : 4 * part + 4] = whole_ref[part, 23:24, 54:58]
+    for part in range(3):
+        for half in range(2):
+            w_out_ref[part : part + 1, half * LANE : (half + 1) * LANE] = whole_ref[
+                part, 24 + half : 25 + half, :
+            ]
+    small = jnp.concatenate([whole_ref[part, 23:24, :] for part in range(parts)], axis=0)
+    small_ref[...] = small.T[48:64, :]
+
+
 def call(kernel, shapes, scratch, *operands, smem=0, flops=0):
     space = [pl.BlockSpec(memory_space=pltpu.SMEM)] * smem
     space += [pl.BlockSpec(memory_space=pltpu.VMEM)] * (len(operands) - smem)
@@ -397,18 +465,13 @@
     )(*operands)
 
 
-def row_of(values):
-    return values.astype(F32).reshape(1, -1)
-
-
-def run_forward(turns, wide_source, weights, members):
-    w_in, b_in, w_depth, b_depth, gain, shift, w_up, b_up, w_down, b_down, head, head_bias = weights
-    w_in_wide = jnp.pad(w_in.reshape(9, 96, 256), ((0, 0), (0, 32), (0, 0))).reshape(1152, 256)
-    source = jnp.pad(wide_source, ((0, 0), (0, 4), (0, 32)))
-    head_wide = jnp.pad(head, ((0, 0), (0, 32)))
-    bias_wide = jnp.pad(row_of(head_bias), ((0, 0), (0, 32)))
-    w_depth_wide = jnp.pad(w_depth.astype(F32), ((0, 7), (0, 0)))
-    outs = call(
+def stack_vectors(b_in, b_depth, gain, shift, b_down, head_bias, b_up):
+    rows = [b_in, b_depth, gain, shift, b_down, jnp.pad(head_bias, (0, 160)), b_up]
+    return jnp.concatenate(rows).astype(F32).reshape(10, 256)
+
+
+def run_forward(seam_turns, source, w_in, w_depth, vectors, w_up, w_down, head, members):
+    return call(
         forward_kernel,
         [
             ((960, 1152), BF16),
@@ -419,32 +482,26 @@
             ((CELLS, 1024), F32),
             ((CELLS, 1024), BF16),
             ((CELLS, 256), BF16),
-            ((CELLS, LANE), F32),
+            ((CELLS, 96), F32),
             ((144, 384), F32),
             ((members, 144, 384), BF16),
+            ((49, 256), F32),
         ],
-        [((36, 40, LANE), F32), ((30, 32, LANE), F32)],
-        turns,
+        [((36, 40, LANE), F32), ((30, 32, LANE), F32), ((1152, 256), BF16)],
+        seam_turns,
         source,
-        w_in_wide,
-        row_of(b_in),
-        w_depth_wide,
-        row_of(b_depth),
-        row_of(gain),
-        row_of(shift),
+        w_in,
+        w_depth,
+        vectors,
         w_up,
-        row_of(b_up),
         w_down,
-        row_of(b_down),
-        head_wide,
-        bias_wide,
+        head,
         smem=1,
-        flops=2_000_000_000,
-    )
-    return outs, head_wide, w_depth_wide
-
-
-def run_mixer_backward(every, tight, target, saved, head_wide, w_down, w_up, coefficient):
+        flops=10_000_000_000,
+    )
+
+
+def run_mixer_backward(every, tight, target, saved, head, w_down, w_up, coefficient):
     hidden, active, slope, scaled = saved
     column = jnp.arange(256)
     owner = 3 * (column % 32) + column // 32
@@ -470,19 +527,19 @@
         tight,
         target,
         hidden,
-        head_wide,
+        head,
         pick,
         active,
         slope,
         scaled,
         w_down,
         w_up,
-        flops=3_000_000_000,
+        flops=12_000_000_000,
     )
 
 
 def run_depth_backward(
-    scaled_grad, normed, inverse, gain, hidden_grad, stem, w_depth_wide, patches, early_small, out_part
+    scaled_grad, normed, inverse, vectors, hidden_grad, stem, w_depth, patches, early_small, out_part
 ):
     column = jnp.arange(256)
     order = (column[:, None] == (8 * (column % 32) + column // 32)[None, :]).astype(BF16)
@@ -500,16 +557,29 @@
         scaled_grad,
         normed,
         inverse,
-        row_of(gain),
+        vectors,
         hidden_grad,
         stem,
-        w_depth_wide,
+        w_depth,
         patches,
         order,
         early_small,
         out_part,
-        flops=3_000_000_000,
+        flops=12_000_000_000,
     )[0]
+
+
+def run_combine(early, late):
+    return call(combine_kernel, [((32, 32, LANE), BF16)], [((32, 32, LANE), F32)], early, late)[0]
+
+
+def run_total(share, members):
+    return call(total_kernel, [((members, 32, LANE), F32)], [], share)[0]
+
+
+def run_unpack(whole):
+    shapes = ((8, 864), (8, 49), (32, 256), (8, 1024), (3, 256), (16, 8), (1, 32))
+    return call(unpack_kernel, [(shape, F32) for shape in shapes], [], whole)
 
 
 def shifted(value, axis, by):
@@ -576,59 +646,45 @@
 
     my_turn = turn_at(0)
     next_turn = turn_at(1)
-    turns = jnp.stack(
-        [
-            my_turn,
-            (4 - next_turn) % 4,
-            turn_at(spaces - row_tiles),
-            (4 - turn_at(spaces - row_tiles + 1)) % 4,
-            turn_at(row_tiles),
-            (4 - turn_at(row_tiles + 1)) % 4,
-        ]
-    )
     source = (
         initial_state.astype(F32) + starting_field_nudges[0].astype(F32)
     ).astype(BF16).reshape(SIDE, SIDE, 96)
     near = seam_pad(source, my_turn, next_turn, 1, row_tiles)
     wide_source = seam_pad(near, my_turn, next_turn, 5, row_tiles)
-    weights = (
-        w_in, b_in, w_depth, b_depth, norm_gain, norm_shift, w_up, b_up, w_down, b_down, head_weight, head_bias
-    )
-    saved, head_wide, w_depth_wide = run_forward(turns, wide_source, weights, members)
-    patches, stem, normed, inverse, scaled, slope, active, hidden, field, tight, sent = saved
+    vectors = stack_vectors(b_in, b_depth, norm_gain, norm_shift, b_down, head_bias, b_up)
+    head = head_weight.T
+    saved = run_forward(seam_turns, wide_source, w_in, w_depth, vectors, w_up, w_down, head, members)
+    patches, stem, normed, inverse, scaled, slope, active, hidden, field, tight, sent, w_depth_wide = saved
+    sent, verifying_analysis, field_again = lax.optimization_barrier((sent, verifying_analysis, field))
     every = swap(sent, "ens")
-    predicted = field[:, :96].reshape(1, SIDE, SIDE * 96)
+    predicted = field_again.reshape(1, SIDE, SIDE * 96)
     target = verifying_analysis.reshape(4, 144, 96).transpose(1, 0, 2).reshape(144, 384)
     coefficient = 1.0 / math.sqrt(spaces * CELLS * 96)
     early, out_part, hidden_grad, scaled_grad, early_small = run_mixer_backward(
-        every, tight, target, (hidden, active, slope, scaled), head_wide, w_down, w_up, coefficient
-    )
-    early_sum = jnp.sum(swap(early, "ens").astype(F32), axis=0).astype(BF16)
+        every, tight, target, (hidden, active, slope, scaled), head, w_down, w_up, coefficient
+    )
     late = run_depth_backward(
-        scaled_grad, normed, inverse, norm_gain, hidden_grad, stem, w_depth_wide, patches, early_small, out_part
-    )
-    late_sum = jnp.sum(swap(late.reshape(8, 32, 1280), "ens").astype(F32), axis=0)
-    early_mine = jnp.sum(swap(early_sum, "space").astype(F32), axis=0)
-    late_mine = jnp.sum(swap(late_sum, "space"), axis=0)
-    mine = jnp.concatenate([early_mine.reshape(2048), late_mine])
-    whole = swap(jnp.broadcast_to(mine, (members, 3328)), "ens")
-    early_whole = whole[:, :2048].reshape(8, 16, LANE)
-    late_whole = whole[:, 2048:]
-    small = late_whole[:, 896:960] + late_whole[:, 960:1024]
+        scaled_grad, normed, inverse, vectors, hidden_grad, stem, w_depth_wide, patches, early_small, out_part
+    )
+    early_parts, late = lax.optimization_barrier((swap(early, "ens"), late))
+    late_parts = swap(late.reshape(8, 32, 1280), "ens")
+    shares = swap(run_combine(early_parts, late_parts), "space")
+    whole = swap(run_total(shares, members), "ens")
+    grad_w_in, grad_w_depth, grad_w_up, grad_w_down, grad_w_out, small, grad_b_up = run_unpack(whole)
     return (
         predicted,
-        late_whole[:, :864].T,
-        small[:, 52],
-        small[:, :49].T,
-        small[:, 49],
-        small[:, 50],
-        small[:, 51],
-        early_whole[:, 8:].reshape(4, 2, 8, LANE).transpose(1, 3, 0, 2).reshape(256, 32),
-        small[:, 54:58].reshape(32),
-        early_whole[:, :8].transpose(0, 2, 1).reshape(1024, 8),
-        small[:, 53],
-        late_whole[:3, 1024:].T,
-        small[:3, 58],
+        grad_w_in.T,
+        small[4],
+        grad_w_depth.T,
+        small[1],
+        small[2],
+        small[3],
+        grad_w_up.T,
+        grad_b_up[0],
+        grad_w_down.T,
+        small[5],
+        grad_w_out.T,
+        small[10, :3],
     )
 
 

time: 194 us -> 169 us (0.87)
  waiting for transfers between devices: 62 us -> 32.7 us
  blocking collectives: 13.1 us -> 32.8 us
  local copies, waits for them, and re-layouts: 16.2 us -> 31.7 us
  starting transfers between devices: 49.8 us -> 35.6 us
  other arithmetic: 9.38 us -> 1.52 us
  Pallas kernels: 37.3 us -> 29.7 us
  between operations: 5.7 us -> 3.67 us
    all_to_all x5 -> x3, waiting for transfers between devices: 45.8 us -> 10.4 us  [swap(): return lax.all_to_all(value, axis, 0, 0, tiled=True)]
    unnamed x32 -> x84, local copies, waits for them, and re-layouts: 1.87 us -> 23.9 us
    all_to_all x1 -> x2, blocking collectives: 13.1 us -> 32.8 us  [swap(): return lax.all_to_all(value, axis, 0, 0, tiled=True)]
    all_to_all x5 -> x3, starting transfers between devices: 29.1 us -> 14.8 us  [swap(): return lax.all_to_all(value, axis, 0, 0, tiled=True)]
    pallas_call x3 -> x6, Pallas kernels: 37.3 us -> 29.7 us  [call(): pl.pallas_call(kernel, out_shape=[jax.ShapeDtypeStruct(s, d) for s, d in...]
    ppermute x8, waiting for transfers between devices: 16.2 us -> 22.3 us  [shifted(): lax.ppermute(value, axis, [(i, (i + by) % peers) for i in range(peers)])]
    reshape x6 -> x0, other arithmetic: 3.4 us -> none  [row_of(): return values.astype(F32).reshape(1, -1)]
    another operation x1 -> x0, local copies, waits for them, and re-layouts: 2.54 us -> none  [body(): jnp.stack([my_turn, (4 - next_turn) % 4, turn_at(spaces - row_tiles), (4...]
  transfers between devices with their start and end apart: 13 -> 11, of which waited for: 11 -> 9; matrix products, arithmetic and copies ran while one was open for 7% -> 4% of each run, Pallas kernels for 0% -> 6%
where the time goes in v1:
time: 169 us; the launch traced here: 168 us
  starting transfers between devices  35.6 us (21%)
  blocking collectives  32.8 us (19%)
  waiting for transfers between devices  32.7 us (19%)
  local copies, waits for them, and re-layouts  31.7 us (19%)
  Pallas kernels  29.7 us (18%)
  between operations  3.67 us (2%)
    all_to_all x2, blocking collectives, swap(): return lax.all_to_all(value, axis, 0, 0, tiled=True)  32.8 us
    pallas_call x6, Pallas kernels, call(): pl.pallas_call(kernel, out_shape=[jax.ShapeDtypeStruct(s, d) for s, d in...  29.7 us
    unnamed x84, local copies, waits for them, and re-layouts  23.9 us
    ppermute x8, waiting for transfers between devices, shifted(): lax.ppermute(value, axis, [(i, (i + by) % peers) for i in range(peers)])  22.3 us
    ppermute x8, starting transfers between devices, shifted(): lax.ppermute(value, axis, [(i, (i + by) % peers) for i in range(peers)])  20.8 us
    all_to_all x3, starting transfers between devices, swap(): return lax.all_to_all(value, axis, 0, 0, tiled=True)  14.8 us
    all_to_all x3, waiting for transfers between devices, swap(): return lax.all_to_all(value, axis, 0, 0, tiled=True)  10.4 us
    reshape x3, local copies, waits for them, and re-layouts, body(): verifying_analysis.reshape(4, 144, 96).transpose(1, 0, 2).reshape(144, 384)  3.56 us
  transfers between devices with their start and end apart: 11, of which 9 were waited for; matrix products, arithmetic and copies ran while one was open for 4% of the time, Pallas kernels for 6%

profile of v1, /device:TPU:2, one launch (start us, length us, event | category | flops | bytes accessed | tf_op | source)
XLA Modules:
  0.0 167.7 jit_solution(17866081200983983393)
XLA Ops:
  0.7 1.3 fusion.13
  6.2 8.0 %collective-permute-start.1 = (bf16[24,1,96]{2,0,1:T(8,128)(2,1)S(1)}, bf16[24,1,96]{2,0,1:T(8,128)(2,1)S(1)}, u32[]{:S(2)}, u32[]{:S(2)}) collective-permute-start(bf16[24,1,96]{2,0,1:T(8,128)(2,1)S(1)} %get-tuple-element.84), channel_id=1, source_target_pairs={{0,248},{8,0},{16,8},{24,16},{32,24},{40,32},{48,40},{56,48},{64,5... | collective-permute-start | bytes 13832 | tf_op jit(solution)/shard_map/ppermute | solution.py:587
  14.2 1.2 collective-permute-done
  15.6 4.9 %collective-permute-start.3 = (bf16[1,26,96]{2,0,1:T(2,128)(2,1)S(1)}, bf16[1,26,96]{2,0,1:T(2,128)(2,1)S(1)}, u32[]{:S(2)}, u32[]{:S(2)}) collective-permute-start(bf16[1,26,96]{2,0,1:T(2,128)(2,1)S(1)} %get-tuple-element.83), channel_id=1, source_target_pairs={{0,192},{8,200},{16,208},{24,216},{32,224},{40,232},{48,240},{56,2... | collective-permute-start | bytes 14984 | tf_op jit(solution)/shard_map/ppermute | solution.py:587
  20.5 1.1 collective-permute-start.2
  21.6 1.7 %collective-permute-done.3 = bf16[1,26,96]{2,0,1:T(2,128)(2,1)S(1)} collective-permute-done((bf16[1,26,96]{2,0,1:T(2,128)(2,1)S(1)}, bf16[1,26,96]{2,0,1:T(2,128)(2,1)S(1)}, u32[]{:S(2)}, u32[]{:S(2)}) %collective-permute-start.3) | collective-permute-done | bytes 5024 | tf_op jit(solution)/shard_map/ppermute | solution.py:587
  23.3 7.2 %collective-permute-done.2 = bf16[1,26,96]{2,0,1:T(2,128)(2,1)S(1)} collective-permute-done((bf16[1,26,96]{2,0,1:T(2,128)(2,1)S(1)}, bf16[1,26,96]{2,0,1:T(2,128)(2,1)S(1)}, u32[]{:S(2)}, u32[]{:S(2)}) %collective-permute-start.2) | collective-permute-done | bytes 5024 | tf_op jit(solution)/shard_map/ppermute | solution.py:587
  33.0 5.6 %collective-permute-done.4 = bf16[26,5,96]{2,1,0:T(8,128)(2,1)S(1)} collective-permute-done((bf16[26,5,96]{2,1,0:T(8,128)(2,1)S(1)}, bf16[26,5,96]{2,1,0:T(8,128)(2,1)S(1)}, u32[]{:S(2)}, u32[]{:S(2)}) %collective-permute-start.4) | collective-permute-done | bytes 24992 | tf_op jit(solution)/shard_map/ppermute | solution.py:587
  38.6 2.6 %collective-permute-start.7 = (bf16[5,36,96]{2,1,0:T(8,128)(2,1)S(1)}, bf16[5,36,96]{2,1,0:T(8,128)(2,1)S(1)}, u32[]{:S(2)}, u32[]{:S(2)}) collective-permute-start(bf16[5,36,96]{2,1,0:T(8,128)(2,1)S(1)} %get-tuple-element.72), channel_id=1, source_target_pairs={{0,192},{8,200},{16,208},{24,216},{32,224},{40,232},{48,240},{56,2... | collective-permute-start | bytes 103688 | tf_op jit(solution)/shard_map/ppermute | solution.py:587
  41.3 3.4 %collective-permute-start.6 = (bf16[5,36,96]{2,1,0:T(8,128)(2,1)S(1)}, bf16[5,36,96]{2,1,0:T(8,128)(2,1)S(1)}, u32[]{:S(2)}, u32[]{:S(2)}) collective-permute-start(bf16[5,36,96]{2,1,0:T(8,128)(2,1)S(1)} %get-tuple-element.71), channel_id=1, source_target_pairs={{0,64},{8,72},{16,80},{24,88},{32,96},{40,104},{48,112},{56,120},{... | collective-permute-start | bytes 103688 | tf_op jit(solution)/shard_map/ppermute | solution.py:587
  46.2 1.3 collective-permute-done.7
  47.5 4.2 %collective-permute-done.6 = bf16[5,36,96]{2,1,0:T(8,128)(2,1)S(1)} collective-permute-done((bf16[5,36,96]{2,1,0:T(8,128)(2,1)S(1)}, bf16[5,36,96]{2,1,0:T(8,128)(2,1)S(1)}, u32[]{:S(2)}, u32[]{:S(2)}) %collective-permute-start.6) | collective-permute-done | bytes 34592 | tf_op jit(solution)/shard_map/ppermute | solution.py:587
  51.9 11.3 %shard_map.255 = (bf16[960,1152]{1,0:T(8,128)(2,1)S(1)}, f32[2,30,32,128]{3,2,1,0:T(8,128)S(1)}, f32[576,256]{1,0:T(8,128)S(1)}, f32[576,128]{1,0:T(8,128)S(1)},...) custom-call(s32[32]{0:T(128)S(1)} %copy-done, ...), custom_call_target="tpu_custom_call" | custom-call | flops 10000000000 | bytes 8000000 | tf_op jit(solution)/shard_map/pallas_call | solution.py:457
  63.2 1.4 copy-done.6
  64.6 1.4 copy-done.8
  70.2 5.7 %all-to-all-start = ((bf16[8,144,384]{2,1,0:T(8,128)(2,1)}), bf16[8,144,384]{2,1,0:T(8,128)(2,1)S(1)}, u32[]{:S(2)}, u32[]{:S(2)}) async-start(bf16[8,144,384]{2,1,0:T(8,128)(2,1)} %get-tuple-element.45), calls=%async_computation | async-start | bytes 1769472 | tf_op jit(solution)/shard_map/all_to_all | solution.py:618
  76.9 1.6 copy.75
  78.5 1.1 reshape.89.target_ref
  79.6 5.8 %all-to-all-done.every_ref = bf16[8,144,384]{2,1,0:T(8,128)(2,1)S(1)} async-done(((bf16[8,144,384]{2,1,0:T(8,128)(2,1)}), bf16[8,144,384]{2,1,0:T(8,128)(2,1)S(1)}, u32[]{:S(2)}, u32[]{:S(2)}) %all-to-all-start) | async-done | bytes 884768 | tf_op jit(solution)/shard_map/all_to_all | solution.py:618
  85.4 1.7 copy-done.7
  87.0 1.3 copy-done.11
  91.2 6.5 %shard_map.256 = (bf16[8,32,16,128]{3,2,1,0:T(8,128)(2,1)}, bf16[256,256]{1,0:T(8,128)(2,1)S(1)}, f32[576,256]{1,0:T(8,128)S(1)}, f32[576,256]{1,0:T(8,128)S(1)}, f32[8,256]{1,0:T(8,128)S(1)}) custom-call(bf16[8,144,384]{2,1,0:T(8,128)(2,1)S(1)} %all-to-all-done.every_ref, f32[144,384]{1,0:T(8,128)S(1)} %copy-done.23, ...), custom_call_target="tpu_custom_call" | custom-call | flops 12000000000 | bytes 8000000 | tf_op jit(solution)/shard_map/pallas_call | solution.py:457
  100.0 4.6 %all-to-all-start.1 = ((bf16[8,32,16,128]{3,2,1,0:T(8,128)(2,1)}), bf16[8,32,16,128]{3,2,1,0:T(8,128)(2,1)S(1)}, u32[]{:S(2)}, u32[]{:S(2)}) async-start(bf16[8,32,16,128]{3,2,1,0:T(8,128)(2,1)} %get-tuple-element.52), calls=%async_computation.1 | async-start | bytes 2097152 | tf_op jit(solution)/shard_map/all_to_all | solution.py:618
  104.6 1.6 copy-done.9
  106.3 1.2 copy-done.13
  107.5 1.1 copy-done.15
  108.5 1.1 copy-done.17
  112.0 10.1 %shard_map.257 = bf16[256,1280]{1,0:T(8,128)(2,1)S(1)} custom-call(f32[576,256]{1,0:T(8,128)S(1)} %copy-done.17, f32[576,256]{1,0:T(8,128)S(1)} %get-tuple-element.54.normed_ref, f32[576,128]{1,0:T(8,128)S(1)} %get-tuple-element.55.inverse_ref, f32[10,256]{1,0:T(8,128)S(1)} %reshape.92.vectors_ref, f32[576,256]{1,0:T(8,128)S(1)} %copy-done.15, ...), custom_call_target="tpu_custom_call" | custom-call | flops 12000000000 | bytes 8000000 | tf_op jit(solution)/shard_map/pallas_call | solution.py:457
  122.2 13.8 %all_to_all.25.late_ref = bf16[8,32,1280]{2,1,0:T(8,128)(2,1)S(1)} all-to-all(bf16[8,32,1280]{2,1,0:T(8,128)(2,1)S(1)} %bitcast.36), channel_id=1, replica_groups=mesh['space'=32,'ens'=8] {'ens'}, dimensions={0} | all-to-all | bytes 1310720 | tf_op jit(solution)/shard_map/all_to_all | solution.py:618
  136.4 19.0 %all_to_all.26.share_ref = bf16[32,32,128]{2,1,0:T(8,128)(2,1)S(1)} all-to-all(bf16[32,32,128]{2,1,0:T(8,128)(2,1)S(1)} %shard_map.258), channel_id=1, replica_groups=mesh['space'=32,'ens'=8] {'space'}, dimensions={0} | all-to-all | bytes 524288 | tf_op jit(solution)/shard_map/all_to_all | solution.py:618
  156.1 4.4 %all-to-all-start.4 = ((f32[8,32,128]{2,1,0:T(8,128)}), f32[8,32,128]{2,1,0:T(8,128)S(1)}, u32[]{:S(2)}, u32[]{:S(2)}) async-start(f32[8,32,128]{2,1,0:T(8,128)} %shard_map.259), calls=%async_computation.4 | async-start | bytes 262144 | tf_op jit(solution)/shard_map/all_to_all | solution.py:618
  161.4 4.6 %all-to-all-done.4.whole_ref = f32[8,32,128]{2,1,0:T(8,128)S(1)} async-done(((f32[8,32,128]{2,1,0:T(8,128)}), f32[8,32,128]{2,1,0:T(8,128)S(1)}, u32[]{:S(2)}, u32[]{:S(2)}) %all-to-all-start.4) | async-done | bytes 131104 | tf_op jit(solution)/shard_map/all_to_all | solution.py:618
  (122 shorter events, 22.1 us)
Async XLA Ops:
  3.9 40.8 %copy-start.37 = (bf16[96]{0:T(256)(128)(2,1)S(1)}, bf16[96]{0:T(256)(128)(2,1)}, u32[]{:S(2)}) copy-start(bf16[96]{0:T(256)(128)(2,1)} %param.31) | copy-start | bytes 580
  3.9 40.8 %copy-start.32 = (bf16[256]{0:T(256)(128)(2,1)S(1)}, bf16[256]{0:T(256)(128)(2,1)}, u32[]{:S(2)}) copy-start(bf16[256]{0:T(256)(128)(2,1)} %param.21) | copy-start | bytes 1540
  3.9 41.0 %copy-start.33 = (bf16[256]{0:T(256)(128)(2,1)S(1)}, bf16[256]{0:T(256)(128)(2,1)}, u32[]{:S(2)}) copy-start(bf16[256]{0:T(256)(128)(2,1)} %param.23) | copy-start | bytes 1540
  3.9 41.3 %copy-start.34 = (bf16[256]{0:T(256)(128)(2,1)S(1)}, bf16[256]{0:T(256)(128)(2,1)}, u32[]{:S(2)}) copy-start(bf16[256]{0:T(256)(128)(2,1)} %param.24) | copy-start | bytes 1540
  3.9 41.5 %copy-start.35 = (bf16[256]{0:T(256)(128)(2,1)S(1)}, bf16[256]{0:T(256)(128)(2,1)}, u32[]{:S(2)}) copy-start(bf16[256]{0:T(256)(128)(2,1)} %param.25) | copy-start | bytes 1540
  3.9 41.7 %copy-start.36 = (bf16[256]{0:T(256)(128)(2,1)S(1)}, bf16[256]{0:T(256)(128)(2,1)}, u32[]{:S(2)}) copy-start(bf16[256]{0:T(256)(128)(2,1)} %param.29) | copy-start | bytes 1540
  3.9 42.1 %copy-start.31 = (bf16[1024]{0:T(1024)(128)(2,1)S(1)}, bf16[1024]{0:T(1024)(128)(2,1)}, u32[]{:S(2)}) copy-start(bf16[1024]{0:T(1024)(128)(2,1)} %param.27) | copy-start | bytes 6148
  6.1 9.3 %collective-permute-start = (bf16[24,1,96]{2,0,1:T(8,128)(2,1)S(1)}, bf16[24,1,96]{2,0,1:T(8,128)(2,1)S(1)}, u32[]{:S(2)}, u32[]{:S(2)}) collective-permute-start(bf16[24,1,96]{2,0,1:T(8,128)(2,1)S(1)} %slice_select_fusion.2), channel_id=1, source_target_pairs={{0,8},{8,16},{16,24},{24,32},{32,40},{40,48},{48,56},{56,64},{64,7... | collective-permute-start | bytes 13832 | tf_op jit(solution)/shard_map/ppermute | solution.py:587
  6.2 9.3 %collective-permute-start.1 = (bf16[24,1,96]{2,0,1:T(8,128)(2,1)S(1)}, bf16[24,1,96]{2,0,1:T(8,128)(2,1)S(1)}, u32[]{:S(2)}, u32[]{:S(2)}) collective-permute-start(bf16[24,1,96]{2,0,1:T(8,128)(2,1)S(1)} %get-tuple-element.84), channel_id=1, source_target_pairs={{0,248},{8,0},{16,8},{24,16},{32,24},{40,32},{48,40},{56,48},{64,5... | collective-permute-start | bytes 13832 | tf_op jit(solution)/shard_map/ppermute | solution.py:587
  15.4 36.4 %copy-start = (s32[32]{0:T(128)S(1)}, s32[32]{0:T(128)}, u32[]{:S(2)}) copy-start(s32[32]{0:T(128)} %seam_turns_ref.1) | copy-start | bytes 388
  15.4 36.4 %copy-start.1 = (bf16[256,1024]{1,0:T(8,128)(2,1)S(1)}, bf16[256,1024]{1,0:T(8,128)(2,1)}, u32[]{:S(2)}) copy-start(bf16[256,1024]{1,0:T(8,128)(2,1)} %w_up_ref.3) | copy-start | bytes 1572868
  15.4 36.4 %copy-start.2 = (bf16[1024,256]{1,0:T(8,128)(2,1)S(1)}, bf16[1024,256]{1,0:T(8,128)(2,1)}, u32[]{:S(2)}) copy-start(bf16[1024,256]{1,0:T(8,128)(2,1)} %w_down_ref.3) | copy-start | bytes 1572868
  15.5 36.4 %copy-start.3 = (bf16[864,256]{1,0:T(8,128)(2,1)S(1)}, bf16[864,256]{1,0:T(8,128)(2,1)}, u32[]{:S(2)}) copy-start(bf16[864,256]{1,0:T(8,128)(2,1)} %w_in_ref.1) | copy-start | bytes 1327108
  15.5 36.4 %copy-start.4 = (bf16[256,96]{0,1:T(8,128)(2,1)S(1)}, bf16[256,96]{0,1:T(8,128)(2,1)}, u32[]{:S(2)}) copy-start(bf16[256,96]{0,1:T(8,128)(2,1)} %param.30) | copy-start | bytes 147460
  15.5 36.4 %copy-start.5 = (bf16[49,256]{1,0:T(8,128)(2,1)S(1)}, bf16[49,256]{1,0:T(8,128)(2,1)}, u32[]{:S(2)}) copy-start(bf16[49,256]{1,0:T(8,128)(2,1)} %w_depth_low_ref.1) | copy-start | bytes 75268
  15.6 7.7 %collective-permute-start.3 = (bf16[1,26,96]{2,0,1:T(2,128)(2,1)S(1)}, bf16[1,26,96]{2,0,1:T(2,128)(2,1)S(1)}, u32[]{:S(2)}, u32[]{:S(2)}) collective-permute-start(bf16[1,26,96]{2,0,1:T(2,128)(2,1)S(1)} %get-tuple-element.83), channel_id=1, source_target_pairs={{0,192},{8,200},{16,208},{24,216},{32,224},{40,232},{48,240},{56,2... | collective-permute-start | bytes 14984 | tf_op jit(solution)/shard_map/ppermute | solution.py:587
  20.5 10.0 %collective-permute-start.2 = (bf16[1,26,96]{2,0,1:T(2,128)(2,1)S(1)}, bf16[1,26,96]{2,0,1:T(2,128)(2,1)S(1)}, u32[]{:S(2)}, u32[]{:S(2)}) collective-permute-start(bf16[1,26,96]{2,0,1:T(2,128)(2,1)S(1)} %get-tuple-element.82), channel_id=1, source_target_pairs={{0,64},{8,72},{16,80},{24,88},{32,96},{40,104},{48,112},{56,120},{... | collective-permute-start | bytes 14984 | tf_op jit(solution)/shard_map/ppermute | solution.py:587
  31.1 1.9 %collective-permute-start.5 = (bf16[26,5,96]{2,1,0:T(8,128)(2,1)S(1)}, bf16[26,5,96]{2,1,0:T(8,128)(2,1)S(1)}, u32[]{:S(2)}, u32[]{:S(2)}) collective-permute-start(bf16[26,5,96]{2,1,0:T(8,128)(2,1)S(1)} %get-tuple-element.77), channel_id=1, source_target_pairs={{0,248},{8,0},{16,8},{24,16},{32,24},{40,32},{48,40},{56,48},{64,5... | collective-permute-start | bytes 74888 | tf_op jit(solution)/shard_map/ppermute | solution.py:587
  31.3 7.3 %collective-permute-start.4 = (bf16[26,5,96]{2,1,0:T(8,128)(2,1)S(1)}, bf16[26,5,96]{2,1,0:T(8,128)(2,1)S(1)}, u32[]{:S(2)}, u32[]{:S(2)}) collective-permute-start(bf16[26,5,96]{2,1,0:T(8,128)(2,1)S(1)} %fusion.5), channel_id=1, source_target_pairs={{0,8},{8,16},{16,24},{24,32},{32,40},{40,48},{48,56},{56,64},{64,7... | collective-permute-start | bytes 74888 | tf_op jit(solution)/shard_map/ppermute | solution.py:587
  38.6 8.8 %collective-permute-start.7 = (bf16[5,36,96]{2,1,0:T(8,128)(2,1)S(1)}, bf16[5,36,96]{2,1,0:T(8,128)(2,1)S(1)}, u32[]{:S(2)}, u32[]{:S(2)}) collective-permute-start(bf16[5,36,96]{2,1,0:T(8,128)(2,1)S(1)} %get-tuple-element.72), channel_id=1, source_target_pairs={{0,192},{8,200},{16,208},{24,216},{32,224},{40,232},{48,240},{56,2... | collective-permute-start | bytes 103688 | tf_op jit(solution)/shard_map/ppermute | solution.py:587
  41.3 10.4 %collective-permute-start.6 = (bf16[5,36,96]{2,1,0:T(8,128)(2,1)S(1)}, bf16[5,36,96]{2,1,0:T(8,128)(2,1)S(1)}, u32[]{:S(2)}, u32[]{:S(2)}) collective-permute-start(bf16[5,36,96]{2,1,0:T(8,128)(2,1)S(1)} %get-tuple-element.71), channel_id=1, source_target_pairs={{0,64},{8,72},{16,80},{24,88},{32,96},{40,104},{48,112},{56,120},{... | collective-permute-start | bytes 103688 | tf_op jit(solution)/shard_map/ppermute | solution.py:587
  51.9 24.1 %copy-start.30 = (bf16[24,2304]{1,0:T(8,128)(2,1)S(1)}, bf16[24,2304]{1,0:T(8,128)(2,1)}, u32[]{:S(2)}) copy-start(bf16[24,2304]{1,0:T(8,128)(2,1)} %param.18) | copy-start | bytes 331780
  63.2 1.4 copy-start.6
  64.6 1.4 copy-start.8
  70.2 5.8 %copy-start.26 = (f32[49,256]{1,0:T(8,128)}, f32[49,256]{1,0:T(8,128)S(1)}, u32[]{:S(2)}) copy-start(f32[49,256]{1,0:T(8,128)S(1)} %get-tuple-element.58.w_depth_ref) | copy-start | bytes 150532
  70.2 15.2 %all-to-all-start = ((bf16[8,144,384]{2,1,0:T(8,128)(2,1)}), bf16[8,144,384]{2,1,0:T(8,128)(2,1)S(1)}, u32[]{:S(2)}, u32[]{:S(2)}) async-start(bf16[8,144,384]{2,1,0:T(8,128)(2,1)} %get-tuple-element.45), calls=%async_computation | async-start | bytes 1769472 | tf_op jit(solution)/shard_map/all_to_all | solution.py:618
  85.4 1.7 copy-start.7
  87.0 1.3 copy-start.11
  100.0 4.6 %copy-start.28 = (f32[8,256]{1,0:T(8,128)}, f32[8,256]{1,0:T(8,128)S(1)}, u32[]{:S(2)}) copy-start(f32[8,256]{1,0:T(8,128)S(1)} %get-tuple-element.60.early_small_ref) | copy-start | bytes 24580
  100.0 22.1 %all-to-all-start.1 = ((bf16[8,32,16,128]{3,2,1,0:T(8,128)(2,1)}), bf16[8,32,16,128]{3,2,1,0:T(8,128)(2,1)S(1)}, u32[]{:S(2)}, u32[]{:S(2)}) async-start(bf16[8,32,16,128]{3,2,1,0:T(8,128)(2,1)} %get-tuple-element.52), calls=%async_computation.1 | async-start | bytes 2097152 | tf_op jit(solution)/shard_map/all_to_all | solution.py:618
  104.6 1.6 copy-start.9
  156.1 9.9 %all-to-all-start.4 = ((f32[8,32,128]{2,1,0:T(8,128)}), f32[8,32,128]{2,1,0:T(8,128)S(1)}, u32[]{:S(2)}, u32[]{:S(2)}) async-start(f32[8,32,128]{2,1,0:T(8,128)} %shard_map.259), calls=%async_computation.4 | async-start | bytes 262144 | tf_op jit(solution)/shard_map/all_to_all | solution.py:618
  (17 other events, 15.0 us)

commit v2 on v1

--- a/solution.py
+++ b/solution.py
@@ -18,7 +18,8 @@
 CELLS = SIDE * SIDE
 LANE = 128
 SMALL = 64
-VMEM_BYTES = 24 * 1024 * 1024
+VMEM_BYTES = 56 * 1024 * 1024
+SMALL_VMEM_BYTES = 16 * 1024 * 1024
 
 
 def dot(left, right, left_dim=1, right_dim=0):
@@ -76,22 +77,37 @@
     w_up_ref,
     w_down_ref,
     head_ref,
-    patches_ref,
-    stem_ref,
+    patches_out,
+    stem_out,
     normed_ref,
     inverse_ref,
     scaled_ref,
-    slope_ref,
-    active_ref,
+    slope_out,
+    active_out,
     hidden_ref,
     field_ref,
     tight_ref,
     sent_ref,
     w_depth_ref,
+    patches_ref,
+    stem_ref,
+    slope_ref,
+    active_ref,
     wide_ref,
     stage_ref,
     w_in_wide_ref,
+    whole_sem,
+    part_sem,
 ):
+    def send_part(part, row):
+        at = pl.ds(row, 96)
+        return (
+            pltpu.make_async_copy(slope_ref.at[at], slope_out.at[at], part_sem.at[0, part]),
+            pltpu.make_async_copy(active_ref.at[at], active_out.at[at], part_sem.at[1, part]),
+        )
+
+    send_patches = pltpu.make_async_copy(patches_ref, patches_out, whole_sem.at[0])
+    send_stem = pltpu.make_async_copy(stem_ref, stem_out, whole_sem.at[1])
     tile = lax.axis_index("space")
     tiles = seam_turns_ref.shape[0]
     across = tiles // 4
@@ -117,6 +133,7 @@
     wide_ref[...] = jnp.zeros_like(wide_ref)
     wide_ref[:, 0:36, 0:96] = source_ref[...].astype(F32)
     gather_patches(turns, wide_ref, stage_ref, patches_ref)
+    send_patches.start()
     for part in range(5):
         rows = slice(part * 192, (part + 1) * 192)
         stem = dot(patches_ref[rows, :], w_in_wide_ref[...]) + b_in
@@ -125,6 +142,8 @@
             stem_ref[half, part * 6 : (part + 1) * 6] = stem[
                 :, half * LANE : (half + 1) * LANE
             ].reshape(6, 32, LANE)
+
+    send_stem.start()
 
     def normalise(block, carry):
         row = block * 4
@@ -159,16 +178,20 @@
     lax.fori_loop(0, 6, normalise, 0)
 
     def mix(part, carry):
-        at = pl.ds(pl.multiple_of(part * 96, 96), 96)
+        row = pl.multiple_of(part * 96, 96)
+        at = pl.ds(row, 96)
         upward = dot(scaled_ref[at, :], w_up_ref[...]) + b_up
         square = upward * upward
         tanh_part = jnp.tanh(ROOT * (upward + CUBIC * square * upward))
         plus = 0.5 * (1.0 + tanh_part)
-        slope_ref[at, :] = plus + 0.5 * upward * (1.0 - tanh_part * tanh_part) * (
+        slope = plus + 0.5 * upward * (1.0 - tanh_part * tanh_part) * (
             ROOT + (3.0 * CUBIC * ROOT) * square
         )
+        slope_ref[at, :] = slope.astype(BF16)
         active = (upward * plus).astype(BF16)
         active_ref[at, :] = active
+        for send in send_part(part, row):
+            send.start()
         own = [
             stem_ref[half, pl.ds(3 + 4 * part, 4), 3 : 3 + SIDE, :].reshape(96, LANE)
             for half in range(2)
@@ -187,6 +210,11 @@
     sent = tight_ref[...].astype(BF16)
     for member in range(sent_ref.shape[0]):
         sent_ref[member] = sent
+    send_patches.wait()
+    send_stem.wait()
+    for part in range(6):
+        for send in send_part(part, 96 * part):
+            send.wait()
 
 
 def mixer_backward_kernel(
@@ -197,15 +225,15 @@
     hidden_ref,
     head_ref,
     pick_ref,
-    active_ref,
-    slope_ref,
+    active_in,
+    slope_in,
     scaled_ref,
-    w_down_ref,
-    w_up_ref,
+    w_down_in,
+    w_up_in,
     early_ref,
     out_part_ref,
-    hidden_grad_ref,
-    scaled_grad_ref,
+    hidden_grad_out,
+    scaled_grad_out,
     small_ref,
     tight_ref,
     field_ref,
@@ -213,7 +241,23 @@
     up_low_ref,
     up_sum_ref,
     down_ref,
+    active_ref,
+    slope_ref,
+    w_down_ref,
+    w_up_ref,
+    hidden_grad_ref,
+    scaled_grad_ref,
+    in_sem,
+    out_sem,
 ):
+    fetch_active = pltpu.make_async_copy(active_in, active_ref, in_sem.at[0])
+    fetch_slope = pltpu.make_async_copy(slope_in, slope_ref, in_sem.at[1])
+    fetch_down = pltpu.make_async_copy(w_down_in, w_down_ref, in_sem.at[2])
+    fetch_up = pltpu.make_async_copy(w_up_in, w_up_ref, in_sem.at[3])
+    for fetch in (fetch_active, fetch_down, fetch_slope, fetch_up):
+        fetch.start()
+    send_hidden = pltpu.make_async_copy(hidden_grad_ref, hidden_grad_out, out_sem.at[0])
+    send_scaled = pltpu.make_async_copy(scaled_grad_ref, scaled_grad_out, out_sem.at[1])
     members = every_ref.shape[0]
     own = own_ref[...]
     own_sent = own.astype(BF16).astype(F32)
@@ -233,17 +277,22 @@
     grad_b_out = jnp.sum(grad_f, axis=0, keepdims=True)
     grad_f_low = grad_f.astype(BF16)
     picked = dot(grad_f_low, pick_ref[...]).astype(BF16)
-    out_part_ref[...] = dot(picked, hidden_ref[...], 0, 0).astype(BF16)
+    out_part_ref[...] = dot(picked, hidden_ref[...], 0, 0)
     grad_hidden = dot(grad_f_low[:, 0:96], head_ref[...])
     hidden_grad_ref[...] = grad_hidden
+    send_hidden.start()
     low_ref[...] = grad_hidden.astype(BF16)
     grad_b_down = jnp.sum(grad_hidden, axis=0, keepdims=True)
+    fetch_active.wait()
     down_ref[...] = dot(low_ref[...], active_ref[...], 0, 0)
     up_sum_ref[...] = jnp.zeros_like(up_sum_ref)
+    fetch_down.wait()
+    fetch_slope.wait()
+    fetch_up.wait()
 
     def widen(part, carry):
         at = pl.ds(pl.multiple_of(part * 96, 96), 96)
-        grad_up = dot(low_ref[at, :], w_down_ref[...], 1, 1) * slope_ref[at, :]
+        grad_up = dot(low_ref[at, :], w_down_ref[...], 1, 1) * slope_ref[at, :].astype(F32)
         up_sum_ref[...] += jnp.sum(grad_up.reshape(12, 8, 1024), axis=0)
         up_low = grad_up.astype(BF16)
         up_low_ref[at, :] = up_low
@@ -251,6 +300,7 @@
         return carry
 
     lax.fori_loop(0, 6, widen, 0)
+    send_scaled.start()
     for chunk in range(4):
         up = dot(up_low_ref[:, chunk * 256 : (chunk + 1) * 256], scaled_ref[...], 0, 0)
         up = up.reshape(8, 4, 8, 256)
@@ -288,6 +338,8 @@
     small_ref[0:1, :] = grad_b_down
     small_ref[1:5, :] = two_part(spread, fold)[0:4]
     small_ref[5:6, :] = two_part(b_out, place)[0:1]
+    send_hidden.wait()
+    send_scaled.wait()
 
 
 def depth_backward_kernel(
@@ -295,10 +347,10 @@
     normed_ref,
     inverse_ref,
     vectors_ref,
-    hidden_grad_ref,
-    stem_ref,
+    hidden_grad_in,
+    stem_in,
     w_depth_ref,
-    patches_ref,
+    patches_in,
     order_ref,
     early_small_ref,
     out_part_ref,
@@ -309,7 +361,16 @@
     sums_ref,
     low_ref,
     tight_ref,
+    hidden_grad_ref,
+    stem_ref,
+    patches_ref,
+    in_sem,
 ):
+    fetch_stem = pltpu.make_async_copy(stem_in, stem_ref, in_sem.at[0])
+    fetch_hidden = pltpu.make_async_copy(hidden_grad_in, hidden_grad_ref, in_sem.at[1])
+    fetch_patches = pltpu.make_async_copy(patches_in, patches_ref, in_sem.at[2])
+    for fetch in (fetch_stem, fetch_hidden, fetch_patches):
+        fetch.start()
     deep_ref[...] = jnp.zeros_like(deep_ref)
     small_ref[...] = jnp.zeros_like(small_ref)
     sums_ref[...] = jnp.zeros_like(sums_ref)
@@ -340,6 +401,8 @@
         return carry
 
     lax.fori_loop(0, 6, unnormalise, 0)
+    fetch_stem.wait()
+    fetch_hidden.wait()
     for half in range(2):
         lanes = slice(half * LANE, (half + 1) * LANE)
 
@@ -387,19 +450,23 @@
     small_ref[50:51, :] = jnp.sum(sums_ref[0], axis=0, keepdims=True)
     small_ref[51:52, :] = jnp.sum(sums_ref[1], axis=0, keepdims=True)
     small_ref[53:59, :] = early_small_ref[0:6, :]
+    fetch_patches.wait()
     order = order_ref[...]
     ordered = dot(low_ref[...], order).astype(BF16)
     wide = dot(ordered, patches_ref[...], 0, 0)
     tight_ref[...] = jnp.zeros_like(tight_ref)
     for offset in range(9):
         tight_ref[:, 96 * offset : 96 * (offset + 1)] = wide[:, LANE * offset : LANE * offset + 96]
-    late_ref[:, 0:896] = tight_ref[...].astype(BF16)
+    for part in range(8):
+        rows = slice(32 * part, 32 * (part + 1))
+        for row, at in enumerate((864, 1024, 1056)):
+            tight_ref[rows, at : at + 32] = out_part_ref[32 * row : 32 * (row + 1), rows]
     small = small_ref[...]
     high = small.astype(BF16)
     rest = (small - high.astype(F32)).astype(BF16)
     both = jnp.concatenate([high, rest], axis=0)
-    late_ref[:, 896:1024] = dot(order, both, 0, 1).astype(BF16)
-    late_ref[:, 1024:1280] = out_part_ref[...]
+    tight_ref[:, 896:1024] = dot(order, both, 0, 1)
+    late_ref[...] = tight_ref[...].astype(BF16)
 
 
 def combine_kernel(early_ref, late_ref, share_ref, rows_ref):
@@ -410,12 +477,11 @@
         early = early + early_ref[member].astype(F32)
         late = late + late_ref[member].astype(F32)
     rows_ref[:, 0:16, :] = early
-    rows_ref[:, 26:32, :] = jnp.zeros_like(rows_ref[:, 26:32, :])
-    for row in range(10):
-        piece = late[:, row * LANE : (row + 1) * LANE]
-        if row == 7:
-            piece = piece + jnp.concatenate([piece[:, SMALL:], jnp.zeros_like(piece[:, SMALL:])], axis=1)
-        rows_ref[:, 16 + row : 17 + row, :] = piece[:, None, :]
+    for row in range(7):
+        rows_ref[:, 16 + row : 17 + row, :] = late[:, row * LANE : (row + 1) * LANE][:, None, :]
+    small = late[:, 896 : 896 + SMALL] + late[:, 960 : 960 + SMALL]
+    last = jnp.concatenate([small, late[:, 1024:1088]], axis=1)
+    rows_ref[:, 23:24, :] = last[:, None, :]
     share_ref[...] = rows_ref[...].astype(BF16)
 
 
@@ -441,26 +507,25 @@
             part, 8:16, :
         ]
         w_depth_ref[part : part + 1, :] = whole_ref[part, 23:24, 0:49]
+        lanes = slice(32 * part, 32 * (part + 1))
+        w_out_ref[0:1, lanes] = whole_ref[part, 22:23, 96:128]
+        w_out_ref[1:2, lanes] = whole_ref[part, 23:24, 64:96]
+        w_out_ref[2:3, lanes] = whole_ref[part, 23:24, 96:128]
         b_up_ref[0:1, 4 * part : 4 * part + 4] = whole_ref[part, 23:24, 54:58]
-    for part in range(3):
-        for half in range(2):
-            w_out_ref[part : part + 1, half * LANE : (half + 1) * LANE] = whole_ref[
-                part, 24 + half : 25 + half, :
-            ]
     small = jnp.concatenate([whole_ref[part, 23:24, :] for part in range(parts)], axis=0)
     small_ref[...] = small.T[48:64, :]
 
 
-def call(kernel, shapes, scratch, *operands, smem=0, flops=0):
-    space = [pl.BlockSpec(memory_space=pltpu.SMEM)] * smem
-    space += [pl.BlockSpec(memory_space=pltpu.VMEM)] * (len(operands) - smem)
+def call(kernel, outs, scratch, *operands, spaces=None, vmem=VMEM_BYTES, flops=0):
+    kinds = {"v": pltpu.VMEM, "s": pltpu.SMEM, "a": pl.ANY}
+    spaces = spaces or "v" * len(operands)
     return pl.pallas_call(
         kernel,
-        out_shape=[jax.ShapeDtypeStruct(s, d) for s, d in shapes],
-        in_specs=space,
-        out_specs=[pl.BlockSpec(memory_space=pltpu.VMEM)] * len(shapes),
-        scratch_shapes=[pltpu.VMEM(s, d) for s, d in scratch],
-        compiler_params=pltpu.CompilerParams(vmem_limit_bytes=VMEM_BYTES),
+        out_shape=[jax.ShapeDtypeStruct(shape, kind) for shape, kind, _ in outs],
+        in_specs=[pl.BlockSpec(memory_space=kinds[letter]) for letter in spaces],
+        out_specs=[pl.BlockSpec(memory_space=kinds[letter]) for _, _, letter in outs],
+        scratch_shapes=[x if not isinstance(x, tuple) else pltpu.VMEM(*x) for x in scratch],
+        compiler_params=pltpu.CompilerParams(vmem_limit_bytes=vmem),
         cost_estimate=pl.CostEstimate(flops=flops, bytes_accessed=8_000_000, transcendentals=0),
     )(*operands)
 
@@ -474,20 +539,30 @@
     return call(
         forward_kernel,
         [
+            ((960, 1152), BF16, "a"),
+            ((2, 30, 32, LANE), F32, "a"),
+            ((CELLS, 256), F32, "v"),
+            ((CELLS, LANE), F32, "v"),
+            ((CELLS, 256), BF16, "v"),
+            ((CELLS, 1024), BF16, "a"),
+            ((CELLS, 1024), BF16, "a"),
+            ((CELLS, 256), BF16, "v"),
+            ((CELLS, 96), F32, "v"),
+            ((144, 384), F32, "v"),
+            ((members, 144, 384), BF16, "v"),
+            ((49, 256), F32, "v"),
+        ],
+        [
             ((960, 1152), BF16),
             ((2, 30, 32, LANE), F32),
-            ((CELLS, 256), F32),
-            ((CELLS, LANE), F32),
-            ((CELLS, 256), BF16),
-            ((CELLS, 1024), F32),
             ((CELLS, 1024), BF16),
-            ((CELLS, 256), BF16),
-            ((CELLS, 96), F32),
-            ((144, 384), F32),
-            ((members, 144, 384), BF16),
-            ((49, 256), F32),
+            ((CELLS, 1024), BF16),
+            ((36, 40, LANE), F32),
+            ((30, 32, LANE), F32),
+            ((1152, 256), BF16),
+            pltpu.SemaphoreType.DMA((2,)),
+            pltpu.SemaphoreType.DMA((2, 6)),
         ],
-        [((36, 40, LANE), F32), ((30, 32, LANE), F32), ((1152, 256), BF16)],
         seam_turns,
         source,
         w_in,
@@ -496,24 +571,24 @@
         w_up,
         w_down,
         head,
-        smem=1,
+        spaces="svvvvvvv",
         flops=10_000_000_000,
     )
 
 
 def run_mixer_backward(every, tight, target, saved, head, w_down, w_up, coefficient):
     hidden, active, slope, scaled = saved
-    column = jnp.arange(256)
+    column = jnp.arange(96)
     owner = 3 * (column % 32) + column // 32
-    pick = ((jnp.arange(LANE)[:, None] == owner[None, :]) & (column[None, :] < 96)).astype(BF16)
+    pick = (jnp.arange(LANE)[:, None] == owner[None, :]).astype(BF16)
     return call(
         functools.partial(mixer_backward_kernel, coefficient),
         [
-            ((8, 32, 16, LANE), BF16),
-            ((256, 256), BF16),
-            ((CELLS, 256), F32),
-            ((CELLS, 256), F32),
-            ((8, 256), F32),
+            ((8, 32, 16, LANE), BF16, "v"),
+            ((96, 256), F32, "v"),
+            ((CELLS, 256), F32, "a"),
+            ((CELLS, 256), F32, "a"),
+            ((8, 256), F32, "v"),
         ],
         [
             ((144, 384), F32),
@@ -522,6 +597,14 @@
             ((CELLS, 1024), BF16),
             ((8, 1024), F32),
             ((256, 1024), F32),
+            ((CELLS, 1024), BF16),
+            ((CELLS, 1024), BF16),
+            ((1024, 256), BF16),
+            ((256, 1024), BF16),
+            ((CELLS, 256), F32),
+            ((CELLS, 256), F32),
+            pltpu.SemaphoreType.DMA((4,)),
+            pltpu.SemaphoreType.DMA((2,)),
         ],
         every,
         tight,
@@ -534,6 +617,7 @@
         scaled,
         w_down,
         w_up,
+        spaces="vvvvvvaavaa",
         flops=12_000_000_000,
     )
 
@@ -545,14 +629,18 @@
     order = (column[:, None] == (8 * (column % 32) + column // 32)[None, :]).astype(BF16)
     return call(
         depth_backward_kernel,
-        [((256, 1280), BF16)],
+        [((256, 1152), BF16, "v")],
         [
             ((2, 36, 40, LANE), F32),
             ((2, 30, 32, LANE), F32),
             ((SMALL, 256), F32),
             ((3, 8, 256), F32),
             ((960, 256), BF16),
-            ((256, 896), F32),
+            ((256, 1152), F32),
+            ((CELLS, 256), F32),
+            ((2, 30, 32, LANE), F32),
+            ((960, 1152), BF16),
+            pltpu.SemaphoreType.DMA((3,)),
         ],
         scaled_grad,
         normed,
@@ -565,21 +653,31 @@
         order,
         early_small,
         out_part,
+        spaces="vvvvaavavvv",
         flops=12_000_000_000,
     )[0]
 
 
 def run_combine(early, late):
-    return call(combine_kernel, [((32, 32, LANE), BF16)], [((32, 32, LANE), F32)], early, late)[0]
+    return call(
+        combine_kernel,
+        [((32, 24, LANE), BF16, "v")],
+        [((32, 24, LANE), F32)],
+        early,
+        late,
+        vmem=SMALL_VMEM_BYTES,
+    )[0]
 
 
 def run_total(share, members):
-    return call(total_kernel, [((members, 32, LANE), F32)], [], share)[0]
+    return call(total_kernel, [((members, 24, LANE), F32, "v")], [], share, vmem=SMALL_VMEM_BYTES)[0]
 
 
 def run_unpack(whole):
     shapes = ((8, 864), (8, 49), (32, 256), (8, 1024), (3, 256), (16, 8), (1, 32))
-    return call(unpack_kernel, [(shape, F32) for shape in shapes], [], whole)
+    return call(
+        unpack_kernel, [(shape, F32, "v") for shape in shapes], [], whole, vmem=SMALL_VMEM_BYTES
+    )
 
 
 def shifted(value, axis, by):
@@ -667,7 +765,7 @@
         scaled_grad, normed, inverse, vectors, hidden_grad, stem, w_depth_wide, patches, early_small, out_part
     )
     early_parts, late = lax.optimization_barrier((swap(early, "ens"), late))
-    late_parts = swap(late.reshape(8, 32, 1280), "ens")
+    late_parts = swap(late.reshape(8, 32, 1152), "ens")
     shares = swap(run_combine(early_parts, late_parts), "space")
     whole = swap(run_total(shares, members), "ens")
     grad_w_in, grad_w_depth, grad_w_up, grad_w_down, grad_w_out, small, grad_b_up = run_unpack(whole)

time: 169 us -> 153 us (0.905)
  local copies, waits for them, and re-layouts: 31.7 us -> 8.25 us
  Pallas kernels: 29.7 us -> 36.2 us
  other arithmetic: 1.52 us -> 3.51 us
    unnamed x84 -> x28, local copies, waits for them, and re-layouts: 23.9 us -> 2.34 us
    pallas_call x6, Pallas kernels: 29.7 us -> 36.2 us  [call(): pl.pallas_call(kernel, out_shape=[jax.ShapeDtypeStruct(shape, kind) for s...]
    reshape x3, local copies, waits for them, and re-layouts: 3.56 us -> 1.06 us  [body(): verifying_analysis.reshape(4, 144, 96).transpose(1, 0, 2).reshape(144, 384)]
  transfers between devices with their start and end apart: 11 -> 11, of which waited for: 9 -> 10; matrix products, arithmetic and copies ran while one was open for 4% -> 4% of each run, Pallas kernels for 6% -> 9%
where the time goes in v2:
time: 153 us; the launch traced here: 152 us
  Pallas kernels  36.2 us (24%)
  starting transfers between devices  35.7 us (23%)
  waiting for transfers between devices  33.3 us (22%)
  blocking collectives  31.8 us (21%)
  local copies, waits for them, and re-layouts  8.25 us (5%)
  between operations  3.55 us (2%)
  other arithmetic  3.51 us (2%)
    pallas_call x6, Pallas kernels, call(): pl.pallas_call(kernel, out_shape=[jax.ShapeDtypeStruct(shape, kind) for s...  36.2 us
    all_to_all x2, blocking collectives, swap(): return lax.all_to_all(value, axis, 0, 0, tiled=True)  31.8 us
    ppermute x8, waiting for transfers between devices, shifted(): lax.ppermute(value, axis, [(i, (i + by) % peers) for i in range(peers)])  21.8 us
    ppermute x8, starting transfers between devices, shifted(): lax.ppermute(value, axis, [(i, (i + by) % peers) for i in range(peers)])  20.8 us
    all_to_all x3, starting transfers between devices, swap(): return lax.all_to_all(value, axis, 0, 0, tiled=True)  15 us
    all_to_all x3, waiting for transfers between devices, swap(): return lax.all_to_all(value, axis, 0, 0, tiled=True)  11.5 us
  transfers between devices with their start and end apart: 11, of which 10 were waited for; matrix products, arithmetic and copies ran while one was open for 4% of the time, Pallas kernels for 9%

profile of v2, /device:TPU:2, one launch (start us, length us, event | category | flops | bytes accessed | tf_op | source)
XLA Modules:
  0.0 152.3 jit_solution(15134735687377498219)
XLA Ops:
  0.7 1.3 fusion.16
  2.7 1.0 fusion.1
  6.1 8.0 %collective-permute-start.1 = (bf16[24,1,96]{2,0,1:T(8,128)(2,1)S(1)}, bf16[24,1,96]{2,0,1:T(8,128)(2,1)S(1)}, u32[]{:S(2)}, u32[]{:S(2)}) collective-permute-start(bf16[24,1,96]{2,0,1:T(8,128)(2,1)S(1)} %get-tuple-element.84), channel_id=1, source_target_pairs={{0,248},{8,0},{16,8},{24,16},{32,24},{40,32},{48,40},{56,48},{64,5... | collective-permute-start | bytes 13832 | tf_op jit(solution)/shard_map/ppermute | solution.py:685
  14.1 1.2 collective-permute-done
  15.5 4.9 %collective-permute-start.3 = (bf16[1,26,96]{2,0,1:T(2,128)(2,1)S(1)}, bf16[1,26,96]{2,0,1:T(2,128)(2,1)S(1)}, u32[]{:S(2)}, u32[]{:S(2)}) collective-permute-start(bf16[1,26,96]{2,0,1:T(2,128)(2,1)S(1)} %get-tuple-element.83), channel_id=1, source_target_pairs={{0,192},{8,200},{16,208},{24,216},{32,224},{40,232},{48,240},{56,2... | collective-permute-start | bytes 14984 | tf_op jit(solution)/shard_map/ppermute | solution.py:685
  20.4 1.2 collective-permute-start.2
  21.5 1.7 %collective-permute-done.3 = bf16[1,26,96]{2,0,1:T(2,128)(2,1)S(1)} collective-permute-done((bf16[1,26,96]{2,0,1:T(2,128)(2,1)S(1)}, bf16[1,26,96]{2,0,1:T(2,128)(2,1)S(1)}, u32[]{:S(2)}, u32[]{:S(2)}) %collective-permute-start.3) | collective-permute-done | bytes 5024 | tf_op jit(solution)/shard_map/ppermute | solution.py:685
  23.2 7.2 %collective-permute-done.2 = bf16[1,26,96]{2,0,1:T(2,128)(2,1)S(1)} collective-permute-done((bf16[1,26,96]{2,0,1:T(2,128)(2,1)S(1)}, bf16[1,26,96]{2,0,1:T(2,128)(2,1)S(1)}, u32[]{:S(2)}, u32[]{:S(2)}) %collective-permute-start.2) | collective-permute-done | bytes 5024 | tf_op jit(solution)/shard_map/ppermute | solution.py:685
  31.9 1.1 collective-permute-done.5
  32.9 5.6 %collective-permute-done.4 = bf16[26,5,96]{2,1,0:T(8,128)(2,1)S(1)} collective-permute-done((bf16[26,5,96]{2,1,0:T(8,128)(2,1)S(1)}, bf16[26,5,96]{2,1,0:T(8,128)(2,1)S(1)}, u32[]{:S(2)}, u32[]{:S(2)}) %collective-permute-start.4) | collective-permute-done | bytes 24992 | tf_op jit(solution)/shard_map/ppermute | solution.py:685
  38.6 2.7 %collective-permute-start.7 = (bf16[5,36,96]{2,1,0:T(8,128)(2,1)S(1)}, bf16[5,36,96]{2,1,0:T(8,128)(2,1)S(1)}, u32[]{:S(2)}, u32[]{:S(2)}) collective-permute-start(bf16[5,36,96]{2,1,0:T(8,128)(2,1)S(1)} %get-tuple-element.72), channel_id=1, source_target_pairs={{0,192},{8,200},{16,208},{24,216},{32,224},{40,232},{48,240},{56,2... | collective-permute-start | bytes 103688 | tf_op jit(solution)/shard_map/ppermute | solution.py:685
  41.3 3.3 %collective-permute-start.6 = (bf16[5,36,96]{2,1,0:T(8,128)(2,1)S(1)}, bf16[5,36,96]{2,1,0:T(8,128)(2,1)S(1)}, u32[]{:S(2)}, u32[]{:S(2)}) collective-permute-start(bf16[5,36,96]{2,1,0:T(8,128)(2,1)S(1)} %get-tuple-element.71), channel_id=1, source_target_pairs={{0,64},{8,72},{16,80},{24,88},{32,96},{40,104},{48,112},{56,120},{... | collective-permute-start | bytes 103688 | tf_op jit(solution)/shard_map/ppermute | solution.py:685
  46.8 0.8 collective-permute-done.7
  47.6 4.1 %collective-permute-done.6 = bf16[5,36,96]{2,1,0:T(8,128)(2,1)S(1)} collective-permute-done((bf16[5,36,96]{2,1,0:T(8,128)(2,1)S(1)}, bf16[5,36,96]{2,1,0:T(8,128)(2,1)S(1)}, u32[]{:S(2)}, u32[]{:S(2)}) %collective-permute-start.6) | collective-permute-done | bytes 34592 | tf_op jit(solution)/shard_map/ppermute | solution.py:685
  51.7 0.9 pad_maximum_fusion.source_ref
  52.6 12.7 %shard_map.255 = (bf16[960,1152]{1,0:T(8,128)(2,1)}, f32[2,30,32,128]{3,2,1,0:T(8,128)}, f32[576,256]{1,0:T(8,128)}, f32[576,128]{1,0:T(8,128)}, bf16[576,256]{1...) custom-call(s32[32]{0:T(128)} %seam_turns_ref.1, ...), custom_call_target="tpu_custom_call" | custom-call | flops 10000000000 | bytes 8000000 | tf_op jit(solution)/shard_map/pallas_call | solution.py:522
  65.3 5.8 %all-to-all-start = ((bf16[8,144,384]{2,1,0:T(8,128)(2,1)}), bf16[8,144,384]{2,1,0:T(8,128)(2,1)S(1)}, u32[]{:S(2)}, u32[]{:S(2)}) async-start(bf16[8,144,384]{2,1,0:T(8,128)(2,1)} %get-tuple-element.45), calls=%async_computation | async-start | bytes 1769472 | tf_op jit(solution)/shard_map/all_to_all | solution.py:716
  71.1 0.6 fusion.2.pick_ref
  71.7 0.7 fusion.order_ref
  72.7 0.8 reshape.102.target_ref
  73.5 7.0 %all-to-all-done.every_ref = bf16[8,144,384]{2,1,0:T(8,128)(2,1)S(1)} async-done(((bf16[8,144,384]{2,1,0:T(8,128)(2,1)}), bf16[8,144,384]{2,1,0:T(8,128)(2,1)S(1)}, u32[]{:S(2)}, u32[]{:S(2)}) %all-to-all-start) | async-done | bytes 884768 | tf_op jit(solution)/shard_map/all_to_all | solution.py:716
  80.5 0.9 copy-done
  81.5 8.8 %shard_map.256 = (bf16[8,32,16,128]{3,2,1,0:T(8,128)(2,1)}, f32[96,256]{1,0:T(8,128)}, f32[576,256]{1,0:T(8,128)}, f32[576,256]{1,0:T(8,128)}, f32[8,256]{1,0:T(8,128)}) custom-call(bf16[8,144,384]{2,1,0:T(8,128)(2,1)} %copy-done, f32[144,384]{1,0:T(8,128)} %get-tuple-element.46.own_ref, bf16[144,384]{1,0:T(8,128)(2,1)} %reshape.102.target_ref, ...), custom_call_target="tpu_custom_call" | custom-call | flops 12000000000 | bytes 8000000 | tf_op jit(solution)/shard_map/pallas_call | solution.py:522
  90.3 4.6 %all-to-all-start.1 = ((bf16[8,32,16,128]{3,2,1,0:T(8,128)(2,1)}), bf16[8,32,16,128]{3,2,1,0:T(8,128)(2,1)S(1)}, u32[]{:S(2)}, u32[]{:S(2)}) async-start(bf16[8,32,16,128]{3,2,1,0:T(8,128)(2,1)} %get-tuple-element.52), calls=%async_computation.1 | async-start | bytes 2097152 | tf_op jit(solution)/shard_map/all_to_all | solution.py:716
  94.9 13.1 %shard_map.257 = bf16[256,1152]{1,0:T(8,128)(2,1)} custom-call(f32[576,256]{1,0:T(8,128)} %get-tuple-element.53.scaled_grad_ref, f32[576,256]{1,0:T(8,128)} %get-tuple-element.54.normed_ref, f32[576,128]{1,0:T(8,128)} %get-tuple-element.55.inverse_ref, f32[10,256]{1,0:T(8,128)} %reshape.105.vectors_ref, f32[576,256]{1,0:T(8,128)} %get-tuple-element.56.hidden_grad_in, ...), custom_call_target="tpu_custom_call" | custom-call | flops 12000000000 | bytes 8000000 | tf_op jit(solution)/shard_map/pallas_call | solution.py:522
  108.0 13.6 %all_to_all.25.late_ref = bf16[8,32,1152]{2,1,0:T(8,128)(2,1)S(1)} all-to-all(bf16[8,32,1152]{2,1,0:T(8,128)(2,1)} %bitcast.38), channel_id=1, replica_groups=mesh['space'=32,'ens'=8] {'ens'}, dimensions={0} | all-to-all | bytes 1179648 | tf_op jit(solution)/shard_map/all_to_all | solution.py:716
  122.0 18.1 %all_to_all.26.share_ref = bf16[32,24,128]{2,1,0:T(8,128)(2,1)S(1)} all-to-all(bf16[32,24,128]{2,1,0:T(8,128)(2,1)S(1)} %shard_map.258), channel_id=1, replica_groups=mesh['space'=32,'ens'=8] {'space'}, dimensions={0} | all-to-all | bytes 393216 | tf_op jit(solution)/shard_map/all_to_all | solution.py:716
  140.1 0.7 shard_map.259
  140.8 4.5 %all-to-all-start.4 = ((f32[8,24,128]{2,1,0:T(8,128)}), f32[8,24,128]{2,1,0:T(8,128)S(1)}, u32[]{:S(2)}, u32[]{:S(2)}) async-start(f32[8,24,128]{2,1,0:T(8,128)} %shard_map.259), calls=%async_computation.4 | async-start | bytes 196608 | tf_op jit(solution)/shard_map/all_to_all | solution.py:716
  145.3 0.8 reshape.100
  146.1 4.5 %all-to-all-done.4.whole_ref = f32[8,24,128]{2,1,0:T(8,128)S(1)} async-done(((f32[8,24,128]{2,1,0:T(8,128)}), f32[8,24,128]{2,1,0:T(8,128)S(1)}, u32[]{:S(2)}, u32[]{:S(2)}) %all-to-all-start.4) | async-done | bytes 98336 | tf_op jit(solution)/shard_map/all_to_all | solution.py:716
  150.6 0.7 shard_map.260
  (65 shorter events, 5.8 us)
Async XLA Ops:
  6.0 9.3 %collective-permute-start = (bf16[24,1,96]{2,0,1:T(8,128)(2,1)S(1)}, bf16[24,1,96]{2,0,1:T(8,128)(2,1)S(1)}, u32[]{:S(2)}, u32[]{:S(2)}) collective-permute-start(bf16[24,1,96]{2,0,1:T(8,128)(2,1)S(1)} %slice_select_fusion.2), channel_id=1, source_target_pairs={{0,8},{8,16},{16,24},{24,32},{32,40},{40,48},{48,56},{56,64},{64,7... | collective-permute-start | bytes 13832 | tf_op jit(solution)/shard_map/ppermute | solution.py:685
  6.1 9.3 %collective-permute-start.1 = (bf16[24,1,96]{2,0,1:T(8,128)(2,1)S(1)}, bf16[24,1,96]{2,0,1:T(8,128)(2,1)S(1)}, u32[]{:S(2)}, u32[]{:S(2)}) collective-permute-start(bf16[24,1,96]{2,0,1:T(8,128)(2,1)S(1)} %get-tuple-element.84), channel_id=1, source_target_pairs={{0,248},{8,0},{16,8},{24,16},{32,24},{40,32},{48,40},{56,48},{64,5... | collective-permute-start | bytes 13832 | tf_op jit(solution)/shard_map/ppermute | solution.py:685
  15.5 7.7 %collective-permute-start.3 = (bf16[1,26,96]{2,0,1:T(2,128)(2,1)S(1)}, bf16[1,26,96]{2,0,1:T(2,128)(2,1)S(1)}, u32[]{:S(2)}, u32[]{:S(2)}) collective-permute-start(bf16[1,26,96]{2,0,1:T(2,128)(2,1)S(1)} %get-tuple-element.83), channel_id=1, source_target_pairs={{0,192},{8,200},{16,208},{24,216},{32,224},{40,232},{48,240},{56,2... | collective-permute-start | bytes 14984 | tf_op jit(solution)/shard_map/ppermute | solution.py:685
  20.4 10.0 %collective-permute-start.2 = (bf16[1,26,96]{2,0,1:T(2,128)(2,1)S(1)}, bf16[1,26,96]{2,0,1:T(2,128)(2,1)S(1)}, u32[]{:S(2)}, u32[]{:S(2)}) collective-permute-start(bf16[1,26,96]{2,0,1:T(2,128)(2,1)S(1)} %get-tuple-element.82), channel_id=1, source_target_pairs={{0,64},{8,72},{16,80},{24,88},{32,96},{40,104},{48,112},{56,120},{... | collective-permute-start | bytes 14984 | tf_op jit(solution)/shard_map/ppermute | solution.py:685
  30.6 14.0 %copy-start.9 = (bf16[96]{0:T(256)(128)(2,1)S(1)}, bf16[96]{0:T(256)(128)(2,1)}, u32[]{:S(2)}) copy-start(bf16[96]{0:T(256)(128)(2,1)} %param.31) | copy-start | bytes 580
  30.6 14.0 %copy-start.4 = (bf16[256]{0:T(256)(128)(2,1)S(1)}, bf16[256]{0:T(256)(128)(2,1)}, u32[]{:S(2)}) copy-start(bf16[256]{0:T(256)(128)(2,1)} %param.21) | copy-start | bytes 1540
  30.6 14.3 %copy-start.5 = (bf16[256]{0:T(256)(128)(2,1)S(1)}, bf16[256]{0:T(256)(128)(2,1)}, u32[]{:S(2)}) copy-start(bf16[256]{0:T(256)(128)(2,1)} %param.23) | copy-start | bytes 1540
  30.6 14.5 %copy-start.6 = (bf16[256]{0:T(256)(128)(2,1)S(1)}, bf16[256]{0:T(256)(128)(2,1)}, u32[]{:S(2)}) copy-start(bf16[256]{0:T(256)(128)(2,1)} %param.24) | copy-start | bytes 1540
  30.6 14.7 %copy-start.7 = (bf16[256]{0:T(256)(128)(2,1)S(1)}, bf16[256]{0:T(256)(128)(2,1)}, u32[]{:S(2)}) copy-start(bf16[256]{0:T(256)(128)(2,1)} %param.25) | copy-start | bytes 1540
  30.6 14.9 %copy-start.8 = (bf16[256]{0:T(256)(128)(2,1)S(1)}, bf16[256]{0:T(256)(128)(2,1)}, u32[]{:S(2)}) copy-start(bf16[256]{0:T(256)(128)(2,1)} %param.29) | copy-start | bytes 1540
  30.7 15.3 %copy-start.3 = (bf16[1024]{0:T(1024)(128)(2,1)S(1)}, bf16[1024]{0:T(1024)(128)(2,1)}, u32[]{:S(2)}) copy-start(bf16[1024]{0:T(1024)(128)(2,1)} %param.27) | copy-start | bytes 6148
  31.0 1.9 %collective-permute-start.5 = (bf16[26,5,96]{2,1,0:T(8,128)(2,1)S(1)}, bf16[26,5,96]{2,1,0:T(8,128)(2,1)S(1)}, u32[]{:S(2)}, u32[]{:S(2)}) collective-permute-start(bf16[26,5,96]{2,1,0:T(8,128)(2,1)S(1)} %get-tuple-element.77), channel_id=1, source_target_pairs={{0,248},{8,0},{16,8},{24,16},{32,24},{40,32},{48,40},{56,48},{64,5... | collective-permute-start | bytes 74888 | tf_op jit(solution)/shard_map/ppermute | solution.py:685
  31.3 7.3 %collective-permute-start.4 = (bf16[26,5,96]{2,1,0:T(8,128)(2,1)S(1)}, bf16[26,5,96]{2,1,0:T(8,128)(2,1)S(1)}, u32[]{:S(2)}, u32[]{:S(2)}) collective-permute-start(bf16[26,5,96]{2,1,0:T(8,128)(2,1)S(1)} %fusion.4), channel_id=1, source_target_pairs={{0,8},{8,16},{16,24},{24,32},{32,40},{40,48},{48,56},{56,64},{64,7... | collective-permute-start | bytes 74888 | tf_op jit(solution)/shard_map/ppermute | solution.py:685
  38.6 9.0 %collective-permute-start.7 = (bf16[5,36,96]{2,1,0:T(8,128)(2,1)S(1)}, bf16[5,36,96]{2,1,0:T(8,128)(2,1)S(1)}, u32[]{:S(2)}, u32[]{:S(2)}) collective-permute-start(bf16[5,36,96]{2,1,0:T(8,128)(2,1)S(1)} %get-tuple-element.72), channel_id=1, source_target_pairs={{0,192},{8,200},{16,208},{24,216},{32,224},{40,232},{48,240},{56,2... | collective-permute-start | bytes 103688 | tf_op jit(solution)/shard_map/ppermute | solution.py:685
  41.3 10.4 %collective-permute-start.6 = (bf16[5,36,96]{2,1,0:T(8,128)(2,1)S(1)}, bf16[5,36,96]{2,1,0:T(8,128)(2,1)S(1)}, u32[]{:S(2)}, u32[]{:S(2)}) collective-permute-start(bf16[5,36,96]{2,1,0:T(8,128)(2,1)S(1)} %get-tuple-element.71), channel_id=1, source_target_pairs={{0,64},{8,72},{16,80},{24,88},{32,96},{40,104},{48,112},{56,120},{... | collective-permute-start | bytes 103688 | tf_op jit(solution)/shard_map/ppermute | solution.py:685
  65.3 7.1 %copy-start.2 = (bf16[24,2304]{1,0:T(8,128)(2,1)S(1)}, bf16[24,2304]{1,0:T(8,128)(2,1)}, u32[]{:S(2)}) copy-start(bf16[24,2304]{1,0:T(8,128)(2,1)} %param.18) | copy-start | bytes 331780
  65.3 15.2 %all-to-all-start = ((bf16[8,144,384]{2,1,0:T(8,128)(2,1)}), bf16[8,144,384]{2,1,0:T(8,128)(2,1)S(1)}, u32[]{:S(2)}, u32[]{:S(2)}) async-start(bf16[8,144,384]{2,1,0:T(8,128)(2,1)} %get-tuple-element.45), calls=%async_computation | async-start | bytes 1769472 | tf_op jit(solution)/shard_map/all_to_all | solution.py:716
  80.5 0.9 copy-start
  90.3 17.7 %all-to-all-start.1 = ((bf16[8,32,16,128]{3,2,1,0:T(8,128)(2,1)}), bf16[8,32,16,128]{3,2,1,0:T(8,128)(2,1)S(1)}, u32[]{:S(2)}, u32[]{:S(2)}) async-start(bf16[8,32,16,128]{3,2,1,0:T(8,128)(2,1)} %get-tuple-element.52), calls=%async_computation.1 | async-start | bytes 2097152 | tf_op jit(solution)/shard_map/all_to_all | solution.py:716
  121.6 23.7 %copy-start.1 = (f32[576,96]{1,0:T(8,128)S(1)}, f32[576,96]{1,0:T(8,128)}, u32[]{:S(2)}) copy-start(f32[576,96]{1,0:T(8,128)} %get-tuple-element.44) | copy-start | bytes 663556
  140.8 9.8 %all-to-all-start.4 = ((f32[8,24,128]{2,1,0:T(8,128)}), f32[8,24,128]{2,1,0:T(8,128)S(1)}, u32[]{:S(2)}, u32[]{:S(2)}) async-start(f32[8,24,128]{2,1,0:T(8,128)} %shard_map.259), calls=%async_computation.4 | async-start | bytes 196608 | tf_op jit(solution)/shard_map/all_to_all | solution.py:716

commit v3 on v2

--- a/solution.py
+++ b/solution.py
@@ -41,168 +41,220 @@
     )[quarter]
 
 
-def gather_patches(turns, wide_ref, stage_ref, patches_ref):
-    bands = ((0, 0, 3), (3, 5, SIDE), (27, 31, 3))
-    turn_of = {(1, 0): 0, (1, 2): 1, (0, 0): 2, (0, 2): 3, (2, 0): 4, (2, 2): 5}
+BANDS = ((0, 0, 3), (3, 5, SIDE), (27, 31, 3))
+
+
+def gather_patches(pieces, wide_ref, stage_ref, patches_ref):
     stage_ref[...] = jnp.zeros_like(stage_ref)
+    cells = patches_ref.shape[0]
     for row_off in range(3):
         for col_off in range(3):
-            for row_band, (row_to, row_from, row_len) in enumerate(bands):
-                for col_band, (col_to, col_from, col_len) in enumerate(bands):
-
-                    def read(quarter):
-                        row, col = turned_offset(quarter, row_off, col_off)
-                        return wide_ref[
-                            row_from + row : row_from + row + row_len,
-                            col_from + col : col_from + col + col_len,
-                            :,
-                        ]
-
-                    piece = read(0)
-                    if (row_band, col_band) in turn_of:
-                        turn = turns[turn_of[row_band, col_band]]
-                        for quarter in range(1, 4):
-                            piece = jnp.where(turn == quarter, read(quarter), piece)
-                    stage_ref[row_to : row_to + row_len, col_to : col_to + col_len, :] = piece
+            for turn, row_to, row_from, row_len, col_to, col_from, col_len in pieces:
+
+                def read(quarter):
+                    row, col = turned_offset(quarter, row_off, col_off)
+                    return wide_ref[
+                        row_from + row : row_from + row + row_len,
+                        col_from + col : col_from + col + col_len,
+                        :,
+                    ]
+
+                piece = read(0)
+                if turn is not None:
+                    for quarter in range(1, 4):
+                        piece = jnp.where(turn == quarter, read(quarter), piece)
+                stage_ref[row_to : row_to + row_len, col_to : col_to + col_len, :] = piece
             at = (3 * row_off + col_off) * LANE
-            patches_ref[:, at : at + LANE] = stage_ref[...].reshape(960, LANE).astype(BF16)
-
-
-def forward_kernel(
-    seam_turns_ref,
-    source_ref,
-    w_in_ref,
-    w_depth_low_ref,
-    vectors_ref,
-    w_up_ref,
-    w_down_ref,
-    head_ref,
-    patches_out,
-    stem_out,
-    normed_ref,
-    inverse_ref,
-    scaled_ref,
-    slope_out,
-    active_out,
-    hidden_ref,
-    field_ref,
-    tight_ref,
-    sent_ref,
-    w_depth_ref,
-    patches_ref,
-    stem_ref,
-    slope_ref,
-    active_ref,
-    wide_ref,
-    stage_ref,
-    w_in_wide_ref,
-    whole_sem,
-    part_sem,
-):
-    def send_part(part, row):
-        at = pl.ds(row, 96)
-        return (
-            pltpu.make_async_copy(slope_ref.at[at], slope_out.at[at], part_sem.at[0, part]),
-            pltpu.make_async_copy(active_ref.at[at], active_out.at[at], part_sem.at[1, part]),
-        )
-
-    send_patches = pltpu.make_async_copy(patches_ref, patches_out, whole_sem.at[0])
-    send_stem = pltpu.make_async_copy(stem_ref, stem_out, whole_sem.at[1])
+            patches_ref[:, at : at + LANE] = stage_ref[...].reshape(cells, LANE).astype(BF16)
+
+
+def turn_reader(seam_turns_ref):
     tile = lax.axis_index("space")
     tiles = seam_turns_ref.shape[0]
-    across = tiles // 4
-
-    def turn_at(offset):
-        return seam_turns_ref[lax.rem(tile + (tiles + offset), tiles)]
-
-    turns = (
-        turn_at(0),
-        (4 - turn_at(1)) & 3,
-        turn_at(-across),
-        (4 - turn_at(1 - across)) & 3,
-        turn_at(across),
-        (4 - turn_at(across + 1)) & 3,
-    )
-    b_in, b_depth, gain, shift, b_down = (vectors_ref[k : k + 1, :] for k in range(5))
-    head_bias = vectors_ref[5:6, 0:96]
-    b_up = jnp.concatenate([vectors_ref[6 + k : 7 + k, :] for k in range(4)], axis=1)
-    w_depth_ref[...] = w_depth_low_ref[...].astype(F32)
+    return lambda offset: seam_turns_ref[lax.rem(tile + (tiles + offset), tiles)], tiles // 4
+
+
+def widen_stem_weight(w_in_ref, w_in_wide_ref):
     for offset in range(9):
         w_in_wide_ref[offset * LANE : offset * LANE + 96, :] = w_in_ref[offset * 96 : (offset + 1) * 96, :]
         w_in_wide_ref[offset * LANE + 96 : (offset + 1) * LANE, :] = jnp.zeros((32, 256), BF16)
+
+
+def normalise_block(slab_row, row, stem_ref, w_depth_ref, vectors_ref, normed_ref, inverse_ref, scaled_ref):
+    halves = []
+    for half in range(2):
+        lanes = slice(half * LANE, (half + 1) * LANE)
+        total = jnp.zeros((4, SIDE, LANE), F32)
+        for col_off in range(7):
+            slab = stem_ref[half, pl.ds(slab_row, 10), col_off : col_off + SIDE, :]
+            for row_off in range(7):
+                tap = 7 * row_off + col_off
+                total = total + slab[row_off : row_off + 4] * w_depth_ref[tap : tap + 1, lanes][None]
+        halves.append(total.reshape(4 * SIDE, LANE) + vectors_ref[1:2, lanes])
+    mean = (
+        jnp.sum(halves[0], axis=-1, keepdims=True) + jnp.sum(halves[1], axis=-1, keepdims=True)
+    ) / 256.0
+    centers = [h - mean for h in halves]
+    spread = (
+        jnp.sum(centers[0] * centers[0], axis=-1, keepdims=True)
+        + jnp.sum(centers[1] * centers[1], axis=-1, keepdims=True)
+    ) / 256.0
+    inverse = lax.rsqrt(spread + EPS)
+    at = pl.ds(row, 96)
+    inverse_ref[at, :] = jnp.broadcast_to(inverse, (96, LANE))
+    for half in range(2):
+        lanes = slice(half * LANE, (half + 1) * LANE)
+        normed = centers[half] * inverse
+        normed_ref[at, lanes] = normed
+        scaled_ref[at, lanes] = (normed * vectors_ref[2:3, lanes] + vectors_ref[3:4, lanes]).astype(BF16)
+
+
+def mix_block(
+    own_row, row, stem_ref, vectors_ref, w_up_ref, w_down_ref, head_ref,
+    scaled_ref, slope_ref, active_ref, hidden_ref,
+):
+    b_up = jnp.concatenate([vectors_ref[6 + k : 7 + k, :] for k in range(4)], axis=1)
+    at = pl.ds(row, 96)
+    upward = dot(scaled_ref[at, :], w_up_ref[...]) + b_up
+    square = upward * upward
+    tanh_part = jnp.tanh(ROOT * (upward + CUBIC * square * upward))
+    plus = 0.5 * (1.0 + tanh_part)
+    slope = plus + 0.5 * upward * (1.0 - tanh_part * tanh_part) * (ROOT + (3.0 * CUBIC * ROOT) * square)
+    slope_ref[at, :] = slope.astype(BF16)
+    active = (upward * plus).astype(BF16)
+    active_ref[at, :] = active
+    own = [
+        stem_ref[half, pl.ds(own_row, 4), 3 : 3 + SIDE, :].reshape(96, LANE) for half in range(2)
+    ]
+    own = jnp.concatenate(own, axis=1)
+    hidden = (own + dot(active, w_down_ref[...]) + vectors_ref[4:5, :]).astype(BF16)
+    hidden_ref[at, :] = hidden
+    return dot(hidden, head_ref[...], 1, 1) + vectors_ref[5:6, 0:96]
+
+
+def middle_forward_kernel(
+    seam_turns_ref, band_ref, w_in_ref, w_depth_low_ref, vectors_ref, w_up_ref, w_down_ref, head_ref,
+    patches_out, stem_out, normed_out, inverse_out, scaled_out, slope_out, active_out, hidden_out,
+    field_ref, w_depth_ref,
+    patches_ref, stem_ref, normed_ref, inverse_ref, scaled_ref, slope_ref, active_ref, hidden_ref,
+    wide_ref, stage_ref, w_in_wide_ref, sem,
+):
+    pairs = ((normed_ref, normed_out), (inverse_ref, inverse_out), (scaled_ref, scaled_out),
+             (slope_ref, slope_out), (active_ref, active_out), (hidden_ref, hidden_out))
+    sends = [pltpu.make_async_copy(a, b.at[96:480], sem.at[2 + k]) for k, (a, b) in enumerate(pairs)]
+    send_patches = pltpu.make_async_copy(patches_ref, patches_out.at[96:864], sem.at[0])
+    send_stem = pltpu.make_async_copy(stem_ref, stem_out.at[:, 3:27], sem.at[1])
+    turn_at, _ = turn_reader(seam_turns_ref)
+    w_depth_ref[...] = w_depth_low_ref[...].astype(F32)
+    widen_stem_weight(w_in_ref, w_in_wide_ref)
     wide_ref[...] = jnp.zeros_like(wide_ref)
-    wide_ref[:, 0:36, 0:96] = source_ref[...].astype(F32)
-    gather_patches(turns, wide_ref, stage_ref, patches_ref)
+    wide_ref[:, 0:36, 0:96] = band_ref[...].astype(F32)
+    turns = (turn_at(0), None, (4 - turn_at(1)) & 3)
+    pieces = [(turn, 0, 0, SIDE) + columns for turn, columns in zip(turns, BANDS)]
+    gather_patches(pieces, wide_ref, stage_ref, patches_ref)
     send_patches.start()
-    for part in range(5):
-        rows = slice(part * 192, (part + 1) * 192)
-        stem = dot(patches_ref[rows, :], w_in_wide_ref[...]) + b_in
+    for part in range(4):
+        stem = dot(patches_ref[part * 192 : (part + 1) * 192, :], w_in_wide_ref[...]) + vectors_ref[0:1, :]
         stem = stem.astype(BF16).astype(F32)
         for half in range(2):
             stem_ref[half, part * 6 : (part + 1) * 6] = stem[
                 :, half * LANE : (half + 1) * LANE
             ].reshape(6, 32, LANE)
-
     send_stem.start()
 
     def normalise(block, carry):
-        row = block * 4
-        halves = []
-        for half in range(2):
-            lanes = slice(half * LANE, (half + 1) * LANE)
-            total = jnp.zeros((4, SIDE, LANE), F32)
-            for col_off in range(7):
-                slab = stem_ref[half, pl.ds(row, 10), col_off : col_off + SIDE, :]
-                for row_off in range(7):
-                    tap = 7 * row_off + col_off
-                    total = total + slab[row_off : row_off + 4] * w_depth_ref[tap : tap + 1, lanes][None]
-            halves.append(total.reshape(4 * SIDE, LANE) + b_depth[:, lanes])
-        mean = (
-            jnp.sum(halves[0], axis=-1, keepdims=True) + jnp.sum(halves[1], axis=-1, keepdims=True)
-        ) / 256.0
-        centers = [h - mean for h in halves]
-        spread = (
-            jnp.sum(centers[0] * centers[0], axis=-1, keepdims=True)
-            + jnp.sum(centers[1] * centers[1], axis=-1, keepdims=True)
-        ) / 256.0
-        inverse = lax.rsqrt(spread + EPS)
-        at = pl.ds(pl.multiple_of(block * 96, 96), 96)
-        inverse_ref[at, :] = jnp.broadcast_to(inverse, (96, LANE))
-        for half in range(2):
-            lanes = slice(half * LANE, (half + 1) * LANE)
-            normed = centers[half] * inverse
-            normed_ref[at, lanes] = normed
-            scaled_ref[at, lanes] = (normed * gain[:, lanes] + shift[:, lanes]).astype(BF16)
+        normalise_block(
+            1 + 4 * block, pl.multiple_of(block * 96, 96), stem_ref, w_depth_ref, vectors_ref,
+            normed_ref, inverse_ref, scaled_ref,
+        )
         return carry
 
-    lax.fori_loop(0, 6, normalise, 0)
-
-    def mix(part, carry):
-        row = pl.multiple_of(part * 96, 96)
-        at = pl.ds(row, 96)
-        upward = dot(scaled_ref[at, :], w_up_ref[...]) + b_up
-        square = upward * upward
-        tanh_part = jnp.tanh(ROOT * (upward + CUBIC * square * upward))
-        plus = 0.5 * (1.0 + tanh_part)
-        slope = plus + 0.5 * upward * (1.0 - tanh_part * tanh_part) * (
-            ROOT + (3.0 * CUBIC * ROOT) * square
+    lax.fori_loop(0, 4, normalise, 0)
+
+    def mix(block, carry):
+        row = pl.multiple_of(block * 96, 96)
+        field_ref[pl.ds(row, 96), :] = mix_block(
+            4 + 4 * block, row, stem_ref, vectors_ref, w_up_ref, w_down_ref, head_ref,
+            scaled_ref, slope_ref, active_ref, hidden_ref,
         )
-        slope_ref[at, :] = slope.astype(BF16)
-        active = (upward * plus).astype(BF16)
-        active_ref[at, :] = active
-        for send in send_part(part, row):
-            send.start()
-        own = [
-            stem_ref[half, pl.ds(3 + 4 * part, 4), 3 : 3 + SIDE, :].reshape(96, LANE)
-            for half in range(2)
-        ]
-        own = jnp.concatenate(own, axis=1)
-        hidden = (own + dot(active, w_down_ref[...]) + b_down).astype(BF16)
-        hidden_ref[at, :] = hidden
-        field_ref[at, :] = dot(hidden, head_ref[...], 1, 1) + head_bias
         return carry
 
-    lax.fori_loop(0, 6, mix, 0)
+    lax.fori_loop(0, 4, mix, 0)
+    for send in sends:
+        send.start()
+    for send in sends + [send_patches, send_stem]:
+        send.wait()
+
+
+def rim_forward_kernel(
+    seam_turns_ref, north_ref, south_ref, w_in_ref, w_depth_ref, vectors_ref, w_up_ref, w_down_ref,
+    head_ref, middle_field_ref,
+    patches_in, stem_in, normed_in, inverse_in, scaled_in, slope_in, active_in, hidden_in,
+    patches_out, stem_out, normed_out, inverse_out, scaled_out, slope_out, active_out, hidden_out,
+    field_ref, tight_ref, sent_ref,
+    patches_ref, stem_ref, normed_ref, inverse_ref, scaled_ref, slope_ref, active_ref, hidden_ref,
+    wide_ref, stage_ref, w_in_wide_ref, sem,
+):
+    fetches = [
+        pltpu.make_async_copy(stem_in.at[:, 3:10], stem_ref.at[:, 3:10], sem.at[0, 0]),
+        pltpu.make_async_copy(stem_in.at[:, 20:27], stem_ref.at[:, 10:17], sem.at[0, 1]),
+    ]
+    for fetch in fetches:
+        fetch.start()
+    pairs = ((normed_ref, normed_out), (inverse_ref, inverse_out), (scaled_ref, scaled_out),
+             (slope_ref, slope_out), (active_ref, active_out), (hidden_ref, hidden_out))
+    sends = []
+    for k, (here, there) in enumerate(pairs):
+        sends.append(pltpu.make_async_copy(here.at[0:96], there.at[0:96], sem.at[1, 2 + k]))
+        sends.append(pltpu.make_async_copy(here.at[96:192], there.at[480:576], sem.at[2, 2 + k]))
+    early_sends = [
+        pltpu.make_async_copy(patches_ref.at[0:96], patches_out.at[0:96], sem.at[1, 0]),
+        pltpu.make_async_copy(patches_ref.at[96:192], patches_out.at[864:960], sem.at[2, 0]),
+        pltpu.make_async_copy(stem_ref.at[:, 0:3], stem_out.at[:, 0:3], sem.at[1, 1]),
+        pltpu.make_async_copy(stem_ref.at[:, 17:20], stem_out.at[:, 27:30], sem.at[2, 1]),
+    ]
+    turn_at, across = turn_reader(seam_turns_ref)
+    widen_stem_weight(w_in_ref, w_in_wide_ref)
+    wide_ref[...] = jnp.zeros_like(wide_ref)
+    wide_ref[0:5, 0:36, 0:96] = north_ref[...].astype(F32)
+    wide_ref[5:10, 0:36, 0:96] = south_ref[...].astype(F32)
+    north = (turn_at(-across), None, (4 - turn_at(1 - across)) & 3)
+    south = (turn_at(across), None, (4 - turn_at(across + 1)) & 3)
+    pieces = [(turn, 0, 0, 3) + columns for turn, columns in zip(north, BANDS)]
+    pieces += [(turn, 3, 5, 3) + columns for turn, columns in zip(south, BANDS)]
+    gather_patches(pieces, wide_ref, stage_ref, patches_ref)
+    stem = dot(patches_ref[...], w_in_wide_ref[...]) + vectors_ref[0:1, :]
+    stem = stem.astype(BF16).astype(F32)
+    for half in range(2):
+        lanes = slice(half * LANE, (half + 1) * LANE)
+        stem_ref[half, 0:3] = stem[0:96, lanes].reshape(3, 32, LANE)
+        stem_ref[half, 17:20] = stem[96:192, lanes].reshape(3, 32, LANE)
+    for send in early_sends:
+        send.start()
+    for fetch in fetches:
+        fetch.wait()
+
+    def normalise(block, carry):
+        normalise_block(
+            10 * block, pl.multiple_of(block * 96, 96), stem_ref, w_depth_ref, vectors_ref,
+            normed_ref, inverse_ref, scaled_ref,
+        )
+        return carry
+
+    lax.fori_loop(0, 2, normalise, 0)
+    field_ref[96:480, :] = middle_field_ref[...]
+
+    def mix(block, carry):
+        row = pl.multiple_of(block * 96, 96)
+        field_ref[pl.ds(pl.multiple_of(block * 480, 96), 96), :] = mix_block(
+            10 * block + 3, row, stem_ref, vectors_ref, w_up_ref, w_down_ref, head_ref,
+            scaled_ref, slope_ref, active_ref, hidden_ref,
+        )
+        return carry
+
+    lax.fori_loop(0, 2, mix, 0)
+    for send in sends:
+        send.start()
     for quarter in range(4):
         tight_ref[:, 96 * quarter : 96 * (quarter + 1)] = field_ref[
             144 * quarter : 144 * (quarter + 1), :
@@ -210,11 +262,8 @@
     sent = tight_ref[...].astype(BF16)
     for member in range(sent_ref.shape[0]):
         sent_ref[member] = sent
-    send_patches.wait()
-    send_stem.wait()
-    for part in range(6):
-        for send in send_part(part, 96 * part):
-            send.wait()
+    for send in sends + early_sends:
+        send.wait()
 
 
 def mixer_backward_kernel(
@@ -516,7 +565,7 @@
     small_ref[...] = small.T[48:64, :]
 
 
-def call(kernel, outs, scratch, *operands, spaces=None, vmem=VMEM_BYTES, flops=0):
+def call(kernel, outs, scratch, *operands, spaces=None, vmem=VMEM_BYTES, flops=0, aliases=None):
     kinds = {"v": pltpu.VMEM, "s": pltpu.SMEM, "a": pl.ANY}
     spaces = spaces or "v" * len(operands)
     return pl.pallas_call(
@@ -525,6 +574,7 @@
         in_specs=[pl.BlockSpec(memory_space=kinds[letter]) for letter in spaces],
         out_specs=[pl.BlockSpec(memory_space=kinds[letter]) for _, _, letter in outs],
         scratch_shapes=[x if not isinstance(x, tuple) else pltpu.VMEM(*x) for x in scratch],
+        input_output_aliases=aliases or {},
         compiler_params=pltpu.CompilerParams(vmem_limit_bytes=vmem),
         cost_estimate=pl.CostEstimate(flops=flops, bytes_accessed=8_000_000, transcendentals=0),
     )(*operands)
@@ -535,45 +585,62 @@
     return jnp.concatenate(rows).astype(F32).reshape(10, 256)
 
 
-def run_forward(seam_turns, source, w_in, w_depth, vectors, w_up, w_down, head, members):
-    return call(
-        forward_kernel,
-        [
-            ((960, 1152), BF16, "a"),
-            ((2, 30, 32, LANE), F32, "a"),
-            ((CELLS, 256), F32, "v"),
-            ((CELLS, LANE), F32, "v"),
-            ((CELLS, 256), BF16, "v"),
-            ((CELLS, 1024), BF16, "a"),
-            ((CELLS, 1024), BF16, "a"),
-            ((CELLS, 256), BF16, "v"),
-            ((CELLS, 96), F32, "v"),
-            ((144, 384), F32, "v"),
-            ((members, 144, 384), BF16, "v"),
-            ((49, 256), F32, "v"),
-        ],
-        [
-            ((960, 1152), BF16),
-            ((2, 30, 32, LANE), F32),
-            ((CELLS, 1024), BF16),
-            ((CELLS, 1024), BF16),
-            ((36, 40, LANE), F32),
-            ((30, 32, LANE), F32),
-            ((1152, 256), BF16),
-            pltpu.SemaphoreType.DMA((2,)),
-            pltpu.SemaphoreType.DMA((2, 6)),
-        ],
-        seam_turns,
-        source,
-        w_in,
-        w_depth,
-        vectors,
-        w_up,
-        w_down,
-        head,
+KEPT = (
+    ((960, 1152), BF16),
+    ((2, 30, 32, LANE), F32),
+    ((CELLS, 256), F32),
+    ((CELLS, LANE), F32),
+    ((CELLS, 256), BF16),
+    ((CELLS, 1024), BF16),
+    ((CELLS, 1024), BF16),
+    ((CELLS, 256), BF16),
+)
+
+
+def forward_scratch(patch_rows, stem_rows, cells, wide_rows, semaphores):
+    return [
+        ((patch_rows, 1152), BF16),
+        ((2, stem_rows, 32, LANE), F32),
+        ((cells, 256), F32),
+        ((cells, LANE), F32),
+        ((cells, 256), BF16),
+        ((cells, 1024), BF16),
+        ((cells, 1024), BF16),
+        ((cells, 256), BF16),
+        ((wide_rows, 40, LANE), F32),
+        ((patch_rows // 32, 32, LANE), F32),
+        ((1152, 256), BF16),
+        pltpu.SemaphoreType.DMA(semaphores),
+    ]
+
+
+def run_middle_forward(seam_turns, band, w_in, w_depth, vectors, w_up, w_down, head):
+    outs = call(
+        middle_forward_kernel,
+        [(shape, kind, "a") for shape, kind in KEPT]
+        + [((384, 96), F32, "v"), ((49, 256), F32, "v")],
+        forward_scratch(768, SIDE, 384, 26, (8,)),
+        seam_turns, band, w_in, w_depth, vectors, w_up, w_down, head,
         spaces="svvvvvvv",
         flops=10_000_000_000,
     )
+    return outs[:8], outs[8], outs[9]
+
+
+def run_rim_forward(
+    seam_turns, north, south, w_in, w_depth, vectors, w_up, w_down, head, middle_field, kept, members
+):
+    outs = call(
+        rim_forward_kernel,
+        [(shape, kind, "a") for shape, kind in KEPT]
+        + [((CELLS, 96), F32, "v"), ((144, 384), F32, "v"), ((members, 144, 384), BF16, "v")],
+        forward_scratch(192, 20, 192, 10, (3, 8)),
+        seam_turns, north, south, w_in, w_depth, vectors, w_up, w_down, head, middle_field, *kept,
+        spaces="svvvvvvvvvaaaaaaaa",
+        aliases={10 + k: k for k in range(8)},
+        flops=5_000_000_000,
+    )
+    return outs[:8], outs[8], outs[9], outs[10]
 
 
 def run_mixer_backward(every, tight, target, saved, head, w_down, w_up, coefficient):
@@ -703,13 +770,13 @@
     return result
 
 
-def seam_pad(tile, my_turn, next_turn, margin, row_tiles):
+def seam_strips(tile, my_turn, next_turn, margin, row_tiles):
     came_west = shifted(turned_edge(tile, next_turn, margin, True), "space", 1)
     came_east = shifted(turned_edge(tile, (4 - my_turn) % 4, margin, False), "space", -1)
     widened = jnp.concatenate([came_west, tile, came_east], axis=1)
     came_north = shifted(widened[-margin:], "space", row_tiles)
     came_south = shifted(widened[:margin], "space", -row_tiles)
-    return jnp.concatenate([came_north, widened, came_south], axis=0)
+    return came_north, widened, came_south
 
 
 def swap(value, axis):
@@ -747,12 +814,17 @@
     source = (
         initial_state.astype(F32) + starting_field_nudges[0].astype(F32)
     ).astype(BF16).reshape(SIDE, SIDE, 96)
-    near = seam_pad(source, my_turn, next_turn, 1, row_tiles)
-    wide_source = seam_pad(near, my_turn, next_turn, 5, row_tiles)
+    near = jnp.concatenate(seam_strips(source, my_turn, next_turn, 1, row_tiles), axis=0)
+    north, band, south = seam_strips(near, my_turn, next_turn, 5, row_tiles)
     vectors = stack_vectors(b_in, b_depth, norm_gain, norm_shift, b_down, head_bias, b_up)
     head = head_weight.T
-    saved = run_forward(seam_turns, wide_source, w_in, w_depth, vectors, w_up, w_down, head, members)
-    patches, stem, normed, inverse, scaled, slope, active, hidden, field, tight, sent, w_depth_wide = saved
+    kept, middle_field, w_depth_wide = run_middle_forward(
+        seam_turns, band, w_in, w_depth, vectors, w_up, w_down, head
+    )
+    kept, field, tight, sent = run_rim_forward(
+        seam_turns, north, south, w_in, w_depth_wide, vectors, w_up, w_down, head, middle_field, kept, members
+    )
+    patches, stem, normed, inverse, scaled, slope, active, hidden = kept
     sent, verifying_analysis, field_again = lax.optimization_barrier((sent, verifying_analysis, field))
     every = swap(sent, "ens")
     predicted = field_again.reshape(1, SIDE, SIDE * 96)

time: 153 us -> 154 us (level)
  waiting for transfers between devices: 33.3 us -> 14.5 us
  starting transfers between devices: 35.7 us -> 46.2 us
  blocking collectives: 31.8 us -> 36.9 us
  Pallas kernels: 36.2 us -> 40.7 us
    ppermute x8, waiting for transfers between devices: 21.8 us -> 3 us  [shifted(): lax.ppermute(value, axis, [(i, (i + by) % peers) for i in range(peers)])]
    ppermute x8, starting transfers between devices: 20.8 us -> 31.1 us  [shifted(): lax.ppermute(value, axis, [(i, (i + by) % peers) for i in range(peers)])]
    all_to_all x2, blocking collectives: 31.8 us -> 36.9 us  [swap(): return lax.all_to_all(value, axis, 0, 0, tiled=True)]
    pallas_call x6 -> x7, Pallas kernels: 36.2 us -> 40.7 us  [call(): pl.pallas_call(kernel, out_shape=[jax.ShapeDtypeStruct(shape, kind) for s...]
  transfers between devices with their start and end apart: 11 -> 11, of which waited for: 10 -> 5; matrix products, arithmetic and copies ran while one was open for 4% -> 3% of each run, Pallas kernels for 9% -> 15%
where the time goes in v3:
time: 154 us
  starting transfers between devices  46.2 us (30%)
  Pallas kernels  40.7 us (26%)
  blocking collectives  36.9 us (24%)
  waiting for transfers between devices  14.5 us (9%)
  local copies, waits for them, and re-layouts  8.86 us (6%)
  between operations  3.61 us (2%)
  other arithmetic  2.69 us (2%)
    pallas_call x7, Pallas kernels, call(): pl.pallas_call(kernel, out_shape=[jax.ShapeDtypeStruct(shape, kind) for s...  40.7 us
    all_to_all x2, blocking collectives, swap(): return lax.all_to_all(value, axis, 0, 0, tiled=True)  36.9 us
    ppermute x8, starting transfers between devices, shifted(): lax.ppermute(value, axis, [(i, (i + by) % peers) for i in range(peers)])  31.1 us
    all_to_all x3, starting transfers between devices, swap(): return lax.all_to_all(value, axis, 0, 0, tiled=True)  15.1 us
    all_to_all x3, waiting for transfers between devices, swap(): return lax.all_to_all(value, axis, 0, 0, tiled=True)  11.5 us
  transfers between devices with their start and end apart: 11, of which 5 were waited for; matrix products, arithmetic and copies ran while one was open for 3% of the time, Pallas kernels for 15%

profile of v3, /device:TPU:2, one launch (start us, length us, event | category | flops | bytes accessed | tf_op | source)
XLA Modules:
  0.0 153.5 jit_solution(16993695947954811668)
XLA Ops:
  0.7 1.3 fusion.17
  2.7 1.0 fusion.1
  6.1 8.0 %collective-permute-start.1 = (bf16[24,1,96]{2,0,1:T(8,128)(2,1)S(1)}, bf16[24,1,96]{2,0,1:T(8,128)(2,1)S(1)}, u32[]{:S(2)}, u32[]{:S(2)}) collective-permute-start(bf16[24,1,96]{2,0,1:T(8,128)(2,1)S(1)} %get-tuple-element.102), channel_id=1, source_target_pairs={{0,248},{8,0},{16,8},{24,16},{32,24},{40,32},{48,40},{56,48},{64,5... | collective-permute-start | bytes 13832 | tf_op jit(solution)/shard_map/ppermute | solution.py:752
  14.1 1.2 collective-permute-done
  15.5 2.2 %collective-permute-start.2 = (bf16[1,26,96]{2,0,1:T(2,128)(2,1)S(1)}, bf16[1,26,96]{2,0,1:T(2,128)(2,1)S(1)}, u32[]{:S(2)}, u32[]{:S(2)}) collective-permute-start(bf16[1,26,96]{2,0,1:T(2,128)(2,1)S(1)} %get-tuple-element.100), channel_id=1, source_target_pairs={{0,64},{8,72},{16,80},{24,88},{32,96},{40,104},{48,112},{56,120},{... | collective-permute-start | bytes 14984 | tf_op jit(solution)/shard_map/ppermute | solution.py:752
  17.7 6.2 %collective-permute-start.3 = (bf16[1,26,96]{2,0,1:T(2,128)(2,1)S(1)}, bf16[1,26,96]{2,0,1:T(2,128)(2,1)S(1)}, u32[]{:S(2)}, u32[]{:S(2)}) collective-permute-start(bf16[1,26,96]{2,0,1:T(2,128)(2,1)S(1)} %get-tuple-element.101), channel_id=1, source_target_pairs={{0,192},{8,200},{16,208},{24,216},{32,224},{40,232},{48,240},{56,2... | collective-permute-start | bytes 14984 | tf_op jit(solution)/shard_map/ppermute | solution.py:752
  23.9 1.7 %collective-permute-done.2 = bf16[1,26,96]{2,0,1:T(2,128)(2,1)S(1)} collective-permute-done((bf16[1,26,96]{2,0,1:T(2,128)(2,1)S(1)}, bf16[1,26,96]{2,0,1:T(2,128)(2,1)S(1)}, u32[]{:S(2)}, u32[]{:S(2)}) %collective-permute-start.2) | collective-permute-done | bytes 5024 | tf_op jit(solution)/shard_map/ppermute | solution.py:752
  26.5 6.1 %collective-permute-start.5 = (bf16[26,5,96]{2,1,0:T(8,128)(2,1)S(1)}, bf16[26,5,96]{2,1,0:T(8,128)(2,1)S(1)}, u32[]{:S(2)}, u32[]{:S(2)}) collective-permute-start(bf16[26,5,96]{2,1,0:T(8,128)(2,1)S(1)} %get-tuple-element.95), channel_id=1, source_target_pairs={{0,248},{8,0},{16,8},{24,16},{32,24},{40,32},{48,40},{56,48},{64,5... | collective-permute-start | bytes 74888 | tf_op jit(solution)/shard_map/ppermute | solution.py:752
  34.2 0.6 reshape.105.vectors_ref
  34.9 2.9 %collective-permute-start.6 = (bf16[5,36,96]{2,1,0:T(8,128)(2,1)S(1)}, bf16[5,36,96]{2,1,0:T(8,128)(2,1)S(1)}, u32[]{:S(2)}, u32[]{:S(2)}) collective-permute-start(bf16[5,36,96]{2,1,0:T(8,128)(2,1)S(1)} %get-tuple-element.90), channel_id=1, source_target_pairs={{0,64},{8,72},{16,80},{24,88},{32,96},{40,104},{48,112},{56,120},{... | collective-permute-start | bytes 103688 | tf_op jit(solution)/shard_map/ppermute | solution.py:752
  37.8 5.6 %collective-permute-start.7 = (bf16[5,36,96]{2,1,0:T(8,128)(2,1)S(1)}, bf16[5,36,96]{2,1,0:T(8,128)(2,1)S(1)}, u32[]{:S(2)}, u32[]{:S(2)}) collective-permute-start(bf16[5,36,96]{2,1,0:T(8,128)(2,1)S(1)} %get-tuple-element.89), channel_id=1, source_target_pairs={{0,192},{8,200},{16,208},{24,216},{32,224},{40,232},{48,240},{56,2... | collective-permute-start | bytes 103688 | tf_op jit(solution)/shard_map/ppermute | solution.py:752
  43.4 9.4 %shard_map.255 = (bf16[960,1152]{1,0:T(8,128)(2,1)}, f32[2,30,32,128]{3,2,1,0:T(8,128)}, f32[576,256]{1,0:T(8,128)}, f32[576,128]{1,0:T(8,128)}, bf16[576,256]{1...) custom-call(s32[32]{0:T(128)} %seam_turns_ref.3, ...), custom_call_target="tpu_custom_call" | custom-call | flops 10000000000 | bytes 8000000 | tf_op jit(solution)/shard_map/pallas_call | solution.py:571
  52.8 0.6 copy-done.10
  53.4 7.7 %shard_map.256 = (bf16[960,1152]{1,0:T(8,128)(2,1)}, f32[2,30,32,128]{3,2,1,0:T(8,128)}, f32[576,256]{1,0:T(8,128)}, f32[576,128]{1,0:T(8,128)}, bf16[576,256]{1...) custom-call(s32[32]{0:T(128)} %seam_turns_ref.3, ...), custom_call_target="tpu_custom_call", output_to_operand_aliasing={{0}: (10, {}), {1}: (11, {}), {2}: (12, {}), {3}: (13, {}),... | custom-call | flops 5000000000 | bytes 8000000 | tf_op jit(solution)/shard_map/pallas_call | solution.py:571
  61.2 6.0 %all-to-all-start = ((bf16[8,144,384]{2,1,0:T(8,128)(2,1)}), bf16[8,144,384]{2,1,0:T(8,128)(2,1)S(1)}, u32[]{:S(2)}, u32[]{:S(2)}) async-start(bf16[8,144,384]{2,1,0:T(8,128)(2,1)} %get-tuple-element.64), calls=%async_computation | async-start | bytes 1769472 | tf_op jit(solution)/shard_map/all_to_all | solution.py:783
  67.2 0.6 fusion.2.pick_ref
  67.8 0.7 fusion.order_ref
  68.7 0.8 reshape.102.target_ref
  69.5 7.1 %all-to-all-done.every_ref = bf16[8,144,384]{2,1,0:T(8,128)(2,1)S(1)} async-done(((bf16[8,144,384]{2,1,0:T(8,128)(2,1)}), bf16[8,144,384]{2,1,0:T(8,128)(2,1)S(1)}, u32[]{:S(2)}, u32[]{:S(2)}) %all-to-all-start) | async-done | bytes 884768 | tf_op jit(solution)/shard_map/all_to_all | solution.py:783
  76.6 0.9 copy-done
  77.5 8.8 %shard_map.257 = (bf16[8,32,16,128]{3,2,1,0:T(8,128)(2,1)}, f32[96,256]{1,0:T(8,128)}, f32[576,256]{1,0:T(8,128)}, f32[576,256]{1,0:T(8,128)}, f32[8,256]{1,0:T(8,128)}) custom-call(bf16[8,144,384]{2,1,0:T(8,128)(2,1)} %copy-done, f32[144,384]{1,0:T(8,128)} %get-tuple-element.65.own_ref, bf16[144,384]{1,0:T(8,128)(2,1)} %reshape.102.target_ref, ...), custom_call_target="tpu_custom_call" | custom-call | flops 12000000000 | bytes 8000000 | tf_op jit(solution)/shard_map/pallas_call | solution.py:571
  86.3 4.6 %all-to-all-start.1 = ((bf16[8,32,16,128]{3,2,1,0:T(8,128)(2,1)}), bf16[8,32,16,128]{3,2,1,0:T(8,128)(2,1)S(1)}, u32[]{:S(2)}, u32[]{:S(2)}) async-start(bf16[8,32,16,128]{3,2,1,0:T(8,128)(2,1)} %get-tuple-element.71), calls=%async_computation.1 | async-start | bytes 2097152 | tf_op jit(solution)/shard_map/all_to_all | solution.py:783
  91.0 13.1 %shard_map.258 = bf16[256,1152]{1,0:T(8,128)(2,1)} custom-call(f32[576,256]{1,0:T(8,128)} %get-tuple-element.72.scaled_grad_ref, f32[576,256]{1,0:T(8,128)} %get-tuple-element.73.normed_ref, f32[576,128]{1,0:T(8,128)} %get-tuple-element.74.inverse_ref, f32[10,256]{1,0:T(8,128)} %reshape.105.vectors_ref, f32[576,256]{1,0:T(8,128)} %get-tuple-element.75.hidden_grad_in, ...), custom_call_target="tpu_custom_call" | custom-call | flops 12000000000 | bytes 8000000 | tf_op jit(solution)/shard_map/pallas_call | solution.py:571
  104.0 13.6 %all_to_all.25.late_ref = bf16[8,32,1152]{2,1,0:T(8,128)(2,1)S(1)} all-to-all(bf16[8,32,1152]{2,1,0:T(8,128)(2,1)} %bitcast.38), channel_id=1, replica_groups=mesh['space'=32,'ens'=8] {'ens'}, dimensions={0} | all-to-all | bytes 1179648 | tf_op jit(solution)/shard_map/all_to_all | solution.py:783
  118.0 23.3 %all_to_all.26.share_ref = bf16[32,24,128]{2,1,0:T(8,128)(2,1)S(1)} all-to-all(bf16[32,24,128]{2,1,0:T(8,128)(2,1)S(1)} %shard_map.259), channel_id=1, replica_groups=mesh['space'=32,'ens'=8] {'space'}, dimensions={0} | all-to-all | bytes 393216 | tf_op jit(solution)/shard_map/all_to_all | solution.py:783
  141.3 0.7 shard_map.260
  142.0 4.5 %all-to-all-start.4 = ((f32[8,24,128]{2,1,0:T(8,128)}), f32[8,24,128]{2,1,0:T(8,128)S(1)}, u32[]{:S(2)}, u32[]{:S(2)}) async-start(f32[8,24,128]{2,1,0:T(8,128)} %shard_map.260), calls=%async_computation.4 | async-start | bytes 196608 | tf_op jit(solution)/shard_map/all_to_all | solution.py:783
  146.5 0.8 reshape.100
  147.3 4.5 %all-to-all-done.4.whole_ref = f32[8,24,128]{2,1,0:T(8,128)S(1)} async-done(((f32[8,24,128]{2,1,0:T(8,128)}), f32[8,24,128]{2,1,0:T(8,128)S(1)}, u32[]{:S(2)}, u32[]{:S(2)}) %all-to-all-start.4) | async-done | bytes 98336 | tf_op jit(solution)/shard_map/all_to_all | solution.py:783
  151.8 0.7 shard_map.261
  152.5 0.5 slice_bitcast_fusion.1
  153.0 0.5 slice_bitcast_fusion
  (72 shorter events, 3.8 us)
Async XLA Ops:
  6.0 9.3 %collective-permute-start = (bf16[24,1,96]{2,0,1:T(8,128)(2,1)S(1)}, bf16[24,1,96]{2,0,1:T(8,128)(2,1)S(1)}, u32[]{:S(2)}, u32[]{:S(2)}) collective-permute-start(bf16[24,1,96]{2,0,1:T(8,128)(2,1)S(1)} %slice_select_fusion.2), channel_id=1, source_target_pairs={{0,8},{8,16},{16,24},{24,32},{32,40},{40,48},{48,56},{56,64},{64,7... | collective-permute-start | bytes 13832 | tf_op jit(solution)/shard_map/ppermute | solution.py:752
  6.1 9.3 %collective-permute-start.1 = (bf16[24,1,96]{2,0,1:T(8,128)(2,1)S(1)}, bf16[24,1,96]{2,0,1:T(8,128)(2,1)S(1)}, u32[]{:S(2)}, u32[]{:S(2)}) collective-permute-start(bf16[24,1,96]{2,0,1:T(8,128)(2,1)S(1)} %get-tuple-element.102), channel_id=1, source_target_pairs={{0,248},{8,0},{16,8},{24,16},{32,24},{40,32},{48,40},{56,48},{64,5... | collective-permute-start | bytes 13832 | tf_op jit(solution)/shard_map/ppermute | solution.py:752
  15.5 10.1 %collective-permute-start.2 = (bf16[1,26,96]{2,0,1:T(2,128)(2,1)S(1)}, bf16[1,26,96]{2,0,1:T(2,128)(2,1)S(1)}, u32[]{:S(2)}, u32[]{:S(2)}) collective-permute-start(bf16[1,26,96]{2,0,1:T(2,128)(2,1)S(1)} %get-tuple-element.100), channel_id=1, source_target_pairs={{0,64},{8,72},{16,80},{24,88},{32,96},{40,104},{48,112},{56,120},{... | collective-permute-start | bytes 14984 | tf_op jit(solution)/shard_map/ppermute | solution.py:752
  17.7 7.9 %collective-permute-start.3 = (bf16[1,26,96]{2,0,1:T(2,128)(2,1)S(1)}, bf16[1,26,96]{2,0,1:T(2,128)(2,1)S(1)}, u32[]{:S(2)}, u32[]{:S(2)}) collective-permute-start(bf16[1,26,96]{2,0,1:T(2,128)(2,1)S(1)} %get-tuple-element.101), channel_id=1, source_target_pairs={{0,192},{8,200},{16,208},{24,216},{32,224},{40,232},{48,240},{56,2... | collective-permute-start | bytes 14984 | tf_op jit(solution)/shard_map/ppermute | solution.py:752
  25.7 6.9 %copy-start.12 = (bf16[96]{0:T(256)(128)(2,1)S(1)}, bf16[96]{0:T(256)(128)(2,1)}, u32[]{:S(2)}) copy-start(bf16[96]{0:T(256)(128)(2,1)} %param.31) | copy-start | bytes 580
  25.7 6.9 %copy-start.5 = (bf16[256]{0:T(256)(128)(2,1)S(1)}, bf16[256]{0:T(256)(128)(2,1)}, u32[]{:S(2)}) copy-start(bf16[256]{0:T(256)(128)(2,1)} %param.21) | copy-start | bytes 1540
  25.8 7.1 %copy-start.6 = (bf16[256]{0:T(256)(128)(2,1)S(1)}, bf16[256]{0:T(256)(128)(2,1)}, u32[]{:S(2)}) copy-start(bf16[256]{0:T(256)(128)(2,1)} %param.23) | copy-start | bytes 1540
  25.8 7.3 %copy-start.7 = (bf16[256]{0:T(256)(128)(2,1)S(1)}, bf16[256]{0:T(256)(128)(2,1)}, u32[]{:S(2)}) copy-start(bf16[256]{0:T(256)(128)(2,1)} %param.24) | copy-start | bytes 1540
  25.8 7.5 %copy-start.8 = (bf16[256]{0:T(256)(128)(2,1)S(1)}, bf16[256]{0:T(256)(128)(2,1)}, u32[]{:S(2)}) copy-start(bf16[256]{0:T(256)(128)(2,1)} %param.25) | copy-start | bytes 1540
  25.8 7.7 %copy-start.9 = (bf16[256]{0:T(256)(128)(2,1)S(1)}, bf16[256]{0:T(256)(128)(2,1)}, u32[]{:S(2)}) copy-start(bf16[256]{0:T(256)(128)(2,1)} %param.29) | copy-start | bytes 1540
  25.8 8.1 %copy-start.4 = (bf16[1024]{0:T(1024)(128)(2,1)S(1)}, bf16[1024]{0:T(1024)(128)(2,1)}, u32[]{:S(2)}) copy-start(bf16[1024]{0:T(1024)(128)(2,1)} %param.27) | copy-start | bytes 6148
  26.4 8.4 %collective-permute-start.4 = (bf16[26,5,96]{2,1,0:T(8,128)(2,1)S(1)}, bf16[26,5,96]{2,1,0:T(8,128)(2,1)S(1)}, u32[]{:S(2)}, u32[]{:S(2)}) collective-permute-start(bf16[26,5,96]{2,1,0:T(8,128)(2,1)S(1)} %fusion.4), channel_id=1, source_target_pairs={{0,8},{8,16},{16,24},{24,32},{32,40},{40,48},{48,56},{56,64},{64,7... | collective-permute-start | bytes 74888 | tf_op jit(solution)/shard_map/ppermute | solution.py:752
  26.5 8.3 %collective-permute-start.5 = (bf16[26,5,96]{2,1,0:T(8,128)(2,1)S(1)}, bf16[26,5,96]{2,1,0:T(8,128)(2,1)S(1)}, u32[]{:S(2)}, u32[]{:S(2)}) collective-permute-start(bf16[26,5,96]{2,1,0:T(8,128)(2,1)S(1)} %get-tuple-element.95), channel_id=1, source_target_pairs={{0,248},{8,0},{16,8},{24,16},{32,24},{40,32},{48,40},{56,48},{64,5... | collective-permute-start | bytes 74888 | tf_op jit(solution)/shard_map/ppermute | solution.py:752
  34.9 8.4 %copy-start.1 = (bf16[26,36,96]{2,1,0:T(8,128)(2,1)}, bf16[26,36,96]{2,1,0:T(8,128)(2,1)S(1)}, u32[]{:S(2)}) copy-start(bf16[26,36,96]{2,1,0:T(8,128)(2,1)S(1)} %pad_maximum_fusion.band_ref) | copy-start | bytes 539140
  34.9 17.8 %collective-permute-start.6 = (bf16[5,36,96]{2,1,0:T(8,128)(2,1)S(1)}, bf16[5,36,96]{2,1,0:T(8,128)(2,1)S(1)}, u32[]{:S(2)}, u32[]{:S(2)}) collective-permute-start(bf16[5,36,96]{2,1,0:T(8,128)(2,1)S(1)} %get-tuple-element.90), channel_id=1, source_target_pairs={{0,64},{8,72},{16,80},{24,88},{32,96},{40,104},{48,112},{56,120},{... | collective-permute-start | bytes 103688 | tf_op jit(solution)/shard_map/ppermute | solution.py:752
  37.8 15.0 %collective-permute-start.7 = (bf16[5,36,96]{2,1,0:T(8,128)(2,1)S(1)}, bf16[5,36,96]{2,1,0:T(8,128)(2,1)S(1)}, u32[]{:S(2)}, u32[]{:S(2)}) collective-permute-start(bf16[5,36,96]{2,1,0:T(8,128)(2,1)S(1)} %get-tuple-element.89), channel_id=1, source_target_pairs={{0,192},{8,200},{16,208},{24,216},{32,224},{40,232},{48,240},{56,2... | collective-permute-start | bytes 103688 | tf_op jit(solution)/shard_map/ppermute | solution.py:752
  52.8 0.6 copy-start.10
  52.8 0.6 copy-start.11
  61.1 7.3 %copy-start.3 = (bf16[24,2304]{1,0:T(8,128)(2,1)S(1)}, bf16[24,2304]{1,0:T(8,128)(2,1)}, u32[]{:S(2)}) copy-start(bf16[24,2304]{1,0:T(8,128)(2,1)} %param.18) | copy-start | bytes 331780
  61.2 15.4 %all-to-all-start = ((bf16[8,144,384]{2,1,0:T(8,128)(2,1)}), bf16[8,144,384]{2,1,0:T(8,128)(2,1)S(1)}, u32[]{:S(2)}, u32[]{:S(2)}) async-start(bf16[8,144,384]{2,1,0:T(8,128)(2,1)} %get-tuple-element.64), calls=%async_computation | async-start | bytes 1769472 | tf_op jit(solution)/shard_map/all_to_all | solution.py:783
  76.6 0.9 copy-start
  86.3 17.7 %all-to-all-start.1 = ((bf16[8,32,16,128]{3,2,1,0:T(8,128)(2,1)}), bf16[8,32,16,128]{3,2,1,0:T(8,128)(2,1)S(1)}, u32[]{:S(2)}, u32[]{:S(2)}) async-start(bf16[8,32,16,128]{3,2,1,0:T(8,128)(2,1)} %get-tuple-element.71), calls=%async_computation.1 | async-start | bytes 2097152 | tf_op jit(solution)/shard_map/all_to_all | solution.py:783
  117.7 28.8 %copy-start.2 = (f32[576,96]{1,0:T(8,128)S(1)}, f32[576,96]{1,0:T(8,128)}, u32[]{:S(2)}) copy-start(f32[576,96]{1,0:T(8,128)} %get-tuple-element.63) | copy-start | bytes 663556
  142.0 9.8 %all-to-all-start.4 = ((f32[8,24,128]{2,1,0:T(8,128)}), f32[8,24,128]{2,1,0:T(8,128)S(1)}, u32[]{:S(2)}, u32[]{:S(2)}) async-start(f32[8,24,128]{2,1,0:T(8,128)} %shard_map.260), calls=%async_computation.4 | async-start | bytes 196608 | tf_op jit(solution)/shard_map/all_to_all | solution.py:783

commit v4 on v3

--- a/solution.py
+++ b/solution.py
@@ -133,11 +133,11 @@
 
 
 def middle_forward_kernel(
-    seam_turns_ref, band_ref, w_in_ref, w_depth_low_ref, vectors_ref, w_up_ref, w_down_ref, head_ref,
+    ready, seam_turns_ref, wide_ref, w_in_ref, w_depth_ref, w_up_ref, w_down_ref, head_ref,
     patches_out, stem_out, normed_out, inverse_out, scaled_out, slope_out, active_out, hidden_out,
-    field_ref, w_depth_ref,
+    field_ref,
     patches_ref, stem_ref, normed_ref, inverse_ref, scaled_ref, slope_ref, active_ref, hidden_ref,
-    wide_ref, stage_ref, w_in_wide_ref, sem,
+    stage_ref, w_in_wide_ref, sem,
 ):
     pairs = ((normed_ref, normed_out), (inverse_ref, inverse_out), (scaled_ref, scaled_out),
              (slope_ref, slope_out), (active_ref, active_out), (hidden_ref, hidden_out))
@@ -145,10 +145,9 @@
     send_patches = pltpu.make_async_copy(patches_ref, patches_out.at[96:864], sem.at[0])
     send_stem = pltpu.make_async_copy(stem_ref, stem_out.at[:, 3:27], sem.at[1])
     turn_at, _ = turn_reader(seam_turns_ref)
-    w_depth_ref[...] = w_depth_low_ref[...].astype(F32)
+    vectors_ref = w_depth_ref.at[VECTORS : VECTORS + 16]
+    ready()
     widen_stem_weight(w_in_ref, w_in_wide_ref)
-    wide_ref[...] = jnp.zeros_like(wide_ref)
-    wide_ref[:, 0:36, 0:96] = band_ref[...].astype(F32)
     turns = (turn_at(0), None, (4 - turn_at(1)) & 3)
     pieces = [(turn, 0, 0, SIDE) + columns for turn, columns in zip(turns, BANDS)]
     gather_patches(pieces, wide_ref, stage_ref, patches_ref)
@@ -182,18 +181,17 @@
     lax.fori_loop(0, 4, mix, 0)
     for send in sends:
         send.start()
-    for send in sends + [send_patches, send_stem]:
-        send.wait()
+    return sends + [send_patches, send_stem]
 
 
 def rim_forward_kernel(
-    seam_turns_ref, north_ref, south_ref, w_in_ref, w_depth_ref, vectors_ref, w_up_ref, w_down_ref,
+    ready, seam_turns_ref, wide_ref, w_in_ref, w_depth_ref, w_up_ref, w_down_ref,
     head_ref, middle_field_ref,
     patches_in, stem_in, normed_in, inverse_in, scaled_in, slope_in, active_in, hidden_in,
     patches_out, stem_out, normed_out, inverse_out, scaled_out, slope_out, active_out, hidden_out,
     field_ref, tight_ref, sent_ref,
     patches_ref, stem_ref, normed_ref, inverse_ref, scaled_ref, slope_ref, active_ref, hidden_ref,
-    wide_ref, stage_ref, w_in_wide_ref, sem,
+    stage_ref, w_in_wide_ref, sem,
 ):
     fetches = [
         pltpu.make_async_copy(stem_in.at[:, 3:10], stem_ref.at[:, 3:10], sem.at[0, 0]),
@@ -214,10 +212,9 @@
         pltpu.make_async_copy(stem_ref.at[:, 17:20], stem_out.at[:, 27:30], sem.at[2, 1]),
     ]
     turn_at, across = turn_reader(seam_turns_ref)
+    vectors_ref = w_depth_ref.at[VECTORS : VECTORS + 16]
+    ready()
     widen_stem_weight(w_in_ref, w_in_wide_ref)
-    wide_ref[...] = jnp.zeros_like(wide_ref)
-    wide_ref[0:5, 0:36, 0:96] = north_ref[...].astype(F32)
-    wide_ref[5:10, 0:36, 0:96] = south_ref[...].astype(F32)
     north = (turn_at(-across), None, (4 - turn_at(1 - across)) & 3)
     south = (turn_at(across), None, (4 - turn_at(across + 1)) & 3)
     pieces = [(turn, 0, 0, 3) + columns for turn, columns in zip(north, BANDS)]
@@ -262,12 +259,12 @@
     sent = tight_ref[...].astype(BF16)
     for member in range(sent_ref.shape[0]):
         sent_ref[member] = sent
-    for send in sends + early_sends:
-        send.wait()
+    return sends + early_sends
 
 
 def mixer_backward_kernel(
     coefficient,
+    ready,
     every_ref,
     own_ref,
     target_ref,
@@ -307,6 +304,7 @@
         fetch.start()
     send_hidden = pltpu.make_async_copy(hidden_grad_ref, hidden_grad_out, out_sem.at[0])
     send_scaled = pltpu.make_async_copy(scaled_grad_ref, scaled_grad_out, out_sem.at[1])
+    ready()
     members = every_ref.shape[0]
     own = own_ref[...]
     own_sent = own.astype(BF16).astype(F32)
@@ -387,15 +385,14 @@
     small_ref[0:1, :] = grad_b_down
     small_ref[1:5, :] = two_part(spread, fold)[0:4]
     small_ref[5:6, :] = two_part(b_out, place)[0:1]
-    send_hidden.wait()
-    send_scaled.wait()
+    return [send_hidden, send_scaled]
 
 
 def depth_backward_kernel(
+    ready,
     scaled_grad_ref,
     normed_ref,
     inverse_ref,
-    vectors_ref,
     hidden_grad_in,
     stem_in,
     w_depth_ref,
@@ -423,6 +420,8 @@
     deep_ref[...] = jnp.zeros_like(deep_ref)
     small_ref[...] = jnp.zeros_like(small_ref)
     sums_ref[...] = jnp.zeros_like(sums_ref)
+    vectors_ref = w_depth_ref.at[VECTORS : VECTORS + 16]
+    ready()
 
     def unnormalise(block, carry):
         at = pl.ds(pl.multiple_of(block * 96, 96), 96)
@@ -518,7 +517,8 @@
     late_ref[...] = tight_ref[...].astype(BF16)
 
 
-def combine_kernel(early_ref, late_ref, share_ref, rows_ref):
+def combine_kernel(ready, early_ref, late_ref, share_ref, rows_ref):
+    ready()
     members = early_ref.shape[0]
     early = early_ref[0].astype(F32)
     late = late_ref[0].astype(F32)
@@ -534,7 +534,8 @@
     share_ref[...] = rows_ref[...].astype(BF16)
 
 
-def total_kernel(share_ref, copies_ref):
+def total_kernel(ready, share_ref, copies_ref):
+    ready()
     total = share_ref[0].astype(F32)
     for tile in range(1, share_ref.shape[0]):
         total = total + share_ref[tile].astype(F32)
@@ -543,8 +544,9 @@
 
 
 def unpack_kernel(
-    whole_ref, w_in_ref, w_depth_ref, w_up_ref, w_down_ref, w_out_ref, small_ref, b_up_ref
+    ready, whole_ref, w_in_ref, w_depth_ref, w_up_ref, w_down_ref, w_out_ref, small_ref, b_up_ref
 ):
+    ready()
     parts = whole_ref.shape[0]
     for part in range(parts):
         for row in range(7):
@@ -566,23 +568,61 @@
 
 
 def call(kernel, outs, scratch, *operands, spaces=None, vmem=VMEM_BYTES, flops=0, aliases=None):
-    kinds = {"v": pltpu.VMEM, "s": pltpu.SMEM, "a": pl.ANY}
     spaces = spaces or "v" * len(operands)
+    count_in, count_out = len(operands), len(outs)
+    copied_in = [k for k in range(count_in) if spaces[k] == "v"]
+    copied_out = [k for k in range(count_out) if outs[k][2] == "v"]
+    buffers = [pltpu.VMEM(operands[k].shape, operands[k].dtype) for k in copied_in]
+    buffers += [pltpu.VMEM(outs[k][0], outs[k][1]) for k in copied_out]
+    own = [x if not isinstance(x, tuple) else pltpu.VMEM(*x) for x in scratch]
+    semaphores = pltpu.SemaphoreType.DMA((len(buffers),))
+
+    def wrapped(*refs):
+        ins, results = list(refs[:count_in]), list(refs[count_in : count_in + count_out])
+        rest = refs[count_in + count_out :]
+        held, sem, working = rest[: len(buffers)], rest[len(buffers)], rest[len(buffers) + 1 :]
+        fetches, sends = [], []
+        for place, k in enumerate(copied_in):
+            fetches.append(pltpu.make_async_copy(ins[k], held[place], sem.at[place]))
+            ins[k] = held[place]
+        for place, k in enumerate(copied_out, len(copied_in)):
+            sends.append(pltpu.make_async_copy(held[place], results[k], sem.at[place]))
+            results[k] = held[place]
+        for fetch in fetches:
+            fetch.start()
+
+        def ready():
+            for fetch in fetches:
+                fetch.wait()
+
+        started = kernel(ready, *ins, *results, *working) or []
+        for send in sends:
+            send.start()
+        for send in list(started) + sends:
+            send.wait()
+
+    place_of = {"s": pltpu.SMEM, "a": pl.ANY, "v": pl.ANY}
     return pl.pallas_call(
-        kernel,
+        wrapped,
         out_shape=[jax.ShapeDtypeStruct(shape, kind) for shape, kind, _ in outs],
-        in_specs=[pl.BlockSpec(memory_space=kinds[letter]) for letter in spaces],
-        out_specs=[pl.BlockSpec(memory_space=kinds[letter]) for _, _, letter in outs],
-        scratch_shapes=[x if not isinstance(x, tuple) else pltpu.VMEM(*x) for x in scratch],
+        in_specs=[pl.BlockSpec(memory_space=place_of[letter]) for letter in spaces],
+        out_specs=[pl.BlockSpec(memory_space=pl.ANY)] * count_out,
+        scratch_shapes=buffers + [semaphores] + own,
         input_output_aliases=aliases or {},
         compiler_params=pltpu.CompilerParams(vmem_limit_bytes=vmem),
         cost_estimate=pl.CostEstimate(flops=flops, bytes_accessed=8_000_000, transcendentals=0),
     )(*operands)
 
 
-def stack_vectors(b_in, b_depth, gain, shift, b_down, head_bias, b_up):
+VECTORS = 56
+
+
+def stack_params(w_depth, b_in, b_depth, gain, shift, b_down, head_bias, b_up):
     rows = [b_in, b_depth, gain, shift, b_down, jnp.pad(head_bias, (0, 160)), b_up]
-    return jnp.concatenate(rows).astype(F32).reshape(10, 256)
+    vectors = jnp.concatenate(rows).reshape(10, 256)
+    return jnp.concatenate(
+        [jnp.pad(w_depth, ((0, VECTORS - 49), (0, 0))), jnp.pad(vectors, ((0, 6), (0, 0)))]
+    ).astype(F32)
 
 
 KEPT = (
@@ -597,7 +637,7 @@
 )
 
 
-def forward_scratch(patch_rows, stem_rows, cells, wide_rows, semaphores):
+def forward_scratch(patch_rows, stem_rows, cells, semaphores):
     return [
         ((patch_rows, 1152), BF16),
         ((2, stem_rows, 32, LANE), F32),
@@ -607,37 +647,40 @@
         ((cells, 1024), BF16),
         ((cells, 1024), BF16),
         ((cells, 256), BF16),
-        ((wide_rows, 40, LANE), F32),
         ((patch_rows // 32, 32, LANE), F32),
         ((1152, 256), BF16),
         pltpu.SemaphoreType.DMA(semaphores),
     ]
 
 
-def run_middle_forward(seam_turns, band, w_in, w_depth, vectors, w_up, w_down, head):
+def widened(source):
+    return jnp.pad(source, ((0, 0), (0, 4), (0, 32))).astype(F32)
+
+
+def run_middle_forward(seam_turns, band, w_in, params, w_up, w_down, head):
     outs = call(
         middle_forward_kernel,
         [(shape, kind, "a") for shape, kind in KEPT]
-        + [((384, 96), F32, "v"), ((49, 256), F32, "v")],
-        forward_scratch(768, SIDE, 384, 26, (8,)),
-        seam_turns, band, w_in, w_depth, vectors, w_up, w_down, head,
-        spaces="svvvvvvv",
+        + [((384, 96), F32, "v")],
+        forward_scratch(768, SIDE, 384, (8,)),
+        seam_turns, widened(band), w_in, params, w_up, w_down, head,
+        spaces="svvvvvv",
         flops=10_000_000_000,
     )
-    return outs[:8], outs[8], outs[9]
+    return outs[:8], outs[8]
 
 
 def run_rim_forward(
-    seam_turns, north, south, w_in, w_depth, vectors, w_up, w_down, head, middle_field, kept, members
+    seam_turns, north, south, w_in, params, w_up, w_down, head, middle_field, kept, members
 ):
     outs = call(
         rim_forward_kernel,
         [(shape, kind, "a") for shape, kind in KEPT]
         + [((CELLS, 96), F32, "v"), ((144, 384), F32, "v"), ((members, 144, 384), BF16, "v")],
-        forward_scratch(192, 20, 192, 10, (3, 8)),
-        seam_turns, north, south, w_in, w_depth, vectors, w_up, w_down, head, middle_field, *kept,
-        spaces="svvvvvvvvvaaaaaaaa",
-        aliases={10 + k: k for k in range(8)},
+        forward_scratch(192, 20, 192, (3, 8)),
+        seam_turns, widened(jnp.concatenate([north, south])), w_in, params, w_up, w_down, head, middle_field, *kept,
+        spaces="svvvvvvvaaaaaaaa",
+        aliases={8 + k: k for k in range(8)},
         flops=5_000_000_000,
     )
     return outs[:8], outs[8], outs[9], outs[10]
@@ -690,7 +733,7 @@
 
 
 def run_depth_backward(
-    scaled_grad, normed, inverse, vectors, hidden_grad, stem, w_depth, patches, early_small, out_part
+    scaled_grad, normed, inverse, hidden_grad, stem, params, patches, early_small, out_part
 ):
     column = jnp.arange(256)
     order = (column[:, None] == (8 * (column % 32) + column // 32)[None, :]).astype(BF16)
@@ -712,15 +755,14 @@
         scaled_grad,
         normed,
         inverse,
-        vectors,
         hidden_grad,
         stem,
-        w_depth,
+        params,
         patches,
         order,
         early_small,
         out_part,
-        spaces="vvvvaavavvv",
+        spaces="vvvaavavvv",
         flops=12_000_000_000,
     )[0]
 
@@ -816,13 +858,11 @@
     ).astype(BF16).reshape(SIDE, SIDE, 96)
     near = jnp.concatenate(seam_strips(source, my_turn, next_turn, 1, row_tiles), axis=0)
     north, band, south = seam_strips(near, my_turn, next_turn, 5, row_tiles)
-    vectors = stack_vectors(b_in, b_depth, norm_gain, norm_shift, b_down, head_bias, b_up)
+    params = stack_params(w_depth, b_in, b_depth, norm_gain, norm_shift, b_down, head_bias, b_up)
     head = head_weight.T
-    kept, middle_field, w_depth_wide = run_middle_forward(
-        seam_turns, band, w_in, w_depth, vectors, w_up, w_down, head
-    )
+    kept, middle_field = run_middle_forward(seam_turns, band, w_in, params, w_up, w_down, head)
     kept, field, tight, sent = run_rim_forward(
-        seam_turns, north, south, w_in, w_depth_wide, vectors, w_up, w_down, head, middle_field, kept, members
+        seam_turns, north, south, w_in, params, w_up, w_down, head, middle_field, kept, members
     )
     patches, stem, normed, inverse, scaled, slope, active, hidden = kept
     sent, verifying_analysis, field_again = lax.optimization_barrier((sent, verifying_analysis, field))
@@ -834,7 +874,7 @@
         every, tight, target, (hidden, active, slope, scaled), head, w_down, w_up, coefficient
     )
     late = run_depth_backward(
-        scaled_grad, normed, inverse, vectors, hidden_grad, stem, w_depth_wide, patches, early_small, out_part
+        scaled_grad, normed, inverse, hidden_grad, stem, params, patches, early_small, out_part
     )
     early_parts, late = lax.optimization_barrier((swap(early, "ens"), late))
     late_parts = swap(late.reshape(8, 32, 1152), "ens")

time: 154 us -> 156 us (1.013)
  other arithmetic: 2.69 us -> 4.91 us
    convert_element_type x0 -> x3, other arithmetic: none -> 2.21 us  [the longest x2 1.57 us: widened(): return jnp.pad(source, ((0, 0), (0, 4), (0, 32))).astype(F32)]
  transfers between devices with their start and end apart: 11 -> 11, of which waited for: 5 -> 7; matrix products, arithmetic and copies ran while one was open for 3% -> 3% of each run, Pallas kernels for 15% -> 15%
where the time goes in v4:
time: 156 us; the launch traced here: 155 us
  starting transfers between devices  46.2 us (30%)
  Pallas kernels  41.5 us (27%)
  blocking collectives  37.2 us (24%)
  waiting for transfers between devices  14.1 us (9%)
  local copies, waits for them, and re-layouts  7.61 us (5%)
  other arithmetic  4.91 us (3%)
  between operations  3.61 us (2%)
    pallas_call x7, Pallas kernels, call(): pl.pallas_call(wrapped, out_shape=[jax.ShapeDtypeStruct(shape, kind) for...  41.5 us
    all_to_all x2, blocking collectives, swap(): return lax.all_to_all(value, axis, 0, 0, tiled=True)  37.2 us
    ppermute x8, starting transfers between devices, shifted(): lax.ppermute(value, axis, [(i, (i + by) % peers) for i in range(peers)])  31.1 us
    all_to_all x3, starting transfers between devices, swap(): return lax.all_to_all(value, axis, 0, 0, tiled=True)  15.1 us
    all_to_all x3, waiting for transfers between devices, swap(): return lax.all_to_all(value, axis, 0, 0, tiled=True)  11.5 us
  transfers between devices with their start and end apart: 11, of which 7 were waited for; matrix products, arithmetic and copies ran while one was open for 3% of the time, Pallas kernels for 15%

profile of v4, /device:TPU:2, one launch (start us, length us, event | category | flops | bytes accessed | tf_op | source)
XLA Modules:
  0.0 155.2 jit_solution(14500443222092860516)
XLA Ops:
  0.7 1.3 fusion.28
  2.7 1.0 fusion.1
  6.2 8.0 %collective-permute-start.1 = (bf16[24,1,96]{2,0,1:T(8,128)(2,1)S(1)}, bf16[24,1,96]{2,0,1:T(8,128)(2,1)S(1)}, u32[]{:S(2)}, u32[]{:S(2)}) collective-permute-start(bf16[24,1,96]{2,0,1:T(8,128)(2,1)S(1)} %get-tuple-element.100), channel_id=1, source_target_pairs={{0,248},{8,0},{16,8},{24,16},{32,24},{40,32},{48,40},{56,48},{64,5... | collective-permute-start | bytes 13832 | tf_op jit(solution)/shard_map/ppermute | solution.py:794
  14.2 1.2 collective-permute-done
  15.6 2.2 %collective-permute-start.2 = (bf16[1,26,96]{2,0,1:T(2,128)(2,1)S(1)}, bf16[1,26,96]{2,0,1:T(2,128)(2,1)S(1)}, u32[]{:S(2)}, u32[]{:S(2)}) collective-permute-start(bf16[1,26,96]{2,0,1:T(2,128)(2,1)S(1)} %get-tuple-element.98), channel_id=1, source_target_pairs={{0,64},{8,72},{16,80},{24,88},{32,96},{40,104},{48,112},{56,120},{... | collective-permute-start | bytes 14984 | tf_op jit(solution)/shard_map/ppermute | solution.py:794
  17.8 6.2 %collective-permute-start.3 = (bf16[1,26,96]{2,0,1:T(2,128)(2,1)S(1)}, bf16[1,26,96]{2,0,1:T(2,128)(2,1)S(1)}, u32[]{:S(2)}, u32[]{:S(2)}) collective-permute-start(bf16[1,26,96]{2,0,1:T(2,128)(2,1)S(1)} %get-tuple-element.99), channel_id=1, source_target_pairs={{0,192},{8,200},{16,208},{24,216},{32,224},{40,232},{48,240},{56,2... | collective-permute-start | bytes 14984 | tf_op jit(solution)/shard_map/ppermute | solution.py:794
  26.5 6.1 %collective-permute-start.5 = (bf16[26,5,96]{2,1,0:T(8,128)(2,1)S(1)}, bf16[26,5,96]{2,1,0:T(8,128)(2,1)S(1)}, u32[]{:S(2)}, u32[]{:S(2)}) collective-permute-start(bf16[26,5,96]{2,1,0:T(8,128)(2,1)S(1)} %get-tuple-element.93), channel_id=1, source_target_pairs={{0,248},{8,0},{16,8},{24,16},{32,24},{40,32},{48,40},{56,48},{64,5... | collective-permute-start | bytes 74888 | tf_op jit(solution)/shard_map/ppermute | solution.py:794
  32.6 0.6 fusion.15.refs_3_.refs_5_
  33.2 1.1 collective-permute-done.4
  34.5 0.8 pad_convert_fusion.refs_1_
  35.4 2.9 %collective-permute-start.6 = (bf16[5,36,96]{2,1,0:T(8,128)(2,1)S(1)}, bf16[5,36,96]{2,1,0:T(8,128)(2,1)S(1)}, u32[]{:S(2)}, u32[]{:S(2)}) collective-permute-start(bf16[5,36,96]{2,1,0:T(8,128)(2,1)S(1)} %get-tuple-element.87), channel_id=1, source_target_pairs={{0,64},{8,72},{16,80},{24,88},{32,96},{40,104},{48,112},{56,120},{... | collective-permute-start | bytes 103688 | tf_op jit(solution)/shard_map/ppermute | solution.py:794
  38.3 5.5 %collective-permute-start.7 = (bf16[5,36,96]{2,1,0:T(8,128)(2,1)S(1)}, bf16[5,36,96]{2,1,0:T(8,128)(2,1)S(1)}, u32[]{:S(2)}, u32[]{:S(2)}) collective-permute-start(bf16[5,36,96]{2,1,0:T(8,128)(2,1)S(1)} %get-tuple-element.88), channel_id=1, source_target_pairs={{0,192},{8,200},{16,208},{24,216},{32,224},{40,232},{48,240},{56,2... | collective-permute-start | bytes 103688 | tf_op jit(solution)/shard_map/ppermute | solution.py:794
  43.8 9.4 %shard_map.255 = (bf16[960,1152]{1,0:T(8,128)(2,1)}, f32[2,30,32,128]{3,2,1,0:T(8,128)}, f32[576,256]{1,0:T(8,128)}, f32[576,128]{1,0:T(8,128)}, bf16[576,256]{1...) custom-call(s32[32]{0:T(128)} %refs_0_.3, ...), custom_call_target="tpu_custom_call" | custom-call | flops 10000000000 | bytes 8000000 | tf_op jit(solution)/shard_map/pallas_call | solution.py:605
  53.2 0.7 fusion.8.refs_1_
  53.9 7.2 %shard_map.256 = (bf16[960,1152]{1,0:T(8,128)(2,1)}, f32[2,30,32,128]{3,2,1,0:T(8,128)}, f32[576,256]{1,0:T(8,128)}, f32[576,128]{1,0:T(8,128)}, bf16[576,256]{1...) custom-call(s32[32]{0:T(128)} %refs_0_.3, ...), custom_call_target="tpu_custom_call", output_to_operand_aliasing={{0}: (8, {}), {1}: (9, {}), {2}: (10, {}), {3}: (11, {}), {... | custom-call | flops 5000000000 | bytes 8000000 | tf_op jit(solution)/shard_map/pallas_call | solution.py:605
  61.2 6.0 %all-to-all-start = ((bf16[8,144,384]{2,1,0:T(8,128)(2,1)}), bf16[8,144,384]{2,1,0:T(8,128)(2,1)S(1)}, u32[]{:S(2)}, u32[]{:S(2)}) async-start(bf16[8,144,384]{2,1,0:T(8,128)(2,1)} %get-tuple-element.62), calls=%async_computation | async-start | bytes 1769472 | tf_op jit(solution)/shard_map/all_to_all | solution.py:825
  67.2 0.6 fusion.11.refs_5_
  67.8 0.7 fusion.refs_7_
  68.8 0.8 reshape.102.refs_2_
  69.5 7.1 %all-to-all-done.refs_0_ = bf16[8,144,384]{2,1,0:T(8,128)(2,1)S(1)} async-done(((bf16[8,144,384]{2,1,0:T(8,128)(2,1)}), bf16[8,144,384]{2,1,0:T(8,128)(2,1)S(1)}, u32[]{:S(2)}, u32[]{:S(2)}) %all-to-all-start) | async-done | bytes 884768 | tf_op jit(solution)/shard_map/all_to_all | solution.py:825
  76.6 0.9 copy-done
  77.5 9.1 %shard_map.257 = (bf16[8,32,16,128]{3,2,1,0:T(8,128)(2,1)}, f32[96,256]{1,0:T(8,128)}, f32[576,256]{1,0:T(8,128)}, f32[576,256]{1,0:T(8,128)}, f32[8,256]{1,0:T(8,128)}) custom-call(bf16[8,144,384]{2,1,0:T(8,128)(2,1)} %copy-done, f32[144,384]{1,0:T(8,128)} %get-tuple-element.63.refs_1_, bf16[144,384]{1,0:T(8,128)(2,1)} %reshape.102.refs_2_, ...), custom_call_target="tpu_custom_call" | custom-call | flops 12000000000 | bytes 8000000 | tf_op jit(solution)/shard_map/pallas_call | solution.py:605
  86.6 4.6 %all-to-all-start.1 = ((bf16[8,32,16,128]{3,2,1,0:T(8,128)(2,1)}), bf16[8,32,16,128]{3,2,1,0:T(8,128)(2,1)S(1)}, u32[]{:S(2)}, u32[]{:S(2)}) async-start(bf16[8,32,16,128]{3,2,1,0:T(8,128)(2,1)} %get-tuple-element.69), calls=%async_computation.1 | async-start | bytes 2097152 | tf_op jit(solution)/shard_map/all_to_all | solution.py:825
  91.3 13.2 %shard_map.258 = bf16[256,1152]{1,0:T(8,128)(2,1)} custom-call(f32[576,256]{1,0:T(8,128)} %get-tuple-element.70.refs_0_, f32[576,256]{1,0:T(8,128)} %get-tuple-element.71.refs_1_, f32[576,128]{1,0:T(8,128)} %get-tuple-element.72.refs_2_, f32[576,256]{1,0:T(8,128)} %get-tuple-element.73.refs_3_, f32[2,30,32,128]{3,2,1,0:T(8,128)} %get-tuple-element.74.refs_4_, ...), custom_call_target="tpu_custom_call" | custom-call | flops 12000000000 | bytes 8000000 | tf_op jit(solution)/shard_map/pallas_call | solution.py:605
  104.5 13.6 %all_to_all.25.refs_1_ = bf16[8,32,1152]{2,1,0:T(8,128)(2,1)S(1)} all-to-all(bf16[8,32,1152]{2,1,0:T(8,128)(2,1)} %bitcast.38), channel_id=1, replica_groups=mesh['space'=32,'ens'=8] {'ens'}, dimensions={0} | all-to-all | bytes 1179648 | tf_op jit(solution)/shard_map/all_to_all | solution.py:825
  118.1 0.8 shard_map.259
  119.0 23.6 %all_to_all.26.refs_0_ = bf16[32,24,128]{2,1,0:T(8,128)(2,1)S(1)} all-to-all(bf16[32,24,128]{2,1,0:T(8,128)(2,1)S(1)} %shard_map.259), channel_id=1, replica_groups=mesh['space'=32,'ens'=8] {'space'}, dimensions={0} | all-to-all | bytes 393216 | tf_op jit(solution)/shard_map/all_to_all | solution.py:825
  142.5 0.9 shard_map.260
  143.4 4.5 %all-to-all-start.4 = ((f32[8,24,128]{2,1,0:T(8,128)}), f32[8,24,128]{2,1,0:T(8,128)S(1)}, u32[]{:S(2)}, u32[]{:S(2)}) async-start(f32[8,24,128]{2,1,0:T(8,128)} %shard_map.260), calls=%async_computation.4 | async-start | bytes 196608 | tf_op jit(solution)/shard_map/all_to_all | solution.py:825
  148.0 0.8 reshape.100
  148.8 4.5 %all-to-all-done.4.refs_0_ = f32[8,24,128]{2,1,0:T(8,128)S(1)} async-done(((f32[8,24,128]{2,1,0:T(8,128)}), f32[8,24,128]{2,1,0:T(8,128)S(1)}, u32[]{:S(2)}, u32[]{:S(2)}) %all-to-all-start.4) | async-done | bytes 98336 | tf_op jit(solution)/shard_map/all_to_all | solution.py:825
  153.2 0.9 shard_map.261
  (71 shorter events, 4.6 us)
Async XLA Ops:
  0.6 23.4 %copy-start.10 = (bf16[96]{0:T(256)(128)(2,1)S(1)}, bf16[96]{0:T(256)(128)(2,1)}, u32[]{:S(2)}) copy-start(bf16[96]{0:T(256)(128)(2,1)} %param.31) | copy-start | bytes 580
  0.7 23.4 %copy-start.5 = (bf16[256]{0:T(256)(128)(2,1)S(1)}, bf16[256]{0:T(256)(128)(2,1)}, u32[]{:S(2)}) copy-start(bf16[256]{0:T(256)(128)(2,1)} %param.21) | copy-start | bytes 1540
  0.7 23.6 %copy-start.6 = (bf16[256]{0:T(256)(128)(2,1)S(1)}, bf16[256]{0:T(256)(128)(2,1)}, u32[]{:S(2)}) copy-start(bf16[256]{0:T(256)(128)(2,1)} %param.23) | copy-start | bytes 1540
  0.7 23.8 %copy-start.7 = (bf16[256]{0:T(256)(128)(2,1)S(1)}, bf16[256]{0:T(256)(128)(2,1)}, u32[]{:S(2)}) copy-start(bf16[256]{0:T(256)(128)(2,1)} %param.24) | copy-start | bytes 1540
  0.7 24.0 %copy-start.8 = (bf16[256]{0:T(256)(128)(2,1)S(1)}, bf16[256]{0:T(256)(128)(2,1)}, u32[]{:S(2)}) copy-start(bf16[256]{0:T(256)(128)(2,1)} %param.25) | copy-start | bytes 1540
  0.7 24.2 %copy-start.9 = (bf16[256]{0:T(256)(128)(2,1)S(1)}, bf16[256]{0:T(256)(128)(2,1)}, u32[]{:S(2)}) copy-start(bf16[256]{0:T(256)(128)(2,1)} %param.29) | copy-start | bytes 1540
  0.7 24.6 %copy-start.4 = (bf16[1024]{0:T(1024)(128)(2,1)S(1)}, bf16[1024]{0:T(1024)(128)(2,1)}, u32[]{:S(2)}) copy-start(bf16[1024]{0:T(1024)(128)(2,1)} %param.27) | copy-start | bytes 6148
  6.1 9.3 %collective-permute-start = (bf16[24,1,96]{2,0,1:T(8,128)(2,1)S(1)}, bf16[24,1,96]{2,0,1:T(8,128)(2,1)S(1)}, u32[]{:S(2)}, u32[]{:S(2)}) collective-permute-start(bf16[24,1,96]{2,0,1:T(8,128)(2,1)S(1)} %slice_select_fusion.2), channel_id=1, source_target_pairs={{0,8},{8,16},{16,24},{24,32},{32,40},{40,48},{48,56},{56,64},{64,7... | collective-permute-start | bytes 13832 | tf_op jit(solution)/shard_map/ppermute | solution.py:794
  6.2 9.3 %collective-permute-start.1 = (bf16[24,1,96]{2,0,1:T(8,128)(2,1)S(1)}, bf16[24,1,96]{2,0,1:T(8,128)(2,1)S(1)}, u32[]{:S(2)}, u32[]{:S(2)}) collective-permute-start(bf16[24,1,96]{2,0,1:T(8,128)(2,1)S(1)} %get-tuple-element.100), channel_id=1, source_target_pairs={{0,248},{8,0},{16,8},{24,16},{32,24},{40,32},{48,40},{56,48},{64,5... | collective-permute-start | bytes 13832 | tf_op jit(solution)/shard_map/ppermute | solution.py:794
  15.6 10.1 %collective-permute-start.2 = (bf16[1,26,96]{2,0,1:T(2,128)(2,1)S(1)}, bf16[1,26,96]{2,0,1:T(2,128)(2,1)S(1)}, u32[]{:S(2)}, u32[]{:S(2)}) collective-permute-start(bf16[1,26,96]{2,0,1:T(2,128)(2,1)S(1)} %get-tuple-element.98), channel_id=1, source_target_pairs={{0,64},{8,72},{16,80},{24,88},{32,96},{40,104},{48,112},{56,120},{... | collective-permute-start | bytes 14984 | tf_op jit(solution)/shard_map/ppermute | solution.py:794
  17.8 7.9 %collective-permute-start.3 = (bf16[1,26,96]{2,0,1:T(2,128)(2,1)S(1)}, bf16[1,26,96]{2,0,1:T(2,128)(2,1)S(1)}, u32[]{:S(2)}, u32[]{:S(2)}) collective-permute-start(bf16[1,26,96]{2,0,1:T(2,128)(2,1)S(1)} %get-tuple-element.99), channel_id=1, source_target_pairs={{0,192},{8,200},{16,208},{24,216},{32,224},{40,232},{48,240},{56,2... | collective-permute-start | bytes 14984 | tf_op jit(solution)/shard_map/ppermute | solution.py:794
  25.8 6.8 %copy-start.3 = (bf16[49,256]{1,0:T(8,128)(2,1)S(1)}, bf16[49,256]{1,0:T(8,128)(2,1)}, u32[]{:S(2)}) copy-start(bf16[49,256]{1,0:T(8,128)(2,1)} %param.22) | copy-start | bytes 75268
  26.4 7.9 %collective-permute-start.4 = (bf16[26,5,96]{2,1,0:T(8,128)(2,1)S(1)}, bf16[26,5,96]{2,1,0:T(8,128)(2,1)S(1)}, u32[]{:S(2)}, u32[]{:S(2)}) collective-permute-start(bf16[26,5,96]{2,1,0:T(8,128)(2,1)S(1)} %fusion.13), channel_id=1, source_target_pairs={{0,8},{8,16},{16,24},{24,32},{32,40},{40,48},{48,56},{56,64},{64,7... | collective-permute-start | bytes 74888 | tf_op jit(solution)/shard_map/ppermute | solution.py:794
  26.5 7.9 %collective-permute-start.5 = (bf16[26,5,96]{2,1,0:T(8,128)(2,1)S(1)}, bf16[26,5,96]{2,1,0:T(8,128)(2,1)S(1)}, u32[]{:S(2)}, u32[]{:S(2)}) collective-permute-start(bf16[26,5,96]{2,1,0:T(8,128)(2,1)S(1)} %get-tuple-element.93), channel_id=1, source_target_pairs={{0,248},{8,0},{16,8},{24,16},{32,24},{40,32},{48,40},{56,48},{64,5... | collective-permute-start | bytes 74888 | tf_op jit(solution)/shard_map/ppermute | solution.py:794
  35.4 17.8 %collective-permute-start.6 = (bf16[5,36,96]{2,1,0:T(8,128)(2,1)S(1)}, bf16[5,36,96]{2,1,0:T(8,128)(2,1)S(1)}, u32[]{:S(2)}, u32[]{:S(2)}) collective-permute-start(bf16[5,36,96]{2,1,0:T(8,128)(2,1)S(1)} %get-tuple-element.87), channel_id=1, source_target_pairs={{0,64},{8,72},{16,80},{24,88},{32,96},{40,104},{48,112},{56,120},{... | collective-permute-start | bytes 103688 | tf_op jit(solution)/shard_map/ppermute | solution.py:794
  38.3 14.9 %collective-permute-start.7 = (bf16[5,36,96]{2,1,0:T(8,128)(2,1)S(1)}, bf16[5,36,96]{2,1,0:T(8,128)(2,1)S(1)}, u32[]{:S(2)}, u32[]{:S(2)}) collective-permute-start(bf16[5,36,96]{2,1,0:T(8,128)(2,1)S(1)} %get-tuple-element.88), channel_id=1, source_target_pairs={{0,192},{8,200},{16,208},{24,216},{32,224},{40,232},{48,240},{56,2... | collective-permute-start | bytes 103688 | tf_op jit(solution)/shard_map/ppermute | solution.py:794
  61.2 7.3 %copy-start.2 = (bf16[24,2304]{1,0:T(8,128)(2,1)S(1)}, bf16[24,2304]{1,0:T(8,128)(2,1)}, u32[]{:S(2)}) copy-start(bf16[24,2304]{1,0:T(8,128)(2,1)} %param.18) | copy-start | bytes 331780
  61.2 15.4 %all-to-all-start = ((bf16[8,144,384]{2,1,0:T(8,128)(2,1)}), bf16[8,144,384]{2,1,0:T(8,128)(2,1)S(1)}, u32[]{:S(2)}, u32[]{:S(2)}) async-start(bf16[8,144,384]{2,1,0:T(8,128)(2,1)} %get-tuple-element.62), calls=%async_computation | async-start | bytes 1769472 | tf_op jit(solution)/shard_map/all_to_all | solution.py:825
  76.6 0.9 copy-start
  86.6 17.9 %all-to-all-start.1 = ((bf16[8,32,16,128]{3,2,1,0:T(8,128)(2,1)}), bf16[8,32,16,128]{3,2,1,0:T(8,128)(2,1)S(1)}, u32[]{:S(2)}, u32[]{:S(2)}) async-start(bf16[8,32,16,128]{3,2,1,0:T(8,128)(2,1)} %get-tuple-element.69), calls=%async_computation.1 | async-start | bytes 2097152 | tf_op jit(solution)/shard_map/all_to_all | solution.py:825
  118.1 29.8 %copy-start.1 = (f32[576,96]{1,0:T(8,128)S(1)}, f32[576,96]{1,0:T(8,128)}, u32[]{:S(2)}) copy-start(f32[576,96]{1,0:T(8,128)} %get-tuple-element.61) | copy-start | bytes 663556
  143.4 9.8 %all-to-all-start.4 = ((f32[8,24,128]{2,1,0:T(8,128)}), f32[8,24,128]{2,1,0:T(8,128)S(1)}, u32[]{:S(2)}, u32[]{:S(2)}) async-start(f32[8,24,128]{2,1,0:T(8,128)} %shard_map.260), calls=%async_computation.4 | async-start | bytes 196608 | tf_op jit(solution)/shard_map/all_to_all | solution.py:825

commit v5 on v4

--- a/solution.py
+++ b/solution.py
@@ -18,6 +18,9 @@
 CELLS = SIDE * SIDE
 LANE = 128
 SMALL = 64
+DEEP_ROWS = 4
+SPREAD_ROWS = 6
+WEIGH_ROWS = 4
 VMEM_BYTES = 56 * 1024 * 1024
 SMALL_VMEM_BYTES = 16 * 1024 * 1024
 
@@ -84,13 +87,16 @@
     halves = []
     for half in range(2):
         lanes = slice(half * LANE, (half + 1) * LANE)
-        total = jnp.zeros((4, SIDE, LANE), F32)
-        for col_off in range(7):
-            slab = stem_ref[half, pl.ds(slab_row, 10), col_off : col_off + SIDE, :]
-            for row_off in range(7):
-                tap = 7 * row_off + col_off
-                total = total + slab[row_off : row_off + 4] * w_depth_ref[tap : tap + 1, lanes][None]
-        halves.append(total.reshape(4 * SIDE, LANE) + vectors_ref[1:2, lanes])
+        parts = []
+        for first in range(0, 4, DEEP_ROWS):
+            total = jnp.zeros((DEEP_ROWS, SIDE, LANE), F32)
+            for col_off in range(7):
+                slab = stem_ref[half, pl.ds(slab_row + first, DEEP_ROWS + 6), col_off : col_off + SIDE, :]
+                for row_off in range(7):
+                    tap = 7 * row_off + col_off
+                    total = total + slab[row_off : row_off + DEEP_ROWS] * w_depth_ref[tap : tap + 1, lanes][None]
+            parts.append(total.reshape(DEEP_ROWS * SIDE, LANE))
+        halves.append(jnp.concatenate(parts, axis=0) + vectors_ref[1:2, lanes])
     mean = (
         jnp.sum(halves[0], axis=-1, keepdims=True) + jnp.sum(halves[1], axis=-1, keepdims=True)
     ) / 256.0
@@ -133,7 +139,7 @@
 
 
 def middle_forward_kernel(
-    ready, seam_turns_ref, wide_ref, w_in_ref, w_depth_ref, w_up_ref, w_down_ref, head_ref,
+    seam_turns_ref, wide_ref, w_in_ref, w_depth_ref, w_up_ref, w_down_ref, head_ref,
     patches_out, stem_out, normed_out, inverse_out, scaled_out, slope_out, active_out, hidden_out,
     field_ref,
     patches_ref, stem_ref, normed_ref, inverse_ref, scaled_ref, slope_ref, active_ref, hidden_ref,
@@ -146,7 +152,6 @@
     send_stem = pltpu.make_async_copy(stem_ref, stem_out.at[:, 3:27], sem.at[1])
     turn_at, _ = turn_reader(seam_turns_ref)
     vectors_ref = w_depth_ref.at[VECTORS : VECTORS + 16]
-    ready()
     widen_stem_weight(w_in_ref, w_in_wide_ref)
     turns = (turn_at(0), None, (4 - turn_at(1)) & 3)
     pieces = [(turn, 0, 0, SIDE) + columns for turn, columns in zip(turns, BANDS)]
@@ -169,6 +174,8 @@
         return carry
 
     lax.fori_loop(0, 4, normalise, 0)
+    for send in sends[:3]:
+        send.start()
 
     def mix(block, carry):
         row = pl.multiple_of(block * 96, 96)
@@ -179,13 +186,13 @@
         return carry
 
     lax.fori_loop(0, 4, mix, 0)
-    for send in sends:
+    for send in sends[3:]:
         send.start()
     return sends + [send_patches, send_stem]
 
 
 def rim_forward_kernel(
-    ready, seam_turns_ref, wide_ref, w_in_ref, w_depth_ref, w_up_ref, w_down_ref,
+    seam_turns_ref, wide_ref, w_in_ref, w_depth_ref, w_up_ref, w_down_ref,
     head_ref, middle_field_ref,
     patches_in, stem_in, normed_in, inverse_in, scaled_in, slope_in, active_in, hidden_in,
     patches_out, stem_out, normed_out, inverse_out, scaled_out, slope_out, active_out, hidden_out,
@@ -213,7 +220,6 @@
     ]
     turn_at, across = turn_reader(seam_turns_ref)
     vectors_ref = w_depth_ref.at[VECTORS : VECTORS + 16]
-    ready()
     widen_stem_weight(w_in_ref, w_in_wide_ref)
     north = (turn_at(-across), None, (4 - turn_at(1 - across)) & 3)
     south = (turn_at(across), None, (4 - turn_at(across + 1)) & 3)
@@ -239,6 +245,8 @@
         return carry
 
     lax.fori_loop(0, 2, normalise, 0)
+    for send in sends[:6]:
+        send.start()
     field_ref[96:480, :] = middle_field_ref[...]
 
     def mix(block, carry):
@@ -250,7 +258,7 @@
         return carry
 
     lax.fori_loop(0, 2, mix, 0)
-    for send in sends:
+    for send in sends[6:]:
         send.start()
     for quarter in range(4):
         tight_ref[:, 96 * quarter : 96 * (quarter + 1)] = field_ref[
@@ -264,7 +272,6 @@
 
 def mixer_backward_kernel(
     coefficient,
-    ready,
     every_ref,
     own_ref,
     target_ref,
@@ -304,7 +311,6 @@
         fetch.start()
     send_hidden = pltpu.make_async_copy(hidden_grad_ref, hidden_grad_out, out_sem.at[0])
     send_scaled = pltpu.make_async_copy(scaled_grad_ref, scaled_grad_out, out_sem.at[1])
-    ready()
     members = every_ref.shape[0]
     own = own_ref[...]
     own_sent = own.astype(BF16).astype(F32)
@@ -389,7 +395,6 @@
 
 
 def depth_backward_kernel(
-    ready,
     scaled_grad_ref,
     normed_ref,
     inverse_ref,
@@ -421,7 +426,6 @@
     small_ref[...] = jnp.zeros_like(small_ref)
     sums_ref[...] = jnp.zeros_like(sums_ref)
     vectors_ref = w_depth_ref.at[VECTORS : VECTORS + 16]
-    ready()
 
     def unnormalise(block, carry):
         at = pl.ds(pl.multiple_of(block * 96, 96), 96)
@@ -455,30 +459,32 @@
         lanes = slice(half * LANE, (half + 1) * LANE)
 
         def spread(block, carry):
-            row = block * 3
-            total = jnp.zeros((3, 32, LANE), F32)
+            row = block * SPREAD_ROWS
+            total = jnp.zeros((SPREAD_ROWS, 32, LANE), F32)
             for col_off in range(7):
-                slab = deep_ref[half, pl.ds(row, 9), 8 - col_off : 40 - col_off, :]
+                slab = deep_ref[half, pl.ds(row, SPREAD_ROWS + 6), 8 - col_off : 40 - col_off, :]
                 for row_off in range(7):
                     tap = 7 * row_off + col_off
-                    total = total + slab[6 - row_off : 9 - row_off] * w_depth_ref[tap : tap + 1, lanes][None]
-            stem_grad_ref[half, pl.ds(row, 3)] = total
+                    total = total + slab[6 - row_off : 6 - row_off + SPREAD_ROWS] * w_depth_ref[tap : tap + 1, lanes][None]
+            stem_grad_ref[half, pl.ds(row, SPREAD_ROWS)] = total
             return carry
 
-        lax.fori_loop(0, 10, spread, 0)
+        lax.fori_loop(0, 30 // SPREAD_ROWS, spread, 0)
         for col_off in range(7):
 
             def weigh(block, totals):
-                row = block * 4
-                deep = deep_ref[half, pl.ds(6 + row, 4), 8 : 8 + SIDE, :]
-                slab = stem_ref[half, pl.ds(row, 10), col_off : col_off + SIDE, :]
+                row = block * WEIGH_ROWS
+                deep = deep_ref[half, pl.ds(6 + row, WEIGH_ROWS), 8 : 8 + SIDE, :]
+                slab = stem_ref[half, pl.ds(row, WEIGH_ROWS + 6), col_off : col_off + SIDE, :]
                 return tuple(
                     totals[row_off]
-                    + jnp.sum((slab[row_off : row_off + 4] * deep).reshape(12, 8, LANE), axis=0)
+                    + jnp.sum(
+                        (slab[row_off : row_off + WEIGH_ROWS] * deep).reshape(3 * WEIGH_ROWS, 8, LANE), axis=0
+                    )
                     for row_off in range(7)
                 )
 
-            totals = lax.fori_loop(0, 6, weigh, tuple(jnp.zeros((8, LANE), F32) for _ in range(7)))
+            totals = lax.fori_loop(0, SIDE // WEIGH_ROWS, weigh, tuple(jnp.zeros((8, LANE), F32) for _ in range(7)))
             for row_off in range(7):
                 tap = 7 * row_off + col_off
                 small_ref[tap : tap + 1, lanes] = jnp.sum(totals[row_off], axis=0, keepdims=True)
@@ -517,8 +523,7 @@
     late_ref[...] = tight_ref[...].astype(BF16)
 
 
-def combine_kernel(ready, early_ref, late_ref, share_ref, rows_ref):
-    ready()
+def combine_kernel(early_ref, late_ref, share_ref, rows_ref):
     members = early_ref.shape[0]
     early = early_ref[0].astype(F32)
     late = late_ref[0].astype(F32)
@@ -534,8 +539,7 @@
     share_ref[...] = rows_ref[...].astype(BF16)
 
 
-def total_kernel(ready, share_ref, copies_ref):
-    ready()
+def total_kernel(share_ref, copies_ref):
     total = share_ref[0].astype(F32)
     for tile in range(1, share_ref.shape[0]):
         total = total + share_ref[tile].astype(F32)
@@ -544,9 +548,8 @@
 
 
 def unpack_kernel(
-    ready, whole_ref, w_in_ref, w_depth_ref, w_up_ref, w_down_ref, w_out_ref, small_ref, b_up_ref
+    whole_ref, w_in_ref, w_depth_ref, w_up_ref, w_down_ref, w_out_ref, small_ref, b_up_ref
 ):
-    ready()
     parts = whole_ref.shape[0]
     for part in range(parts):
         for row in range(7):
@@ -568,46 +571,18 @@
 
 
 def call(kernel, outs, scratch, *operands, spaces=None, vmem=VMEM_BYTES, flops=0, aliases=None):
-    spaces = spaces or "v" * len(operands)
-    count_in, count_out = len(operands), len(outs)
-    copied_in = [k for k in range(count_in) if spaces[k] == "v"]
-    copied_out = [k for k in range(count_out) if outs[k][2] == "v"]
-    buffers = [pltpu.VMEM(operands[k].shape, operands[k].dtype) for k in copied_in]
-    buffers += [pltpu.VMEM(outs[k][0], outs[k][1]) for k in copied_out]
-    own = [x if not isinstance(x, tuple) else pltpu.VMEM(*x) for x in scratch]
-    semaphores = pltpu.SemaphoreType.DMA((len(buffers),))
+    kinds = {"v": pltpu.VMEM, "s": pltpu.SMEM, "a": pl.ANY}
 
     def wrapped(*refs):
-        ins, results = list(refs[:count_in]), list(refs[count_in : count_in + count_out])
-        rest = refs[count_in + count_out :]
-        held, sem, working = rest[: len(buffers)], rest[len(buffers)], rest[len(buffers) + 1 :]
-        fetches, sends = [], []
-        for place, k in enumerate(copied_in):
-            fetches.append(pltpu.make_async_copy(ins[k], held[place], sem.at[place]))
-            ins[k] = held[place]
-        for place, k in enumerate(copied_out, len(copied_in)):
-            sends.append(pltpu.make_async_copy(held[place], results[k], sem.at[place]))
-            results[k] = held[place]
-        for fetch in fetches:
-            fetch.start()
-
-        def ready():
-            for fetch in fetches:
-                fetch.wait()
-
-        started = kernel(ready, *ins, *results, *working) or []
-        for send in sends:
-            send.start()
-        for send in list(started) + sends:
+        for send in kernel(*refs) or ():
             send.wait()
 
-    place_of = {"s": pltpu.SMEM, "a": pl.ANY, "v": pl.ANY}
     return pl.pallas_call(
         wrapped,
         out_shape=[jax.ShapeDtypeStruct(shape, kind) for shape, kind, _ in outs],
-        in_specs=[pl.BlockSpec(memory_space=place_of[letter]) for letter in spaces],
-        out_specs=[pl.BlockSpec(memory_space=pl.ANY)] * count_out,
-        scratch_shapes=buffers + [semaphores] + own,
+        in_specs=[pl.BlockSpec(memory_space=kinds[k]) for k in spaces or "v" * len(operands)],
+        out_specs=[pl.BlockSpec(memory_space=kinds[k]) for _, _, k in outs],
+        scratch_shapes=[x if not isinstance(x, tuple) else pltpu.VMEM(*x) for x in scratch],
         input_output_aliases=aliases or {},
         compiler_params=pltpu.CompilerParams(vmem_limit_bytes=vmem),
         cost_estimate=pl.CostEstimate(flops=flops, bytes_accessed=8_000_000, transcendentals=0),
@@ -812,13 +787,47 @@
     return result
 
 
-def seam_strips(tile, my_turn, next_turn, margin, row_tiles):
-    came_west = shifted(turned_edge(tile, next_turn, margin, True), "space", 1)
-    came_east = shifted(turned_edge(tile, (4 - my_turn) % 4, margin, False), "space", -1)
-    widened = jnp.concatenate([came_west, tile, came_east], axis=1)
-    came_north = shifted(widened[-margin:], "space", row_tiles)
-    came_south = shifted(widened[:margin], "space", -row_tiles)
-    return came_north, widened, came_south
+def turned_side(rows, turns, east):
+    size = rows.shape[0]
+    width = rows.shape[1] // size
+    west_side, east_side = rows[:, :width], rows[:, -width:]
+    north_side, south_side = rows[0].reshape(size, width), rows[-1].reshape(size, width)
+    if east:
+        sides = (east_side, south_side[::-1], west_side[::-1], north_side)
+    else:
+        sides = (west_side, north_side[::-1], east_side[::-1], south_side)
+    result = sides[0]
+    for quarter in range(1, 4):
+        result = jnp.where(turns == quarter, sides[quarter], result)
+    return result[:, None]
+
+
+def near_source(rows, my_turn, next_turn, row_tiles):
+    tile = rows.reshape(SIDE, SIDE, -1)
+    came_west = shifted(turned_side(rows, next_turn, True), "space", 1)
+    came_east = shifted(turned_side(rows, (4 - my_turn) % 4, False), "space", -1)
+    widened_rows = jnp.concatenate([came_west, tile, came_east], axis=1)
+    came_north = shifted(widened_rows[-1:], "space", row_tiles)
+    came_south = shifted(widened_rows[:1], "space", -row_tiles)
+    return jnp.concatenate([came_north, widened_rows, came_south], axis=0)
+
+
+def widened_band(near, my_turn, next_turn, margin):
+    came_west = shifted(turned_edge(near, next_turn, margin, True), "space", 1)
+    came_east = shifted(turned_edge(near, (4 - my_turn) % 4, margin, False), "space", -1)
+    return jnp.concatenate([came_west, near, came_east], axis=1)
+
+
+def exchange_rows(band, margin, tile_index, spaces):
+    row_tiles = spaces // 4
+    place = tile_index // row_tiles
+    to_south = (jnp.arange(4) == (place + 1) % 4)[:, None, None, None]
+    parts = jnp.where(to_south, band[None, -margin:], band[None, :margin])
+    columns = [[column + row_tiles * k for k in range(4)] for column in range(row_tiles)]
+    came = lax.all_to_all(parts, "space", 0, 0, axis_index_groups=columns, tiled=True)
+    north = lax.dynamic_index_in_dim(came, (place + 3) % 4, keepdims=False)
+    south = lax.dynamic_index_in_dim(came, (place + 1) % 4, keepdims=False)
+    return north, south
 
 
 def swap(value, axis):
@@ -853,11 +862,10 @@
 
     my_turn = turn_at(0)
     next_turn = turn_at(1)
-    source = (
-        initial_state.astype(F32) + starting_field_nudges[0].astype(F32)
-    ).astype(BF16).reshape(SIDE, SIDE, 96)
-    near = jnp.concatenate(seam_strips(source, my_turn, next_turn, 1, row_tiles), axis=0)
-    north, band, south = seam_strips(near, my_turn, next_turn, 5, row_tiles)
+    source = (initial_state.astype(F32) + starting_field_nudges[0].astype(F32)).astype(BF16)
+    near = near_source(source, my_turn, next_turn, row_tiles)
+    band = widened_band(near, my_turn, next_turn, 5)
+    north, south = exchange_rows(band, 5, tile_index, spaces)
     params = stack_params(w_depth, b_in, b_depth, norm_gain, norm_shift, b_down, head_bias, b_up)
     head = head_weight.T
     kept, middle_field = run_middle_forward(seam_turns, band, w_in, params, w_up, w_down, head)

time: 156 us -> 160 us (1.026)
  local copies, waits for them, and re-layouts: 7.61 us -> 12.2 us
  starting transfers between devices: 46.2 us -> 43.3 us
  Pallas kernels: 41.5 us -> 39.6 us
    ppermute x8 -> x6, starting transfers between devices: 31.1 us -> 21.9 us  [shifted(): lax.ppermute(value, axis, [(i, (i + by) % peers) for i in range(peers)])]
    all_to_all x0 -> x1, starting transfers between devices: none -> 7.2 us  [exchange_rows(): lax.all_to_all(parts, 'space', 0, 0, axis_index_groups=columns, tiled=True)]
    unnamed x30 -> x16, local copies, waits for them, and re-layouts: 2.31 us -> 5.33 us
    pallas_call x7, Pallas kernels: 41.5 us -> 39.6 us  [call(): pl.pallas_call(wrapped, out_shape=[jax.ShapeDtypeStruct(shape, kind) for...]
  transfers between devices with their start and end apart: 11 -> 10, of which waited for: 7 -> 5; matrix products, arithmetic and copies ran while one was open for 3% -> 6% of each run, Pallas kernels for 15% -> 14%
where the time goes in v5:
time: 160 us; the launch traced here: 159 us
  starting transfers between devices  43.3 us (27%)
  Pallas kernels  39.6 us (25%)
  blocking collectives  38.7 us (24%)
  waiting for transfers between devices  15.6 us (10%)
  local copies, waits for them, and re-layouts  12.2 us (8%)
  other arithmetic  5.67 us (4%)
  between operations  3.52 us (2%)
    pallas_call x7, Pallas kernels, call(): pl.pallas_call(wrapped, out_shape=[jax.ShapeDtypeStruct(shape, kind) for...  39.6 us
    all_to_all x2, blocking collectives, swap(): return lax.all_to_all(value, axis, 0, 0, tiled=True)  38.7 us
    ppermute x6, starting transfers between devices, shifted(): lax.ppermute(value, axis, [(i, (i + by) % peers) for i in range(peers)])  21.9 us
    all_to_all x3, starting transfers between devices, swap(): return lax.all_to_all(value, axis, 0, 0, tiled=True)  14.3 us
    all_to_all x3, waiting for transfers between devices, swap(): return lax.all_to_all(value, axis, 0, 0, tiled=True)  11.5 us
    all_to_all x1, starting transfers between devices, exchange_rows(): lax.all_to_all(parts, 'space', 0, 0, axis_index_groups=columns, tiled=True)  7.2 us
    unnamed x16, local copies, waits for them, and re-layouts  5.33 us
  transfers between devices with their start and end apart: 10, of which 5 were waited for; matrix products, arithmetic and copies ran while one was open for 6% of the time, Pallas kernels for 14%

profile of v5, /device:TPU:2, one launch (start us, length us, event | category | flops | bytes accessed | tf_op | source)
XLA Modules:
  0.0 158.7 jit_solution(2272760197956443666)
XLA Ops:
  0.7 1.3 fusion.28
  2.7 1.0 fusion.1
  6.1 8.0 %collective-permute-start.1 = (bf16[24,1,96]{2,0,1:T(8,128)(2,1)S(1)}, bf16[24,1,96]{2,0,1:T(8,128)(2,1)S(1)}, u32[]{:S(2)}, u32[]{:S(2)}) collective-permute-start(bf16[24,1,96]{2,0,1:T(8,128)(2,1)S(1)} %get-tuple-element.104), channel_id=1, source_target_pairs={{0,248},{8,0},{16,8},{24,16},{32,24},{40,32},{48,40},{56,48},{64,5... | collective-permute-start | bytes 13832 | tf_op jit(solution)/shard_map/ppermute | solution.py:769
  15.0 0.8 dynamic-update-slice
  15.8 0.8 dynamic-update-slice.1
  16.7 0.8 dynamic-update-slice.2
  17.5 0.8 dynamic-update-slice.3
  18.3 0.8 dynamic-update-slice.4
  19.4 0.8 dynamic-update-slice.6
  20.4 2.2 %collective-permute-start.2 = (bf16[1,26,96]{2,0,1:T(2,128)(2,1)S(1)}, bf16[1,26,96]{2,0,1:T(2,128)(2,1)S(1)}, u32[]{:S(2)}, u32[]{:S(2)}) collective-permute-start(bf16[1,26,96]{2,0,1:T(2,128)(2,1)S(1)} %get-tuple-element.102), channel_id=1, source_target_pairs={{0,64},{8,72},{16,80},{24,88},{32,96},{40,104},{48,112},{56,120},{... | collective-permute-start | bytes 14984 | tf_op jit(solution)/shard_map/ppermute | solution.py:769
  22.6 6.2 %collective-permute-start.3 = (bf16[1,26,96]{2,0,1:T(2,128)(2,1)S(1)}, bf16[1,26,96]{2,0,1:T(2,128)(2,1)S(1)}, u32[]{:S(2)}, u32[]{:S(2)}) collective-permute-start(bf16[1,26,96]{2,0,1:T(2,128)(2,1)S(1)} %get-tuple-element.103), channel_id=1, source_target_pairs={{0,192},{8,200},{16,208},{24,216},{32,224},{40,232},{48,240},{56,2... | collective-permute-start | bytes 14984 | tf_op jit(solution)/shard_map/ppermute | solution.py:769
  29.4 1.0 collective-permute-done.2
  31.3 5.3 %collective-permute-start.5 = (bf16[26,5,96]{2,1,0:T(8,128)(2,1)S(1)}, bf16[26,5,96]{2,1,0:T(8,128)(2,1)S(1)}, u32[]{:S(2)}, u32[]{:S(2)}) collective-permute-start(bf16[26,5,96]{2,1,0:T(8,128)(2,1)S(1)} %get-tuple-element.95), channel_id=1, source_target_pairs={{0,248},{8,0},{16,8},{24,16},{32,24},{40,32},{48,40},{56,48},{64,5... | collective-permute-start | bytes 74888 | tf_op jit(solution)/shard_map/ppermute | solution.py:769
  36.6 1.8 %collective-permute-done.4 = bf16[26,5,96]{2,1,0:T(8,128)(2,1)S(1)} collective-permute-done((bf16[26,5,96]{2,1,0:T(8,128)(2,1)S(1)}, bf16[26,5,96]{2,1,0:T(8,128)(2,1)S(1)}, u32[]{:S(2)}, u32[]{:S(2)}) %collective-permute-start.4) | collective-permute-done | bytes 24992 | tf_op jit(solution)/shard_map/ppermute | solution.py:769
  38.6 0.8 pad_convert_fusion.refs_1_
  39.4 0.8 broadcast_select_fusion
  40.2 7.2 %all-to-all-start = ((bf16[4,5,36,96]{3,2,1,0:T(8,128)(2,1)}), bf16[4,5,36,96]{3,2,1,0:T(8,128)(2,1)S(1)}, u32[]{:S(2)}, u32[]{:S(2)}) async-start(bf16[4,5,36,96]{3,2,1,0:T(8,128)(2,1)} %broadcast_select_fusion), calls=%async_computation | async-start | bytes 409600 | tf_op jit(solution)/shard_map/all_to_all | solution.py:827
  47.4 9.4 %shard_map.255 = (bf16[960,1152]{1,0:T(8,128)(2,1)}, f32[2,30,32,128]{3,2,1,0:T(8,128)}, f32[576,256]{1,0:T(8,128)}, f32[576,128]{1,0:T(8,128)}, bf16[576,256]{1...) custom-call(s32[32]{0:T(128)} %refs_0_.3, ...), custom_call_target="tpu_custom_call" | custom-call | flops 10000000000 | bytes 8000000 | tf_op jit(solution)/shard_map/pallas_call | solution.py:580
  56.8 1.3 all-to-all-done
  58.8 7.4 %shard_map.256 = (bf16[960,1152]{1,0:T(8,128)(2,1)}, f32[2,30,32,128]{3,2,1,0:T(8,128)}, f32[576,256]{1,0:T(8,128)}, f32[576,128]{1,0:T(8,128)}, bf16[576,256]{1...) custom-call(s32[32]{0:T(128)} %refs_0_.3, ...), custom_call_target="tpu_custom_call", output_to_operand_aliasing={{0}: (8, {}), {1}: (9, {}), {2}: (10, {}), {3}: (11, {}), {... | custom-call | flops 5000000000 | bytes 8000000 | tf_op jit(solution)/shard_map/pallas_call | solution.py:580
  66.2 5.1 %all-to-all-start.1 = ((bf16[8,144,384]{2,1,0:T(8,128)(2,1)}), bf16[8,144,384]{2,1,0:T(8,128)(2,1)S(1)}, u32[]{:S(2)}, u32[]{:S(2)}) async-start(bf16[8,144,384]{2,1,0:T(8,128)(2,1)} %get-tuple-element.62), calls=%async_computation.1 | async-start | bytes 1769472 | tf_op jit(solution)/shard_map/all_to_all | solution.py:834
  72.9 0.8 reshape.108.refs_2_
  73.7 7.1 %all-to-all-done.1.refs_0_ = bf16[8,144,384]{2,1,0:T(8,128)(2,1)S(1)} async-done(((bf16[8,144,384]{2,1,0:T(8,128)(2,1)}), bf16[8,144,384]{2,1,0:T(8,128)(2,1)S(1)}, u32[]{:S(2)}, u32[]{:S(2)}) %all-to-all-start.1) | async-done | bytes 884768 | tf_op jit(solution)/shard_map/all_to_all | solution.py:834
  80.8 0.9 copy-done
  81.7 8.8 %shard_map.257 = (bf16[8,32,16,128]{3,2,1,0:T(8,128)(2,1)}, f32[96,256]{1,0:T(8,128)}, f32[576,256]{1,0:T(8,128)}, f32[576,256]{1,0:T(8,128)}, f32[8,256]{1,0:T(8,128)}) custom-call(bf16[8,144,384]{2,1,0:T(8,128)(2,1)} %copy-done, f32[144,384]{1,0:T(8,128)} %get-tuple-element.63.refs_1_, bf16[144,384]{1,0:T(8,128)(2,1)} %reshape.108.refs_2_, ...), custom_call_target="tpu_custom_call" | custom-call | flops 12000000000 | bytes 8000000 | tf_op jit(solution)/shard_map/pallas_call | solution.py:580
  90.5 4.6 %all-to-all-start.2 = ((bf16[8,32,16,128]{3,2,1,0:T(8,128)(2,1)}), bf16[8,32,16,128]{3,2,1,0:T(8,128)(2,1)S(1)}, u32[]{:S(2)}, u32[]{:S(2)}) async-start(bf16[8,32,16,128]{3,2,1,0:T(8,128)(2,1)} %get-tuple-element.69), calls=%async_computation.2 | async-start | bytes 2097152 | tf_op jit(solution)/shard_map/all_to_all | solution.py:834
  95.1 12.2 %shard_map.258 = bf16[256,1152]{1,0:T(8,128)(2,1)} custom-call(f32[576,256]{1,0:T(8,128)} %get-tuple-element.70.refs_0_, f32[576,256]{1,0:T(8,128)} %get-tuple-element.71.refs_1_, f32[576,128]{1,0:T(8,128)} %get-tuple-element.72.refs_2_, f32[576,256]{1,0:T(8,128)} %get-tuple-element.73.refs_3_, f32[2,30,32,128]{3,2,1,0:T(8,128)} %get-tuple-element.74.refs_4_, ...), custom_call_target="tpu_custom_call" | custom-call | flops 12000000000 | bytes 8000000 | tf_op jit(solution)/shard_map/pallas_call | solution.py:580
  107.4 13.6 %all_to_all.30.refs_1_ = bf16[8,32,1152]{2,1,0:T(8,128)(2,1)S(1)} all-to-all(bf16[8,32,1152]{2,1,0:T(8,128)(2,1)} %bitcast.41), channel_id=1, replica_groups=mesh['space'=32,'ens'=8] {'ens'}, dimensions={0} | all-to-all | bytes 1179648 | tf_op jit(solution)/shard_map/all_to_all | solution.py:834
  121.3 25.1 %all_to_all.31.refs_0_ = bf16[32,24,128]{2,1,0:T(8,128)(2,1)S(1)} all-to-all(bf16[32,24,128]{2,1,0:T(8,128)(2,1)S(1)} %shard_map.259), channel_id=1, replica_groups=mesh['space'=32,'ens'=8] {'space'}, dimensions={0} | all-to-all | bytes 393216 | tf_op jit(solution)/shard_map/all_to_all | solution.py:834
  147.1 4.5 %all-to-all-start.5 = ((f32[8,24,128]{2,1,0:T(8,128)}), f32[8,24,128]{2,1,0:T(8,128)S(1)}, u32[]{:S(2)}, u32[]{:S(2)}) async-start(f32[8,24,128]{2,1,0:T(8,128)} %shard_map.260), calls=%async_computation.5 | async-start | bytes 196608 | tf_op jit(solution)/shard_map/all_to_all | solution.py:834
  151.7 0.8 reshape.106
  152.5 4.5 %all-to-all-done.5.refs_0_ = f32[8,24,128]{2,1,0:T(8,128)S(1)} async-done(((f32[8,24,128]{2,1,0:T(8,128)}), f32[8,24,128]{2,1,0:T(8,128)S(1)}, u32[]{:S(2)}, u32[]{:S(2)}) %all-to-all-start.5) | async-done | bytes 98336 | tf_op jit(solution)/shard_map/all_to_all | solution.py:834
  (60 shorter events, 8.3 us)
Async XLA Ops:
  0.6 28.1 %copy-start.3 = (bf16[49,256]{1,0:T(8,128)(2,1)S(1)}, bf16[49,256]{1,0:T(8,128)(2,1)}, u32[]{:S(2)}) copy-start(bf16[49,256]{1,0:T(8,128)(2,1)} %param.22) | copy-start | bytes 75268
  6.1 14.1 %collective-permute-start = (bf16[24,1,96]{2,0,1:T(8,128)(2,1)S(1)}, bf16[24,1,96]{2,0,1:T(8,128)(2,1)S(1)}, u32[]{:S(2)}, u32[]{:S(2)}) collective-permute-start(bf16[24,1,96]{2,0,1:T(8,128)(2,1)S(1)} %get-tuple-element.105), channel_id=1, source_target_pairs={{0,8},{8,16},{16,24},{24,32},{32,40},{40,48},{48,56},{56,64},{64,7... | collective-permute-start | bytes 13832 | tf_op jit(solution)/shard_map/ppermute | solution.py:769
  6.1 14.2 %collective-permute-start.1 = (bf16[24,1,96]{2,0,1:T(8,128)(2,1)S(1)}, bf16[24,1,96]{2,0,1:T(8,128)(2,1)S(1)}, u32[]{:S(2)}, u32[]{:S(2)}) collective-permute-start(bf16[24,1,96]{2,0,1:T(8,128)(2,1)S(1)} %get-tuple-element.104), channel_id=1, source_target_pairs={{0,248},{8,0},{16,8},{24,16},{32,24},{40,32},{48,40},{56,48},{64,5... | collective-permute-start | bytes 13832 | tf_op jit(solution)/shard_map/ppermute | solution.py:769
  20.4 10.1 %collective-permute-start.2 = (bf16[1,26,96]{2,0,1:T(2,128)(2,1)S(1)}, bf16[1,26,96]{2,0,1:T(2,128)(2,1)S(1)}, u32[]{:S(2)}, u32[]{:S(2)}) collective-permute-start(bf16[1,26,96]{2,0,1:T(2,128)(2,1)S(1)} %get-tuple-element.102), channel_id=1, source_target_pairs={{0,64},{8,72},{16,80},{24,88},{32,96},{40,104},{48,112},{56,120},{... | collective-permute-start | bytes 14984 | tf_op jit(solution)/shard_map/ppermute | solution.py:769
  22.6 7.9 %collective-permute-start.3 = (bf16[1,26,96]{2,0,1:T(2,128)(2,1)S(1)}, bf16[1,26,96]{2,0,1:T(2,128)(2,1)S(1)}, u32[]{:S(2)}, u32[]{:S(2)}) collective-permute-start(bf16[1,26,96]{2,0,1:T(2,128)(2,1)S(1)} %get-tuple-element.103), channel_id=1, source_target_pairs={{0,192},{8,200},{16,208},{24,216},{32,224},{40,232},{48,240},{56,2... | collective-permute-start | bytes 14984 | tf_op jit(solution)/shard_map/ppermute | solution.py:769
  31.2 7.3 %collective-permute-start.4 = (bf16[26,5,96]{2,1,0:T(8,128)(2,1)S(1)}, bf16[26,5,96]{2,1,0:T(8,128)(2,1)S(1)}, u32[]{:S(2)}, u32[]{:S(2)}) collective-permute-start(bf16[26,5,96]{2,1,0:T(8,128)(2,1)S(1)} %fusion.13), channel_id=1, source_target_pairs={{0,8},{8,16},{16,24},{24,32},{32,40},{40,48},{48,56},{56,64},{64,7... | collective-permute-start | bytes 74888 | tf_op jit(solution)/shard_map/ppermute | solution.py:769
  31.3 7.2 %collective-permute-start.5 = (bf16[26,5,96]{2,1,0:T(8,128)(2,1)S(1)}, bf16[26,5,96]{2,1,0:T(8,128)(2,1)S(1)}, u32[]{:S(2)}, u32[]{:S(2)}) collective-permute-start(bf16[26,5,96]{2,1,0:T(8,128)(2,1)S(1)} %get-tuple-element.95), channel_id=1, source_target_pairs={{0,248},{8,0},{16,8},{24,16},{32,24},{40,32},{48,40},{56,48},{64,5... | collective-permute-start | bytes 74888 | tf_op jit(solution)/shard_map/ppermute | solution.py:769
  40.2 17.8 %all-to-all-start = ((bf16[4,5,36,96]{3,2,1,0:T(8,128)(2,1)}), bf16[4,5,36,96]{3,2,1,0:T(8,128)(2,1)S(1)}, u32[]{:S(2)}, u32[]{:S(2)}) async-start(bf16[4,5,36,96]{3,2,1,0:T(8,128)(2,1)} %broadcast_select_fusion), calls=%async_computation | async-start | bytes 409600 | tf_op jit(solution)/shard_map/all_to_all | solution.py:827
  66.2 6.4 %copy-start.2 = (bf16[24,2304]{1,0:T(8,128)(2,1)S(1)}, bf16[24,2304]{1,0:T(8,128)(2,1)}, u32[]{:S(2)}) copy-start(bf16[24,2304]{1,0:T(8,128)(2,1)} %param.18) | copy-start | bytes 331780
  66.2 14.5 %all-to-all-start.1 = ((bf16[8,144,384]{2,1,0:T(8,128)(2,1)}), bf16[8,144,384]{2,1,0:T(8,128)(2,1)S(1)}, u32[]{:S(2)}, u32[]{:S(2)}) async-start(bf16[8,144,384]{2,1,0:T(8,128)(2,1)} %get-tuple-element.62), calls=%async_computation.1 | async-start | bytes 1769472 | tf_op jit(solution)/shard_map/all_to_all | solution.py:834
  80.8 0.9 copy-start
  90.5 16.9 %all-to-all-start.2 = ((bf16[8,32,16,128]{3,2,1,0:T(8,128)(2,1)}), bf16[8,32,16,128]{3,2,1,0:T(8,128)(2,1)S(1)}, u32[]{:S(2)}, u32[]{:S(2)}) async-start(bf16[8,32,16,128]{3,2,1,0:T(8,128)(2,1)} %get-tuple-element.69), calls=%async_computation.2 | async-start | bytes 2097152 | tf_op jit(solution)/shard_map/all_to_all | solution.py:834
  121.0 30.6 %copy-start.1 = (f32[576,96]{1,0:T(8,128)S(1)}, f32[576,96]{1,0:T(8,128)}, u32[]{:S(2)}) copy-start(f32[576,96]{1,0:T(8,128)} %get-tuple-element.61) | copy-start | bytes 663556
  147.1 9.8 %all-to-all-start.5 = ((f32[8,24,128]{2,1,0:T(8,128)}), f32[8,24,128]{2,1,0:T(8,128)S(1)}, u32[]{:S(2)}, u32[]{:S(2)}) async-start(f32[8,24,128]{2,1,0:T(8,128)} %shard_map.260), calls=%async_computation.5 | async-start | bytes 196608 | tf_op jit(solution)/shard_map/all_to_all | solution.py:834

commit v6 on v2

--- a/solution.py
+++ b/solution.py
@@ -407,17 +407,17 @@
         lanes = slice(half * LANE, (half + 1) * LANE)
 
         def spread(block, carry):
-            row = block * 3
-            total = jnp.zeros((3, 32, LANE), F32)
+            row = block * 6
+            total = jnp.zeros((6, 32, LANE), F32)
             for col_off in range(7):
-                slab = deep_ref[half, pl.ds(row, 9), 8 - col_off : 40 - col_off, :]
+                slab = deep_ref[half, pl.ds(row, 12), 8 - col_off : 40 - col_off, :]
                 for row_off in range(7):
                     tap = 7 * row_off + col_off
-                    total = total + slab[6 - row_off : 9 - row_off] * w_depth_ref[tap : tap + 1, lanes][None]
-            stem_grad_ref[half, pl.ds(row, 3)] = total
+                    total = total + slab[6 - row_off : 12 - row_off] * w_depth_ref[tap : tap + 1, lanes][None]
+            stem_grad_ref[half, pl.ds(row, 6)] = total
             return carry
 
-        lax.fori_loop(0, 10, spread, 0)
+        lax.fori_loop(0, 5, spread, 0)
         for col_off in range(7):
 
             def weigh(block, totals):
@@ -494,7 +494,19 @@
 
 
 def unpack_kernel(
-    whole_ref, w_in_ref, w_depth_ref, w_up_ref, w_down_ref, w_out_ref, small_ref, b_up_ref
+    whole_ref,
+    w_in_ref,
+    w_depth_ref,
+    w_up_ref,
+    w_down_ref,
+    w_out_ref,
+    b_up_ref,
+    b_depth_ref,
+    gain_ref,
+    shift_ref,
+    b_in_ref,
+    b_down_ref,
+    b_out_ref,
 ):
     parts = whole_ref.shape[0]
     for part in range(parts):
@@ -513,7 +525,10 @@
         w_out_ref[2:3, lanes] = whole_ref[part, 23:24, 96:128]
         b_up_ref[0:1, 4 * part : 4 * part + 4] = whole_ref[part, 23:24, 54:58]
     small = jnp.concatenate([whole_ref[part, 23:24, :] for part in range(parts)], axis=0)
-    small_ref[...] = small.T[48:64, :]
+    by_row = small.T
+    for row, out_ref in enumerate((b_depth_ref, gain_ref, shift_ref, b_in_ref, b_down_ref), 49):
+        out_ref[...] = by_row[row : row + 1, :]
+    b_out_ref[...] = by_row[58:59, 0:3]
 
 
 def call(kernel, outs, scratch, *operands, spaces=None, vmem=VMEM_BYTES, flops=0):
@@ -674,7 +689,7 @@
 
 
 def run_unpack(whole):
-    shapes = ((8, 864), (8, 49), (32, 256), (8, 1024), (3, 256), (16, 8), (1, 32))
+    shapes = ((8, 864), (8, 49), (32, 256), (8, 1024), (3, 256), (1, 32)) + ((1, 8),) * 5 + ((1, 3),)
     return call(
         unpack_kernel, [(shape, F32, "v") for shape in shapes], [], whole, vmem=SMALL_VMEM_BYTES
     )
@@ -768,21 +783,24 @@
     late_parts = swap(late.reshape(8, 32, 1152), "ens")
     shares = swap(run_combine(early_parts, late_parts), "space")
     whole = swap(run_total(shares, members), "ens")
-    grad_w_in, grad_w_depth, grad_w_up, grad_w_down, grad_w_out, small, grad_b_up = run_unpack(whole)
+    (
+        grad_w_in, grad_w_depth, grad_w_up, grad_w_down, grad_w_out,
+        grad_b_up, grad_b_depth, grad_gain, grad_shift, grad_b_in, grad_b_down, grad_b_out,
+    ) = run_unpack(whole)
     return (
         predicted,
         grad_w_in.T,
-        small[4],
+        grad_b_in[0],
         grad_w_depth.T,
-        small[1],
-        small[2],
-        small[3],
+        grad_b_depth[0],
+        grad_gain[0],
+        grad_shift[0],
         grad_w_up.T,
         grad_b_up[0],
         grad_w_down.T,
-        small[5],
+        grad_b_down[0],
         grad_w_out.T,
-        small[10, :3],
+        grad_b_out[0],
     )
 
 

time: 153 us -> 152 us (level)
  transfers between devices with their start and end apart: 11 -> 11, of which waited for: 10 -> 10; matrix products, arithmetic and copies ran while one was open for 4% -> 4% of each run, Pallas kernels for 9% -> 8%
where the time goes in v6:
time: 152 us; the launch traced here: 151 us
  starting transfers between devices  35.7 us (23%)
  Pallas kernels  35.4 us (23%)
  waiting for transfers between devices  33.3 us (22%)
  blocking collectives  32.6 us (21%)
  local copies, waits for them, and re-layouts  7.2 us (5%)
  between operations  3.69 us (2%)
  other arithmetic  3.5 us (2%)
    pallas_call x6, Pallas kernels, call(): pl.pallas_call(kernel, out_shape=[jax.ShapeDtypeStruct(shape, kind) for s...  35.4 us
    all_to_all x2, blocking collectives, swap(): return lax.all_to_all(value, axis, 0, 0, tiled=True)  32.6 us
    ppermute x8, waiting for transfers between devices, shifted(): lax.ppermute(value, axis, [(i, (i + by) % peers) for i in range(peers)])  21.8 us
    ppermute x8, starting transfers between devices, shifted(): lax.ppermute(value, axis, [(i, (i + by) % peers) for i in range(peers)])  20.8 us
    all_to_all x3, starting transfers between devices, swap(): return lax.all_to_all(value, axis, 0, 0, tiled=True)  15 us
    all_to_all x3, waiting for transfers between devices, swap(): return lax.all_to_all(value, axis, 0, 0, tiled=True)  11.5 us
  transfers between devices with their start and end apart: 11, of which 10 were waited for; matrix products, arithmetic and copies ran while one was open for 4% of the time, Pallas kernels for 8%

profile of v6, /device:TPU:2, one launch (start us, length us, event | category | flops | bytes accessed | tf_op | source)
XLA Modules:
  0.0 151.4 jit_solution(4212375279837226462)
XLA Ops:
  0.7 1.3 fusion.16
  2.7 1.0 fusion.1
  6.1 8.0 %collective-permute-start.1 = (bf16[24,1,96]{2,0,1:T(8,128)(2,1)S(1)}, bf16[24,1,96]{2,0,1:T(8,128)(2,1)S(1)}, u32[]{:S(2)}, u32[]{:S(2)}) collective-permute-start(bf16[24,1,96]{2,0,1:T(8,128)(2,1)S(1)} %get-tuple-element.94), channel_id=1, source_target_pairs={{0,248},{8,0},{16,8},{24,16},{32,24},{40,32},{48,40},{56,48},{64,5... | collective-permute-start | bytes 13832 | tf_op jit(solution)/shard_map/ppermute | solution.py:700
  14.1 1.2 collective-permute-done
  15.5 4.9 %collective-permute-start.3 = (bf16[1,26,96]{2,0,1:T(2,128)(2,1)S(1)}, bf16[1,26,96]{2,0,1:T(2,128)(2,1)S(1)}, u32[]{:S(2)}, u32[]{:S(2)}) collective-permute-start(bf16[1,26,96]{2,0,1:T(2,128)(2,1)S(1)} %get-tuple-element.93), channel_id=1, source_target_pairs={{0,192},{8,200},{16,208},{24,216},{32,224},{40,232},{48,240},{56,2... | collective-permute-start | bytes 14984 | tf_op jit(solution)/shard_map/ppermute | solution.py:700
  20.4 1.2 collective-permute-start.2
  21.5 1.7 %collective-permute-done.3 = bf16[1,26,96]{2,0,1:T(2,128)(2,1)S(1)} collective-permute-done((bf16[1,26,96]{2,0,1:T(2,128)(2,1)S(1)}, bf16[1,26,96]{2,0,1:T(2,128)(2,1)S(1)}, u32[]{:S(2)}, u32[]{:S(2)}) %collective-permute-start.3) | collective-permute-done | bytes 5024 | tf_op jit(solution)/shard_map/ppermute | solution.py:700
  23.2 7.2 %collective-permute-done.2 = bf16[1,26,96]{2,0,1:T(2,128)(2,1)S(1)} collective-permute-done((bf16[1,26,96]{2,0,1:T(2,128)(2,1)S(1)}, bf16[1,26,96]{2,0,1:T(2,128)(2,1)S(1)}, u32[]{:S(2)}, u32[]{:S(2)}) %collective-permute-start.2) | collective-permute-done | bytes 5024 | tf_op jit(solution)/shard_map/ppermute | solution.py:700
  31.9 1.1 collective-permute-done.5
  32.9 5.6 %collective-permute-done.4 = bf16[26,5,96]{2,1,0:T(8,128)(2,1)S(1)} collective-permute-done((bf16[26,5,96]{2,1,0:T(8,128)(2,1)S(1)}, bf16[26,5,96]{2,1,0:T(8,128)(2,1)S(1)}, u32[]{:S(2)}, u32[]{:S(2)}) %collective-permute-start.4) | collective-permute-done | bytes 24992 | tf_op jit(solution)/shard_map/ppermute | solution.py:700
  38.6 2.7 %collective-permute-start.7 = (bf16[5,36,96]{2,1,0:T(8,128)(2,1)S(1)}, bf16[5,36,96]{2,1,0:T(8,128)(2,1)S(1)}, u32[]{:S(2)}, u32[]{:S(2)}) collective-permute-start(bf16[5,36,96]{2,1,0:T(8,128)(2,1)S(1)} %get-tuple-element.82), channel_id=1, source_target_pairs={{0,192},{8,200},{16,208},{24,216},{32,224},{40,232},{48,240},{56,2... | collective-permute-start | bytes 103688 | tf_op jit(solution)/shard_map/ppermute | solution.py:700
  41.3 3.3 %collective-permute-start.6 = (bf16[5,36,96]{2,1,0:T(8,128)(2,1)S(1)}, bf16[5,36,96]{2,1,0:T(8,128)(2,1)S(1)}, u32[]{:S(2)}, u32[]{:S(2)}) collective-permute-start(bf16[5,36,96]{2,1,0:T(8,128)(2,1)S(1)} %get-tuple-element.81), channel_id=1, source_target_pairs={{0,64},{8,72},{16,80},{24,88},{32,96},{40,104},{48,112},{56,120},{... | collective-permute-start | bytes 103688 | tf_op jit(solution)/shard_map/ppermute | solution.py:700
  46.8 0.8 collective-permute-done.7
  47.6 4.1 %collective-permute-done.6 = bf16[5,36,96]{2,1,0:T(8,128)(2,1)S(1)} collective-permute-done((bf16[5,36,96]{2,1,0:T(8,128)(2,1)S(1)}, bf16[5,36,96]{2,1,0:T(8,128)(2,1)S(1)}, u32[]{:S(2)}, u32[]{:S(2)}) %collective-permute-start.6) | collective-permute-done | bytes 34592 | tf_op jit(solution)/shard_map/ppermute | solution.py:700
  51.7 0.9 pad_maximum_fusion.source_ref
  52.6 12.7 %shard_map.255 = (bf16[960,1152]{1,0:T(8,128)(2,1)}, f32[2,30,32,128]{3,2,1,0:T(8,128)}, f32[576,256]{1,0:T(8,128)}, f32[576,128]{1,0:T(8,128)}, bf16[576,256]{1...) custom-call(s32[32]{0:T(128)} %seam_turns_ref.1, ...), custom_call_target="tpu_custom_call" | custom-call | flops 10000000000 | bytes 8000000 | tf_op jit(solution)/shard_map/pallas_call | solution.py:537
  65.3 5.8 %all-to-all-start = ((bf16[8,144,384]{2,1,0:T(8,128)(2,1)}), bf16[8,144,384]{2,1,0:T(8,128)(2,1)S(1)}, u32[]{:S(2)}, u32[]{:S(2)}) async-start(bf16[8,144,384]{2,1,0:T(8,128)(2,1)} %get-tuple-element.50), calls=%async_computation | async-start | bytes 1769472 | tf_op jit(solution)/shard_map/all_to_all | solution.py:731
  71.1 0.6 fusion.2.pick_ref
  71.7 0.7 fusion.order_ref
  72.7 0.8 reshape.102.target_ref
  73.5 7.1 %all-to-all-done.every_ref = bf16[8,144,384]{2,1,0:T(8,128)(2,1)S(1)} async-done(((bf16[8,144,384]{2,1,0:T(8,128)(2,1)}), bf16[8,144,384]{2,1,0:T(8,128)(2,1)S(1)}, u32[]{:S(2)}, u32[]{:S(2)}) %all-to-all-start) | async-done | bytes 884768 | tf_op jit(solution)/shard_map/all_to_all | solution.py:731
  80.5 0.9 copy-done
  81.5 8.8 %shard_map.256 = (bf16[8,32,16,128]{3,2,1,0:T(8,128)(2,1)}, f32[96,256]{1,0:T(8,128)}, f32[576,256]{1,0:T(8,128)}, f32[576,256]{1,0:T(8,128)}, f32[8,256]{1,0:T(8,128)}) custom-call(bf16[8,144,384]{2,1,0:T(8,128)(2,1)} %copy-done, f32[144,384]{1,0:T(8,128)} %get-tuple-element.51.own_ref, bf16[144,384]{1,0:T(8,128)(2,1)} %reshape.102.target_ref, ...), custom_call_target="tpu_custom_call" | custom-call | flops 12000000000 | bytes 8000000 | tf_op jit(solution)/shard_map/pallas_call | solution.py:537
  90.3 4.6 %all-to-all-start.1 = ((bf16[8,32,16,128]{3,2,1,0:T(8,128)(2,1)}), bf16[8,32,16,128]{3,2,1,0:T(8,128)(2,1)S(1)}, u32[]{:S(2)}, u32[]{:S(2)}) async-start(bf16[8,32,16,128]{3,2,1,0:T(8,128)(2,1)} %get-tuple-element.57), calls=%async_computation.1 | async-start | bytes 2097152 | tf_op jit(solution)/shard_map/all_to_all | solution.py:731
  94.9 12.3 %shard_map.257 = bf16[256,1152]{1,0:T(8,128)(2,1)} custom-call(f32[576,256]{1,0:T(8,128)} %get-tuple-element.58.scaled_grad_ref, f32[576,256]{1,0:T(8,128)} %get-tuple-element.59.normed_ref, f32[576,128]{1,0:T(8,128)} %get-tuple-element.60.inverse_ref, f32[10,256]{1,0:T(8,128)} %reshape.105.vectors_ref, f32[576,256]{1,0:T(8,128)} %get-tuple-element.61.hidden_grad_in, ...), custom_call_target="tpu_custom_call" | custom-call | flops 12000000000 | bytes 8000000 | tf_op jit(solution)/shard_map/pallas_call | solution.py:537
  107.2 13.6 %all_to_all.25.late_ref = bf16[8,32,1152]{2,1,0:T(8,128)(2,1)S(1)} all-to-all(bf16[8,32,1152]{2,1,0:T(8,128)(2,1)} %bitcast.32), channel_id=1, replica_groups=mesh['space'=32,'ens'=8] {'ens'}, dimensions={0} | all-to-all | bytes 1179648 | tf_op jit(solution)/shard_map/all_to_all | solution.py:731
  121.1 19.0 %all_to_all.26.share_ref = bf16[32,24,128]{2,1,0:T(8,128)(2,1)S(1)} all-to-all(bf16[32,24,128]{2,1,0:T(8,128)(2,1)S(1)} %shard_map.258), channel_id=1, replica_groups=mesh['space'=32,'ens'=8] {'space'}, dimensions={0} | all-to-all | bytes 393216 | tf_op jit(solution)/shard_map/all_to_all | solution.py:731
  140.1 0.7 shard_map.259
  140.8 4.5 %all-to-all-start.4 = ((f32[8,24,128]{2,1,0:T(8,128)}), f32[8,24,128]{2,1,0:T(8,128)S(1)}, u32[]{:S(2)}, u32[]{:S(2)}) async-start(f32[8,24,128]{2,1,0:T(8,128)} %shard_map.259), calls=%async_computation.4 | async-start | bytes 196608 | tf_op jit(solution)/shard_map/all_to_all | solution.py:731
  145.3 0.8 reshape.100
  146.1 4.5 %all-to-all-done.4.whole_ref = f32[8,24,128]{2,1,0:T(8,128)S(1)} async-done(((f32[8,24,128]{2,1,0:T(8,128)}), f32[8,24,128]{2,1,0:T(8,128)S(1)}, u32[]{:S(2)}, u32[]{:S(2)}) %all-to-all-start.4) | async-done | bytes 98336 | tf_op jit(solution)/shard_map/all_to_all | solution.py:731
  150.6 0.7 shard_map.260
  (63 shorter events, 4.8 us)
Async XLA Ops:
  6.0 9.3 %collective-permute-start = (bf16[24,1,96]{2,0,1:T(8,128)(2,1)S(1)}, bf16[24,1,96]{2,0,1:T(8,128)(2,1)S(1)}, u32[]{:S(2)}, u32[]{:S(2)}) collective-permute-start(bf16[24,1,96]{2,0,1:T(8,128)(2,1)S(1)} %slice_select_fusion.2), channel_id=1, source_target_pairs={{0,8},{8,16},{16,24},{24,32},{32,40},{40,48},{48,56},{56,64},{64,7... | collective-permute-start | bytes 13832 | tf_op jit(solution)/shard_map/ppermute | solution.py:700
  6.1 9.3 %collective-permute-start.1 = (bf16[24,1,96]{2,0,1:T(8,128)(2,1)S(1)}, bf16[24,1,96]{2,0,1:T(8,128)(2,1)S(1)}, u32[]{:S(2)}, u32[]{:S(2)}) collective-permute-start(bf16[24,1,96]{2,0,1:T(8,128)(2,1)S(1)} %get-tuple-element.94), channel_id=1, source_target_pairs={{0,248},{8,0},{16,8},{24,16},{32,24},{40,32},{48,40},{56,48},{64,5... | collective-permute-start | bytes 13832 | tf_op jit(solution)/shard_map/ppermute | solution.py:700
  15.5 7.7 %collective-permute-start.3 = (bf16[1,26,96]{2,0,1:T(2,128)(2,1)S(1)}, bf16[1,26,96]{2,0,1:T(2,128)(2,1)S(1)}, u32[]{:S(2)}, u32[]{:S(2)}) collective-permute-start(bf16[1,26,96]{2,0,1:T(2,128)(2,1)S(1)} %get-tuple-element.93), channel_id=1, source_target_pairs={{0,192},{8,200},{16,208},{24,216},{32,224},{40,232},{48,240},{56,2... | collective-permute-start | bytes 14984 | tf_op jit(solution)/shard_map/ppermute | solution.py:700
  20.4 10.0 %collective-permute-start.2 = (bf16[1,26,96]{2,0,1:T(2,128)(2,1)S(1)}, bf16[1,26,96]{2,0,1:T(2,128)(2,1)S(1)}, u32[]{:S(2)}, u32[]{:S(2)}) collective-permute-start(bf16[1,26,96]{2,0,1:T(2,128)(2,1)S(1)} %get-tuple-element.92), channel_id=1, source_target_pairs={{0,64},{8,72},{16,80},{24,88},{32,96},{40,104},{48,112},{56,120},{... | collective-permute-start | bytes 14984 | tf_op jit(solution)/shard_map/ppermute | solution.py:700
  30.6 14.0 %copy-start.9 = (bf16[96]{0:T(256)(128)(2,1)S(1)}, bf16[96]{0:T(256)(128)(2,1)}, u32[]{:S(2)}) copy-start(bf16[96]{0:T(256)(128)(2,1)} %param.31) | copy-start | bytes 580
  30.6 14.0 %copy-start.4 = (bf16[256]{0:T(256)(128)(2,1)S(1)}, bf16[256]{0:T(256)(128)(2,1)}, u32[]{:S(2)}) copy-start(bf16[256]{0:T(256)(128)(2,1)} %param.21) | copy-start | bytes 1540
  30.6 14.3 %copy-start.5 = (bf16[256]{0:T(256)(128)(2,1)S(1)}, bf16[256]{0:T(256)(128)(2,1)}, u32[]{:S(2)}) copy-start(bf16[256]{0:T(256)(128)(2,1)} %param.23) | copy-start | bytes 1540
  30.6 14.5 %copy-start.6 = (bf16[256]{0:T(256)(128)(2,1)S(1)}, bf16[256]{0:T(256)(128)(2,1)}, u32[]{:S(2)}) copy-start(bf16[256]{0:T(256)(128)(2,1)} %param.24) | copy-start | bytes 1540
  30.6 14.7 %copy-start.7 = (bf16[256]{0:T(256)(128)(2,1)S(1)}, bf16[256]{0:T(256)(128)(2,1)}, u32[]{:S(2)}) copy-start(bf16[256]{0:T(256)(128)(2,1)} %param.25) | copy-start | bytes 1540
  30.6 14.9 %copy-start.8 = (bf16[256]{0:T(256)(128)(2,1)S(1)}, bf16[256]{0:T(256)(128)(2,1)}, u32[]{:S(2)}) copy-start(bf16[256]{0:T(256)(128)(2,1)} %param.29) | copy-start | bytes 1540
  30.7 15.3 %copy-start.3 = (bf16[1024]{0:T(1024)(128)(2,1)S(1)}, bf16[1024]{0:T(1024)(128)(2,1)}, u32[]{:S(2)}) copy-start(bf16[1024]{0:T(1024)(128)(2,1)} %param.27) | copy-start | bytes 6148
  31.0 1.9 %collective-permute-start.5 = (bf16[26,5,96]{2,1,0:T(8,128)(2,1)S(1)}, bf16[26,5,96]{2,1,0:T(8,128)(2,1)S(1)}, u32[]{:S(2)}, u32[]{:S(2)}) collective-permute-start(bf16[26,5,96]{2,1,0:T(8,128)(2,1)S(1)} %get-tuple-element.87), channel_id=1, source_target_pairs={{0,248},{8,0},{16,8},{24,16},{32,24},{40,32},{48,40},{56,48},{64,5... | collective-permute-start | bytes 74888 | tf_op jit(solution)/shard_map/ppermute | solution.py:700
  31.3 7.3 %collective-permute-start.4 = (bf16[26,5,96]{2,1,0:T(8,128)(2,1)S(1)}, bf16[26,5,96]{2,1,0:T(8,128)(2,1)S(1)}, u32[]{:S(2)}, u32[]{:S(2)}) collective-permute-start(bf16[26,5,96]{2,1,0:T(8,128)(2,1)S(1)} %fusion.4), channel_id=1, source_target_pairs={{0,8},{8,16},{16,24},{24,32},{32,40},{40,48},{48,56},{56,64},{64,7... | collective-permute-start | bytes 74888 | tf_op jit(solution)/shard_map/ppermute | solution.py:700
  38.6 9.0 %collective-permute-start.7 = (bf16[5,36,96]{2,1,0:T(8,128)(2,1)S(1)}, bf16[5,36,96]{2,1,0:T(8,128)(2,1)S(1)}, u32[]{:S(2)}, u32[]{:S(2)}) collective-permute-start(bf16[5,36,96]{2,1,0:T(8,128)(2,1)S(1)} %get-tuple-element.82), channel_id=1, source_target_pairs={{0,192},{8,200},{16,208},{24,216},{32,224},{40,232},{48,240},{56,2... | collective-permute-start | bytes 103688 | tf_op jit(solution)/shard_map/ppermute | solution.py:700
  41.3 10.4 %collective-permute-start.6 = (bf16[5,36,96]{2,1,0:T(8,128)(2,1)S(1)}, bf16[5,36,96]{2,1,0:T(8,128)(2,1)S(1)}, u32[]{:S(2)}, u32[]{:S(2)}) collective-permute-start(bf16[5,36,96]{2,1,0:T(8,128)(2,1)S(1)} %get-tuple-element.81), channel_id=1, source_target_pairs={{0,64},{8,72},{16,80},{24,88},{32,96},{40,104},{48,112},{56,120},{... | collective-permute-start | bytes 103688 | tf_op jit(solution)/shard_map/ppermute | solution.py:700
  65.3 7.1 %copy-start.2 = (bf16[24,2304]{1,0:T(8,128)(2,1)S(1)}, bf16[24,2304]{1,0:T(8,128)(2,1)}, u32[]{:S(2)}) copy-start(bf16[24,2304]{1,0:T(8,128)(2,1)} %param.18) | copy-start | bytes 331780
  65.3 15.2 %all-to-all-start = ((bf16[8,144,384]{2,1,0:T(8,128)(2,1)}), bf16[8,144,384]{2,1,0:T(8,128)(2,1)S(1)}, u32[]{:S(2)}, u32[]{:S(2)}) async-start(bf16[8,144,384]{2,1,0:T(8,128)(2,1)} %get-tuple-element.50), calls=%async_computation | async-start | bytes 1769472 | tf_op jit(solution)/shard_map/all_to_all | solution.py:731
  80.5 0.9 copy-start
  90.3 16.9 %all-to-all-start.1 = ((bf16[8,32,16,128]{3,2,1,0:T(8,128)(2,1)}), bf16[8,32,16,128]{3,2,1,0:T(8,128)(2,1)S(1)}, u32[]{:S(2)}, u32[]{:S(2)}) async-start(bf16[8,32,16,128]{3,2,1,0:T(8,128)(2,1)} %get-tuple-element.57), calls=%async_computation.1 | async-start | bytes 2097152 | tf_op jit(solution)/shard_map/all_to_all | solution.py:731
  120.8 24.5 %copy-start.1 = (f32[576,96]{1,0:T(8,128)S(1)}, f32[576,96]{1,0:T(8,128)}, u32[]{:S(2)}) copy-start(f32[576,96]{1,0:T(8,128)} %get-tuple-element.49) | copy-start | bytes 663556
  140.8 9.8 %all-to-all-start.4 = ((f32[8,24,128]{2,1,0:T(8,128)}), f32[8,24,128]{2,1,0:T(8,128)S(1)}, u32[]{:S(2)}, u32[]{:S(2)}) async-start(f32[8,24,128]{2,1,0:T(8,128)} %shard_map.259), calls=%async_computation.4 | async-start | bytes 196608 | tf_op jit(solution)/shard_map/all_to_all | solution.py:731

commit v7 on v6

--- a/solution.py
+++ b/solution.py
@@ -79,9 +79,9 @@
     head_ref,
     patches_out,
     stem_out,
-    normed_ref,
-    inverse_ref,
-    scaled_ref,
+    normed_out,
+    inverse_out,
+    scaled_out,
     slope_out,
     active_out,
     hidden_ref,
@@ -93,6 +93,9 @@
     stem_ref,
     slope_ref,
     active_ref,
+    normed_ref,
+    inverse_ref,
+    scaled_ref,
     wide_ref,
     stage_ref,
     w_in_wide_ref,
@@ -108,6 +111,11 @@
 
     send_patches = pltpu.make_async_copy(patches_ref, patches_out, whole_sem.at[0])
     send_stem = pltpu.make_async_copy(stem_ref, stem_out, whole_sem.at[1])
+    send_norms = [
+        pltpu.make_async_copy(normed_ref, normed_out, whole_sem.at[2]),
+        pltpu.make_async_copy(inverse_ref, inverse_out, whole_sem.at[3]),
+        pltpu.make_async_copy(scaled_ref, scaled_out, whole_sem.at[4]),
+    ]
     tile = lax.axis_index("space")
     tiles = seam_turns_ref.shape[0]
     across = tiles // 4
@@ -176,6 +184,8 @@
         return carry
 
     lax.fori_loop(0, 6, normalise, 0)
+    for send in send_norms:
+        send.start()
 
     def mix(part, carry):
         row = pl.multiple_of(part * 96, 96)
@@ -212,6 +222,8 @@
         sent_ref[member] = sent
     send_patches.wait()
     send_stem.wait()
+    for send in send_norms:
+        send.wait()
     for part in range(6):
         for send in send_part(part, 96 * part):
             send.wait()
@@ -556,9 +568,9 @@
         [
             ((960, 1152), BF16, "a"),
             ((2, 30, 32, LANE), F32, "a"),
-            ((CELLS, 256), F32, "v"),
-            ((CELLS, LANE), F32, "v"),
-            ((CELLS, 256), BF16, "v"),
+            ((CELLS, 256), F32, "a"),
+            ((CELLS, LANE), F32, "a"),
+            ((CELLS, 256), BF16, "a"),
             ((CELLS, 1024), BF16, "a"),
             ((CELLS, 1024), BF16, "a"),
             ((CELLS, 256), BF16, "v"),
@@ -572,10 +584,13 @@
             ((2, 30, 32, LANE), F32),
             ((CELLS, 1024), BF16),
             ((CELLS, 1024), BF16),
+            ((CELLS, 256), F32),
+            ((CELLS, LANE), F32),
+            ((CELLS, 256), BF16),
             ((36, 40, LANE), F32),
             ((30, 32, LANE), F32),
             ((1152, 256), BF16),
-            pltpu.SemaphoreType.DMA((2,)),
+            pltpu.SemaphoreType.DMA((5,)),
             pltpu.SemaphoreType.DMA((2, 6)),
         ],
         seam_turns,

time: 152 us -> 152 us (level)
  no operation moved by 1% of the time
where the time goes in v7:
time: 152 us; the launch traced here: 151 us
  starting transfers between devices  35.7 us (23%)
  Pallas kernels  35.1 us (23%)
  waiting for transfers between devices  33.3 us (22%)
  blocking collectives  32.6 us (21%)
  local copies, waits for them, and re-layouts  7.2 us (5%)
  between operations  3.69 us (2%)
  other arithmetic  3.5 us (2%)
    pallas_call x6, Pallas kernels, call(): pl.pallas_call(kernel, out_shape=[jax.ShapeDtypeStruct(shape, kind) for s...  35.1 us
    all_to_all x2, blocking collectives, swap(): return lax.all_to_all(value, axis, 0, 0, tiled=True)  32.6 us
    ppermute x8, waiting for transfers between devices, shifted(): lax.ppermute(value, axis, [(i, (i + by) % peers) for i in range(peers)])  21.8 us
    ppermute x8, starting transfers between devices, shifted(): lax.ppermute(value, axis, [(i, (i + by) % peers) for i in range(peers)])  20.8 us
    all_to_all x3, starting transfers between devices, swap(): return lax.all_to_all(value, axis, 0, 0, tiled=True)  15 us
    all_to_all x3, waiting for transfers between devices, swap(): return lax.all_to_all(value, axis, 0, 0, tiled=True)  11.5 us
  transfers between devices with their start and end apart: 11, of which 10 were waited for; matrix products, arithmetic and copies ran while one was open for 4% of the time, Pallas kernels for 8%

profile of v7, /device:TPU:2, one launch (start us, length us, event | category | flops | bytes accessed | tf_op | source)
XLA Modules:
  0.0 151.1 jit_solution(6008229957856947124)
XLA Ops:
  0.7 1.3 fusion.16
  2.7 1.0 fusion.1
  6.1 8.0 %collective-permute-start.1 = (bf16[24,1,96]{2,0,1:T(8,128)(2,1)S(1)}, bf16[24,1,96]{2,0,1:T(8,128)(2,1)S(1)}, u32[]{:S(2)}, u32[]{:S(2)}) collective-permute-start(bf16[24,1,96]{2,0,1:T(8,128)(2,1)S(1)} %get-tuple-element.94), channel_id=1, source_target_pairs={{0,248},{8,0},{16,8},{24,16},{32,24},{40,32},{48,40},{56,48},{64,5... | collective-permute-start | bytes 13832 | tf_op jit(solution)/shard_map/ppermute | solution.py:715
  14.1 1.2 collective-permute-done
  15.5 4.9 %collective-permute-start.3 = (bf16[1,26,96]{2,0,1:T(2,128)(2,1)S(1)}, bf16[1,26,96]{2,0,1:T(2,128)(2,1)S(1)}, u32[]{:S(2)}, u32[]{:S(2)}) collective-permute-start(bf16[1,26,96]{2,0,1:T(2,128)(2,1)S(1)} %get-tuple-element.93), channel_id=1, source_target_pairs={{0,192},{8,200},{16,208},{24,216},{32,224},{40,232},{48,240},{56,2... | collective-permute-start | bytes 14984 | tf_op jit(solution)/shard_map/ppermute | solution.py:715
  20.4 1.2 collective-permute-start.2
  21.5 1.7 %collective-permute-done.3 = bf16[1,26,96]{2,0,1:T(2,128)(2,1)S(1)} collective-permute-done((bf16[1,26,96]{2,0,1:T(2,128)(2,1)S(1)}, bf16[1,26,96]{2,0,1:T(2,128)(2,1)S(1)}, u32[]{:S(2)}, u32[]{:S(2)}) %collective-permute-start.3) | collective-permute-done | bytes 5024 | tf_op jit(solution)/shard_map/ppermute | solution.py:715
  23.2 7.2 %collective-permute-done.2 = bf16[1,26,96]{2,0,1:T(2,128)(2,1)S(1)} collective-permute-done((bf16[1,26,96]{2,0,1:T(2,128)(2,1)S(1)}, bf16[1,26,96]{2,0,1:T(2,128)(2,1)S(1)}, u32[]{:S(2)}, u32[]{:S(2)}) %collective-permute-start.2) | collective-permute-done | bytes 5024 | tf_op jit(solution)/shard_map/ppermute | solution.py:715
  31.9 1.1 collective-permute-done.5
  32.9 5.6 %collective-permute-done.4 = bf16[26,5,96]{2,1,0:T(8,128)(2,1)S(1)} collective-permute-done((bf16[26,5,96]{2,1,0:T(8,128)(2,1)S(1)}, bf16[26,5,96]{2,1,0:T(8,128)(2,1)S(1)}, u32[]{:S(2)}, u32[]{:S(2)}) %collective-permute-start.4) | collective-permute-done | bytes 24992 | tf_op jit(solution)/shard_map/ppermute | solution.py:715
  38.6 2.7 %collective-permute-start.7 = (bf16[5,36,96]{2,1,0:T(8,128)(2,1)S(1)}, bf16[5,36,96]{2,1,0:T(8,128)(2,1)S(1)}, u32[]{:S(2)}, u32[]{:S(2)}) collective-permute-start(bf16[5,36,96]{2,1,0:T(8,128)(2,1)S(1)} %get-tuple-element.82), channel_id=1, source_target_pairs={{0,192},{8,200},{16,208},{24,216},{32,224},{40,232},{48,240},{56,2... | collective-permute-start | bytes 103688 | tf_op jit(solution)/shard_map/ppermute | solution.py:715
  41.3 3.3 %collective-permute-start.6 = (bf16[5,36,96]{2,1,0:T(8,128)(2,1)S(1)}, bf16[5,36,96]{2,1,0:T(8,128)(2,1)S(1)}, u32[]{:S(2)}, u32[]{:S(2)}) collective-permute-start(bf16[5,36,96]{2,1,0:T(8,128)(2,1)S(1)} %get-tuple-element.81), channel_id=1, source_target_pairs={{0,64},{8,72},{16,80},{24,88},{32,96},{40,104},{48,112},{56,120},{... | collective-permute-start | bytes 103688 | tf_op jit(solution)/shard_map/ppermute | solution.py:715
  46.8 0.8 collective-permute-done.7
  47.6 4.1 %collective-permute-done.6 = bf16[5,36,96]{2,1,0:T(8,128)(2,1)S(1)} collective-permute-done((bf16[5,36,96]{2,1,0:T(8,128)(2,1)S(1)}, bf16[5,36,96]{2,1,0:T(8,128)(2,1)S(1)}, u32[]{:S(2)}, u32[]{:S(2)}) %collective-permute-start.6) | collective-permute-done | bytes 34592 | tf_op jit(solution)/shard_map/ppermute | solution.py:715
  51.7 0.9 pad_maximum_fusion.source_ref
  52.6 12.3 %shard_map.255 = (bf16[960,1152]{1,0:T(8,128)(2,1)}, f32[2,30,32,128]{3,2,1,0:T(8,128)}, f32[576,256]{1,0:T(8,128)}, f32[576,128]{1,0:T(8,128)}, bf16[576,256]{1...) custom-call(s32[32]{0:T(128)} %seam_turns_ref.1, ...), custom_call_target="tpu_custom_call" | custom-call | flops 10000000000 | bytes 8000000 | tf_op jit(solution)/shard_map/pallas_call | solution.py:549
  64.9 5.8 %all-to-all-start = ((bf16[8,144,384]{2,1,0:T(8,128)(2,1)}), bf16[8,144,384]{2,1,0:T(8,128)(2,1)S(1)}, u32[]{:S(2)}, u32[]{:S(2)}) async-start(bf16[8,144,384]{2,1,0:T(8,128)(2,1)} %get-tuple-element.50), calls=%async_computation | async-start | bytes 1769472 | tf_op jit(solution)/shard_map/all_to_all | solution.py:746
  70.7 0.6 fusion.2.pick_ref
  71.3 0.7 fusion.order_ref
  72.3 0.8 reshape.102.target_ref
  73.1 7.1 %all-to-all-done.every_ref = bf16[8,144,384]{2,1,0:T(8,128)(2,1)S(1)} async-done(((bf16[8,144,384]{2,1,0:T(8,128)(2,1)}), bf16[8,144,384]{2,1,0:T(8,128)(2,1)S(1)}, u32[]{:S(2)}, u32[]{:S(2)}) %all-to-all-start) | async-done | bytes 884768 | tf_op jit(solution)/shard_map/all_to_all | solution.py:746
  80.2 0.9 copy-done
  81.1 8.8 %shard_map.256 = (bf16[8,32,16,128]{3,2,1,0:T(8,128)(2,1)}, f32[96,256]{1,0:T(8,128)}, f32[576,256]{1,0:T(8,128)}, f32[576,256]{1,0:T(8,128)}, f32[8,256]{1,0:T(8,128)}) custom-call(bf16[8,144,384]{2,1,0:T(8,128)(2,1)} %copy-done, f32[144,384]{1,0:T(8,128)} %get-tuple-element.51.own_ref, bf16[144,384]{1,0:T(8,128)(2,1)} %reshape.102.target_ref, ...), custom_call_target="tpu_custom_call" | custom-call | flops 12000000000 | bytes 8000000 | tf_op jit(solution)/shard_map/pallas_call | solution.py:549
  89.9 4.6 %all-to-all-start.1 = ((bf16[8,32,16,128]{3,2,1,0:T(8,128)(2,1)}), bf16[8,32,16,128]{3,2,1,0:T(8,128)(2,1)S(1)}, u32[]{:S(2)}, u32[]{:S(2)}) async-start(bf16[8,32,16,128]{3,2,1,0:T(8,128)(2,1)} %get-tuple-element.57), calls=%async_computation.1 | async-start | bytes 2097152 | tf_op jit(solution)/shard_map/all_to_all | solution.py:746
  94.5 12.3 %shard_map.257 = bf16[256,1152]{1,0:T(8,128)(2,1)} custom-call(f32[576,256]{1,0:T(8,128)} %get-tuple-element.58.scaled_grad_ref, f32[576,256]{1,0:T(8,128)} %get-tuple-element.59.normed_ref, f32[576,128]{1,0:T(8,128)} %get-tuple-element.60.inverse_ref, f32[10,256]{1,0:T(8,128)} %reshape.105.vectors_ref, f32[576,256]{1,0:T(8,128)} %get-tuple-element.61.hidden_grad_in, ...), custom_call_target="tpu_custom_call" | custom-call | flops 12000000000 | bytes 8000000 | tf_op jit(solution)/shard_map/pallas_call | solution.py:549
  106.8 13.6 %all_to_all.25.late_ref = bf16[8,32,1152]{2,1,0:T(8,128)(2,1)S(1)} all-to-all(bf16[8,32,1152]{2,1,0:T(8,128)(2,1)} %bitcast.32), channel_id=1, replica_groups=mesh['space'=32,'ens'=8] {'ens'}, dimensions={0} | all-to-all | bytes 1179648 | tf_op jit(solution)/shard_map/all_to_all | solution.py:746
  120.8 19.0 %all_to_all.26.share_ref = bf16[32,24,128]{2,1,0:T(8,128)(2,1)S(1)} all-to-all(bf16[32,24,128]{2,1,0:T(8,128)(2,1)S(1)} %shard_map.258), channel_id=1, replica_groups=mesh['space'=32,'ens'=8] {'space'}, dimensions={0} | all-to-all | bytes 393216 | tf_op jit(solution)/shard_map/all_to_all | solution.py:746
  139.7 0.7 shard_map.259
  140.4 4.5 %all-to-all-start.4 = ((f32[8,24,128]{2,1,0:T(8,128)}), f32[8,24,128]{2,1,0:T(8,128)S(1)}, u32[]{:S(2)}, u32[]{:S(2)}) async-start(f32[8,24,128]{2,1,0:T(8,128)} %shard_map.259), calls=%async_computation.4 | async-start | bytes 196608 | tf_op jit(solution)/shard_map/all_to_all | solution.py:746
  145.0 0.8 reshape.100
  145.8 4.5 %all-to-all-done.4.whole_ref = f32[8,24,128]{2,1,0:T(8,128)S(1)} async-done(((f32[8,24,128]{2,1,0:T(8,128)}), f32[8,24,128]{2,1,0:T(8,128)S(1)}, u32[]{:S(2)}, u32[]{:S(2)}) %all-to-all-start.4) | async-done | bytes 98336 | tf_op jit(solution)/shard_map/all_to_all | solution.py:746
  150.2 0.7 shard_map.260
  (63 shorter events, 4.8 us)
Async XLA Ops:
  6.0 9.3 %collective-permute-start = (bf16[24,1,96]{2,0,1:T(8,128)(2,1)S(1)}, bf16[24,1,96]{2,0,1:T(8,128)(2,1)S(1)}, u32[]{:S(2)}, u32[]{:S(2)}) collective-permute-start(bf16[24,1,96]{2,0,1:T(8,128)(2,1)S(1)} %slice_select_fusion.2), channel_id=1, source_target_pairs={{0,8},{8,16},{16,24},{24,32},{32,40},{40,48},{48,56},{56,64},{64,7... | collective-permute-start | bytes 13832 | tf_op jit(solution)/shard_map/ppermute | solution.py:715
  6.1 9.3 %collective-permute-start.1 = (bf16[24,1,96]{2,0,1:T(8,128)(2,1)S(1)}, bf16[24,1,96]{2,0,1:T(8,128)(2,1)S(1)}, u32[]{:S(2)}, u32[]{:S(2)}) collective-permute-start(bf16[24,1,96]{2,0,1:T(8,128)(2,1)S(1)} %get-tuple-element.94), channel_id=1, source_target_pairs={{0,248},{8,0},{16,8},{24,16},{32,24},{40,32},{48,40},{56,48},{64,5... | collective-permute-start | bytes 13832 | tf_op jit(solution)/shard_map/ppermute | solution.py:715
  15.5 7.7 %collective-permute-start.3 = (bf16[1,26,96]{2,0,1:T(2,128)(2,1)S(1)}, bf16[1,26,96]{2,0,1:T(2,128)(2,1)S(1)}, u32[]{:S(2)}, u32[]{:S(2)}) collective-permute-start(bf16[1,26,96]{2,0,1:T(2,128)(2,1)S(1)} %get-tuple-element.93), channel_id=1, source_target_pairs={{0,192},{8,200},{16,208},{24,216},{32,224},{40,232},{48,240},{56,2... | collective-permute-start | bytes 14984 | tf_op jit(solution)/shard_map/ppermute | solution.py:715
  20.4 10.0 %collective-permute-start.2 = (bf16[1,26,96]{2,0,1:T(2,128)(2,1)S(1)}, bf16[1,26,96]{2,0,1:T(2,128)(2,1)S(1)}, u32[]{:S(2)}, u32[]{:S(2)}) collective-permute-start(bf16[1,26,96]{2,0,1:T(2,128)(2,1)S(1)} %get-tuple-element.92), channel_id=1, source_target_pairs={{0,64},{8,72},{16,80},{24,88},{32,96},{40,104},{48,112},{56,120},{... | collective-permute-start | bytes 14984 | tf_op jit(solution)/shard_map/ppermute | solution.py:715
  30.6 14.0 %copy-start.9 = (bf16[96]{0:T(256)(128)(2,1)S(1)}, bf16[96]{0:T(256)(128)(2,1)}, u32[]{:S(2)}) copy-start(bf16[96]{0:T(256)(128)(2,1)} %param.31) | copy-start | bytes 580
  30.6 14.0 %copy-start.4 = (bf16[256]{0:T(256)(128)(2,1)S(1)}, bf16[256]{0:T(256)(128)(2,1)}, u32[]{:S(2)}) copy-start(bf16[256]{0:T(256)(128)(2,1)} %param.21) | copy-start | bytes 1540
  30.6 14.3 %copy-start.5 = (bf16[256]{0:T(256)(128)(2,1)S(1)}, bf16[256]{0:T(256)(128)(2,1)}, u32[]{:S(2)}) copy-start(bf16[256]{0:T(256)(128)(2,1)} %param.23) | copy-start | bytes 1540
  30.6 14.5 %copy-start.6 = (bf16[256]{0:T(256)(128)(2,1)S(1)}, bf16[256]{0:T(256)(128)(2,1)}, u32[]{:S(2)}) copy-start(bf16[256]{0:T(256)(128)(2,1)} %param.24) | copy-start | bytes 1540
  30.6 14.7 %copy-start.7 = (bf16[256]{0:T(256)(128)(2,1)S(1)}, bf16[256]{0:T(256)(128)(2,1)}, u32[]{:S(2)}) copy-start(bf16[256]{0:T(256)(128)(2,1)} %param.25) | copy-start | bytes 1540
  30.6 14.9 %copy-start.8 = (bf16[256]{0:T(256)(128)(2,1)S(1)}, bf16[256]{0:T(256)(128)(2,1)}, u32[]{:S(2)}) copy-start(bf16[256]{0:T(256)(128)(2,1)} %param.29) | copy-start | bytes 1540
  30.7 15.3 %copy-start.3 = (bf16[1024]{0:T(1024)(128)(2,1)S(1)}, bf16[1024]{0:T(1024)(128)(2,1)}, u32[]{:S(2)}) copy-start(bf16[1024]{0:T(1024)(128)(2,1)} %param.27) | copy-start | bytes 6148
  31.0 1.9 %collective-permute-start.5 = (bf16[26,5,96]{2,1,0:T(8,128)(2,1)S(1)}, bf16[26,5,96]{2,1,0:T(8,128)(2,1)S(1)}, u32[]{:S(2)}, u32[]{:S(2)}) collective-permute-start(bf16[26,5,96]{2,1,0:T(8,128)(2,1)S(1)} %get-tuple-element.87), channel_id=1, source_target_pairs={{0,248},{8,0},{16,8},{24,16},{32,24},{40,32},{48,40},{56,48},{64,5... | collective-permute-start | bytes 74888 | tf_op jit(solution)/shard_map/ppermute | solution.py:715
  31.3 7.3 %collective-permute-start.4 = (bf16[26,5,96]{2,1,0:T(8,128)(2,1)S(1)}, bf16[26,5,96]{2,1,0:T(8,128)(2,1)S(1)}, u32[]{:S(2)}, u32[]{:S(2)}) collective-permute-start(bf16[26,5,96]{2,1,0:T(8,128)(2,1)S(1)} %fusion.4), channel_id=1, source_target_pairs={{0,8},{8,16},{16,24},{24,32},{32,40},{40,48},{48,56},{56,64},{64,7... | collective-permute-start | bytes 74888 | tf_op jit(solution)/shard_map/ppermute | solution.py:715
  38.6 9.0 %collective-permute-start.7 = (bf16[5,36,96]{2,1,0:T(8,128)(2,1)S(1)}, bf16[5,36,96]{2,1,0:T(8,128)(2,1)S(1)}, u32[]{:S(2)}, u32[]{:S(2)}) collective-permute-start(bf16[5,36,96]{2,1,0:T(8,128)(2,1)S(1)} %get-tuple-element.82), channel_id=1, source_target_pairs={{0,192},{8,200},{16,208},{24,216},{32,224},{40,232},{48,240},{56,2... | collective-permute-start | bytes 103688 | tf_op jit(solution)/shard_map/ppermute | solution.py:715
  41.3 10.4 %collective-permute-start.6 = (bf16[5,36,96]{2,1,0:T(8,128)(2,1)S(1)}, bf16[5,36,96]{2,1,0:T(8,128)(2,1)S(1)}, u32[]{:S(2)}, u32[]{:S(2)}) collective-permute-start(bf16[5,36,96]{2,1,0:T(8,128)(2,1)S(1)} %get-tuple-element.81), channel_id=1, source_target_pairs={{0,64},{8,72},{16,80},{24,88},{32,96},{40,104},{48,112},{56,120},{... | collective-permute-start | bytes 103688 | tf_op jit(solution)/shard_map/ppermute | solution.py:715
  64.9 7.1 %copy-start.2 = (bf16[24,2304]{1,0:T(8,128)(2,1)S(1)}, bf16[24,2304]{1,0:T(8,128)(2,1)}, u32[]{:S(2)}) copy-start(bf16[24,2304]{1,0:T(8,128)(2,1)} %param.18) | copy-start | bytes 331780
  64.9 15.2 %all-to-all-start = ((bf16[8,144,384]{2,1,0:T(8,128)(2,1)}), bf16[8,144,384]{2,1,0:T(8,128)(2,1)S(1)}, u32[]{:S(2)}, u32[]{:S(2)}) async-start(bf16[8,144,384]{2,1,0:T(8,128)(2,1)} %get-tuple-element.50), calls=%async_computation | async-start | bytes 1769472 | tf_op jit(solution)/shard_map/all_to_all | solution.py:746
  80.1 0.9 copy-start
  89.9 16.9 %all-to-all-start.1 = ((bf16[8,32,16,128]{3,2,1,0:T(8,128)(2,1)}), bf16[8,32,16,128]{3,2,1,0:T(8,128)(2,1)S(1)}, u32[]{:S(2)}, u32[]{:S(2)}) async-start(bf16[8,32,16,128]{3,2,1,0:T(8,128)(2,1)} %get-tuple-element.57), calls=%async_computation.1 | async-start | bytes 2097152 | tf_op jit(solution)/shard_map/all_to_all | solution.py:746
  120.4 24.5 %copy-start.1 = (f32[576,96]{1,0:T(8,128)S(1)}, f32[576,96]{1,0:T(8,128)}, u32[]{:S(2)}) copy-start(f32[576,96]{1,0:T(8,128)} %get-tuple-element.49) | copy-start | bytes 663556
  140.4 9.8 %all-to-all-start.4 = ((f32[8,24,128]{2,1,0:T(8,128)}), f32[8,24,128]{2,1,0:T(8,128)S(1)}, u32[]{:S(2)}, u32[]{:S(2)}) async-start(f32[8,24,128]{2,1,0:T(8,128)} %shard_map.259), calls=%async_computation.4 | async-start | bytes 196608 | tf_op jit(solution)/shard_map/all_to_all | solution.py:746
